TPU v7x, 256 devices: a whole 4x4x8 slice. The times are simulated.
256 devices in a mesh: seq: 64 (over z_hi, y, x), chan: 4 (over z_lo, core).
Axes of the slice: x: 4, y: 4, z: 8 (z_hi: 4, z_lo: 2; z = z_hi * 2 + z_lo), core: 2. Of those that a mesh axis runs over, the one named last changes fastest.
Arguments:
- queries: bfloat16 [16384, 1024], P('seq', 'chan'), may hold values from -6 to 6
- keys: bfloat16 [16384, 1024], P('seq', 'chan'), may hold values from -6 to 6
- values: bfloat16 [16384, 1024], P('seq', 'chan'), may hold values from -6 to 6
- upstream: bfloat16 [16384, 1024], P('seq', 'chan'), may hold values from -6 to 6
- residues: float32 [1024, 16], P('chan'), may hold values from -1.5 to 1.5
- decay: float32 [1024, 16], P('chan'), may hold values from 3.0517578e-05 to 0.03
- skip: float32 [1024], P('chan'), may hold values from -3 to 3
Outputs:
- grad_queries: bfloat16 [16384, 1024], P('seq', 'chan')
- grad_keys: bfloat16 [16384, 1024], P('seq', 'chan')
- grad_values: bfloat16 [16384, 1024], P('seq', 'chan')
- grad_residues: float32 [1024, 16], P('chan')
- grad_decay: float32 [1024, 16], P('chan')
- grad_skip: float32 [1024], P('chan')
All inputs are finite; a program needn't handle non-finite values.
Results may differ from a plain program's by a relative error of at most 0.013.
Values may be sent and summed in bfloat16 or wider, within the bound.
No kernel may reach another device: no remote copies, remote signals or barrier semaphores. Data moves between devices by JAX's collectives and lax.ppermute only.
A program may use at most 64 MiB of HBM per device.

v0:
```python
import math

import jax
import jax.numpy as jnp
from jax import lax
from jax.sharding import PartitionSpec as P


def as_sent(array):

    def short(part):
        return part.astype(jnp.bfloat16) if part.dtype == jnp.float32 else part

    return jax.tree.map(short, array)


def split_length(total):
    best = 2
    for cand in range(2, total + 1, 2):
        if cand * cand > total:
            break
        if total % cand == 0:
            best = cand
    return (best, total // best)


def make_tables(first, second):
    total = first * second
    idx_one = jnp.arange(first, dtype=jnp.int32)
    idx_two = jnp.arange(second, dtype=jnp.int32)
    ang_one = (
        2.0 * math.pi / first * (idx_one[:, None] * idx_one[None, :] % first).astype(jnp.float32)
    )
    ang_two = (
        2.0 * math.pi / second * (idx_two[:, None] * idx_two[None, :] % second).astype(jnp.float32)
    )
    ang_tw = (
        2.0 * math.pi / total * (idx_one[:, None] * idx_two[None, :] % total).astype(jnp.float32)
    )
    return (
        jnp.cos(ang_one),
        jnp.sin(ang_one),
        jnp.cos(ang_two),
        jnp.sin(ang_two),
        jnp.cos(ang_tw),
        jnp.sin(ang_tw),
    )


def forward_dft(signal, tables):
    cos_one, sin_one, cos_two, sin_two, tw_cos, tw_sin = tables
    high = lax.Precision.HIGHEST
    half = signal.shape[1]
    a_real = jnp.einsum("cat,ak->ckt", signal, cos_one[:half], precision=high)
    a_imag = -jnp.einsum("cat,ak->ckt", signal, sin_one[:half], precision=high)
    b_real = a_real * tw_cos + a_imag * tw_sin
    b_imag = a_imag * tw_cos - a_real * tw_sin
    x_real = jnp.einsum("ckt,tm->ckm", b_real, cos_two, precision=high) + jnp.einsum(
        "ckt,tm->ckm", b_imag, sin_two, precision=high
    )
    x_imag = jnp.einsum("ckt,tm->ckm", b_imag, cos_two, precision=high) - jnp.einsum(
        "ckt,tm->ckm", b_real, sin_two, precision=high
    )
    return (x_real, x_imag)


def inverse_dft(x_real, x_imag, tables):
    cos_one, sin_one, cos_two, sin_two, tw_cos, tw_sin = tables
    high = lax.Precision.HIGHEST
    first = cos_one.shape[0]
    half = first // 2
    total = first * cos_two.shape[0]
    e_real = jnp.einsum("ckm,tm->ckt", x_real, cos_two, precision=high) - jnp.einsum(
        "ckm,tm->ckt", x_imag, sin_two, precision=high
    )
    e_imag = jnp.einsum("ckm,tm->ckt", x_real, sin_two, precision=high) + jnp.einsum(
        "ckm,tm->ckt", x_imag, cos_two, precision=high
    )
    f_real = e_real * tw_cos - e_imag * tw_sin
    f_imag = e_real * tw_sin + e_imag * tw_cos
    out = jnp.einsum("ckt,ka->cat", f_real, cos_one[:, :half], precision=high) - jnp.einsum(
        "ckt,ka->cat", f_imag, sin_one[:, :half], precision=high
    )
    return (out / total).reshape(out.shape[0], -1)


def lag_sums(grad_filt, decay_part, lags):
    expo = jnp.exp(-decay_part[:, :, None] * lags[None, None, :])
    proj = jnp.sum(grad_filt[:, None, :] * expo, axis=2)
    tproj = jnp.sum(grad_filt[:, None, :] * lags[None, None, :] * expo, axis=2)
    return (proj, tproj)


def finish_filter(proj, tproj, residues_part, decay_part):
    roots = jnp.sqrt(decay_part)
    return (roots * proj, residues_part * (proj / (2.0 * roots) - roots * tproj))


def channel_work(gated_ch, grad_ch, residues_part, decay_part, skip_part):
    count, length = gated_ch.shape
    first, second = split_length(2 * length)
    tables = make_tables(first, second)
    lags = jnp.arange(length, dtype=jnp.float32)
    roots = jnp.sqrt(decay_part)
    filt = jnp.sum(
        (residues_part * roots)[:, :, None]
        * jnp.exp(-decay_part[:, :, None] * lags[None, None, :]),
        axis=1,
    )
    gated_f = gated_ch.astype(jnp.float32)
    grad_f = grad_ch.astype(jnp.float32)
    shape = (count, first // 2, second)
    h_real, h_imag = forward_dft(filt.reshape(shape), tables)
    g_real, g_imag = forward_dft(gated_f.reshape(shape), tables)
    d_real, d_imag = forward_dft(grad_f.reshape(shape), tables)
    conv_out = inverse_dft(
        h_real * g_real - h_imag * g_imag, h_real * g_imag + h_imag * g_real, tables
    )
    conv_out = (conv_out + skip_part[:, None] * gated_f).astype(jnp.bfloat16)
    grad_gated = inverse_dft(
        h_real * d_real + h_imag * d_imag, h_real * d_imag - h_imag * d_real, tables
    )
    grad_gated = (grad_gated + skip_part[:, None] * grad_f).astype(jnp.bfloat16)
    grad_filt = inverse_dft(
        g_real * d_real + g_imag * d_imag, g_real * d_imag - g_imag * d_real, tables
    )
    return (conv_out, grad_gated, grad_filt, lags)


def shards(queries, keys, values, upstream, residues, decay, skip):
    tok_rows, width = queries.shape
    groups = lax.axis_size("seq")
    count = width // groups
    start = lax.axis_index("seq") * count
    res_part = lax.dynamic_slice_in_dim(residues, start, count, 0)
    dec_part = lax.dynamic_slice_in_dim(decay, start, count, 0)
    skip_part = lax.dynamic_slice_in_dim(skip, start, count, 0)
    q_ch, k_ch, v_ch, u_ch = (
        lax.all_to_all(queries.T, "seq", split_axis=0, concat_axis=1, tiled=True),
        lax.all_to_all(keys.T, "seq", split_axis=0, concat_axis=1, tiled=True),
        lax.all_to_all(values.T, "seq", split_axis=0, concat_axis=1, tiled=True),
        lax.all_to_all(upstream.T, "seq", split_axis=0, concat_axis=1, tiled=True),
    )
    gated_ch = (k_ch.astype(jnp.float32) * v_ch.astype(jnp.float32)).astype(jnp.bfloat16)
    grad_ch = (u_ch.astype(jnp.float32) * q_ch.astype(jnp.float32)).astype(jnp.bfloat16)
    conv_out, grad_gated, grad_filt, lags = channel_work(
        gated_ch, grad_ch, res_part, dec_part, skip_part
    )
    gg_f = grad_gated.astype(jnp.float32)
    dq_ch = (u_ch.astype(jnp.float32) * conv_out.astype(jnp.float32)).astype(jnp.bfloat16)
    dk_ch = (gg_f * v_ch.astype(jnp.float32)).astype(jnp.bfloat16)
    dv_ch = (gg_f * k_ch.astype(jnp.float32)).astype(jnp.bfloat16)
    dq_t, dk_t, dv_t = (
        lax.all_to_all(dq_ch, "seq", split_axis=1, concat_axis=0, tiled=True),
        lax.all_to_all(dk_ch, "seq", split_axis=1, concat_axis=0, tiled=True),
        lax.all_to_all(dv_ch, "seq", split_axis=1, concat_axis=0, tiled=True),
    )
    grad_queries, grad_keys, grad_values = (dq_t.T, dk_t.T, dv_t.T)
    filt_rows = lax.all_to_all(
        as_sent(grad_filt), "seq", split_axis=1, concat_axis=0, tiled=True
    ).astype(grad_filt.dtype)
    local_lags = (lax.axis_index("seq") * tok_rows + jnp.arange(tok_rows, dtype=jnp.int32)).astype(
        jnp.float32
    )
    proj_part, tproj_part = lag_sums(filt_rows, decay, local_lags)
    gated_seq = (
        (keys.astype(jnp.float32) * values.astype(jnp.float32))
        .astype(jnp.bfloat16)
        .astype(jnp.float32)
    )
    grad_seq = (
        (upstream.astype(jnp.float32) * queries.astype(jnp.float32))
        .astype(jnp.bfloat16)
        .astype(jnp.float32)
    )
    skip_part_sum = jnp.sum(gated_seq * grad_seq, axis=0)
    proj, tproj, grad_skip = lax.psum((proj_part, tproj_part, skip_part_sum), "seq")
    grad_residues, grad_decay = finish_filter(proj, tproj, residues, decay)
    return (grad_queries, grad_keys, grad_values, grad_residues, grad_decay, grad_skip)


def solution(mesh):
    placed = (
        P("seq", "chan"),
        P("seq", "chan"),
        P("seq", "chan"),
        P("seq", "chan"),
        P("chan", None),
        P("chan", None),
        P("chan"),
    )
    return jax.shard_map(
        shards,
        mesh=mesh,
        in_specs=placed,
        out_specs=(
            P("seq", "chan"),
            P("seq", "chan"),
            P("seq", "chan"),
            P("chan", None),
            P("chan", None),
            P("chan"),
        ),
        check_vma=False,
    )
```

profile of v0, /device:TPU:32, one launch (start us, length us, event | category | flops | bytes accessed | tf_op | source)
XLA Modules:
  0.0 573.8 jit_solution(12592393741418983591)
XLA Ops:
  0.6 1.0 copy.98
  1.7 0.7 all_to_all.84
  2.4 13.7 %all-to-all-start = ((bf16[64,4,256]{2,1,0:T(4,128)(2,1)}), bf16[64,4,256]{2,1,0:T(4,128)(2,1)S(1)}, u32[]{:S(2)}, u32[]{:S(2)}) async-start(bf16[64,4,256]{2,1,0:T(4,128)(2,1)} %all_to_all.84), calls=%async_computation | async-start | bytes 262144 | tf_op jit(solution)/shard_map/all_to_all | solution.py:142
  16.6 0.5 fusion.146
  17.4 1.3 multiply_reduce_fusion.2
  18.7 0.6 convolution_negate_fusion.2
  19.3 0.6 fusion.58
  20.0 1.6 fusion.31
  21.6 1.6 convolution_add_fusion.5
  23.3 0.7 all_to_all.86
  24.2 0.7 all_to_all.88
  24.9 0.6 multiply_reduce_fusion.3
  25.6 0.7 all_to_all.93
  26.3 0.6 add_convert_fusion
  26.9 0.8 copy.118
  27.7 0.6 dynamic_slice.11
  28.2 1.6 fusion.27
  29.8 13.0 %all-to-all-start.4 = ((bf16[64,4,256]{2,1,0:T(4,128)(2,1)}), bf16[64,4,256]{2,1,0:T(4,128)(2,1)S(1)}, u32[]{:S(2)}, u32[]{:S(2)}) async-start(bf16[64,4,256]{2,1,0:T(4,128)(2,1)} %all_to_all.93), calls=%async_computation.4 | async-start | bytes 262144 | tf_op jit(solution)/shard_map/all_to_all | solution.py:139
  42.8 2.4 convolution_subtract_fusion.5
  45.2 10.1 %all-to-all-done.4 = bf16[64,4,256]{2,1,0:T(4,128)(2,1)S(1)} async-done(((bf16[64,4,256]{2,1,0:T(4,128)(2,1)}), bf16[64,4,256]{2,1,0:T(4,128)(2,1)S(1)}, u32[]{:S(2)}, u32[]{:S(2)}) %all-to-all-start.4) | async-done | bytes 131104 | tf_op jit(solution)/shard_map/all_to_all | solution.py:139
  55.3 4.6 all-to-all-start.1
  60.8 1.6 fusion.15
  62.4 10.1 %all-to-all-done.1 = bf16[64,4,256]{2,1,0:T(4,128)(2,1)S(1)} async-done(((bf16[64,4,256]{2,1,0:T(4,128)(2,1)}), bf16[64,4,256]{2,1,0:T(4,128)(2,1)S(1)}, u32[]{:S(2)}, u32[]{:S(2)}) %all-to-all-start.1) | async-done | bytes 131104 | tf_op jit(solution)/shard_map/all_to_all | solution.py:140
  72.5 4.6 all-to-all-start.2
  77.1 1.6 fusion.19
  78.7 11.1 %all-to-all-done.2 = bf16[64,4,256]{2,1,0:T(4,128)(2,1)S(1)} async-done(((bf16[64,4,256]{2,1,0:T(4,128)(2,1)}), bf16[64,4,256]{2,1,0:T(4,128)(2,1)S(1)}, u32[]{:S(2)}, u32[]{:S(2)}) %all-to-all-start.2) | async-done | bytes 131104 | tf_op jit(solution)/shard_map/all_to_all | solution.py:141
  90.6 1.6 fusion.25
  92.2 1.6 fusion.21
  93.8 1.6 convolution_add_fusion.4
  95.4 1.6 convolution_subtract_fusion.2
  97.0 1.6 convolution_add_fusion.2
  98.6 10.7 %multiply_subtract_fusion = (f32[4,128,256]{2,1,0:T(8,128)S(1)}, f32[4,128,256]{2,1,0:T(8,128)S(1)}, f32[4,128,256]{2,1,0:T(8,128)S(1)}, f32[4,128,256]{2,1,0:T(...) fusion(f32[4,128,256]{2,1,0:T(8,128)S(1)} %convolution_add_fusion.2, ...), kind=kOutput, calls=%fused_computation.62 | convolution fusion | flops 406454272 | bytes 7602176 | tf_op jit(solution)/shard_map/ckt,tm->ckm/dot_general | solution.py:61
  109.3 1.6 fusion.80
  110.9 1.6 fusion.64
  112.4 2.4 fusion.83
  114.8 1.6 fusion.67
  116.4 2.4 fusion.88
  118.7 1.6 fusion.72
  120.3 1.6 convolution_subtract_fusion
  121.9 1.8 convolution_add_fusion
  124.7 0.8 copy.117
  125.4 5.5 all-to-all-start.7
  130.9 1.6 convolution_subtract_fusion.1
  132.5 1.6 convolution_add_fusion.1
  134.7 0.5 fusion.63
  135.2 0.8 copy.113
  136.0 0.8 copy.114
  136.8 1.6 convolution_subtract_fusion.3
  138.3 1.6 convolution_add_fusion.3
  140.4 3.0 all-to-all-done.7
  143.4 9.7 %all-to-all-start.5 = ((bf16[4,64,256]{2,0,1:T(4,128)(2,1)}), bf16[4,64,256]{2,0,1:T(4,128)(2,1)S(1)}, u32[]{:S(2)}, u32[]{:S(2)}) async-start(bf16[4,64,256]{2,0,1:T(4,128)(2,1)} %copy.113), calls=%async_computation.5 | async-start | bytes 262144 | tf_op jit(solution)/shard_map/all_to_all | solution.py:155
  153.6 0.8 copy.108
  154.4 11.2 %all-to-all-done.5 = bf16[4,64,256]{2,0,1:T(4,128)(2,1)S(1)} async-done(((bf16[4,64,256]{2,0,1:T(4,128)(2,1)}), bf16[4,64,256]{2,0,1:T(4,128)(2,1)S(1)}, u32[]{:S(2)}, u32[]{:S(2)}) %all-to-all-start.5) | async-done | bytes 131104 | tf_op jit(solution)/shard_map/all_to_all | solution.py:155
  165.6 4.6 all-to-all-start.6
  170.2 0.9 convert_bitcast_fusion
  171.3 11.6 %all-to-all-done.6 = bf16[4,64,256]{2,0,1:T(4,128)(2,1)S(1)} async-done(((bf16[4,64,256]{2,0,1:T(4,128)(2,1)}), bf16[4,64,256]{2,0,1:T(4,128)(2,1)S(1)}, u32[]{:S(2)}, u32[]{:S(2)}) %all-to-all-start.6) | async-done | bytes 131104 | tf_op jit(solution)/shard_map/all_to_all | solution.py:156
  182.9 4.6 all-to-all-start.3
  187.6 2.1 multiply_reduce_fusion
  189.8 0.8 copy.122
  190.6 0.8 copy.123
  191.4 8.7 %all-to-all-done.3 = bf16[4,64,256]{2,0,1:T(4,128)(2,1)S(1)} async-done(((bf16[4,64,256]{2,0,1:T(4,128)(2,1)}), bf16[4,64,256]{2,0,1:T(4,128)(2,1)S(1)}, u32[]{:S(2)}, u32[]{:S(2)}) %all-to-all-start.3) | async-done | bytes 131104 | tf_op jit(solution)/shard_map/all_to_all | solution.py:154
  200.2 0.8 copy.121
  200.9 371.8 %all-reduce = (f32[256,16]{0,1:T(8,128)S(1)}, f32[256,16]{0,1:T(8,128)S(1)}, f32[256]{0:T(256)}) all-reduce(f32[256,16]{0,1:T(8,128)S(1)} %copy.119, f32[256,16]{0,1:T(8,128)S(1)} %copy.120, f32[256]{0:T(256)S(1)} %copy-done.11), channel_id=1, replica_groups=mesh['seq'=64,'chan'=4] {'seq'}, use_global_device_ids=true, to_apply=%region_2.3 | all-reduce | flops 8448 | bytes 67584 | tf_op jit(solution)/shard_map/psum | solution.py:177
  572.7 0.6 subtract_multiply_fusion
  (57 shorter events, 5.8 us)
Async XLA Ops:
  1.6 15.5 %copy-start.8 = (f32[256,16]{0,1:T(8,128)S(1)}, f32[256,16]{0,1:T(8,128)}, u32[]{:S(2)}) copy-start(f32[256,16]{0,1:T(8,128)} %param.12) | copy-start | bytes 49156
  1.7 15.5 %copy-start.9 = (f32[256,16]{0,1:T(8,128)S(1)}, f32[256,16]{0,1:T(8,128)}, u32[]{:S(2)}) copy-start(f32[256,16]{0,1:T(8,128)} %param.11) | copy-start | bytes 49156
  2.4 27.5 %all-to-all-start = ((bf16[64,4,256]{2,1,0:T(4,128)(2,1)}), bf16[64,4,256]{2,1,0:T(4,128)(2,1)S(1)}, u32[]{:S(2)}, u32[]{:S(2)}) async-start(bf16[64,4,256]{2,1,0:T(4,128)(2,1)} %all_to_all.84), calls=%async_computation | async-start | bytes 262144 | tf_op jit(solution)/shard_map/all_to_all | solution.py:142
  21.6 1.6 copy-start.5
  23.2 0.9 copy-start.4
  23.2 1.7 copy-start.3
  23.2 1.7 copy-start.6
  24.9 2.8 copy-start.14
  29.8 25.5 %all-to-all-start.4 = ((bf16[64,4,256]{2,1,0:T(4,128)(2,1)}), bf16[64,4,256]{2,1,0:T(4,128)(2,1)S(1)}, u32[]{:S(2)}, u32[]{:S(2)}) async-start(bf16[64,4,256]{2,1,0:T(4,128)(2,1)} %all_to_all.93), calls=%async_computation.4 | async-start | bytes 262144 | tf_op jit(solution)/shard_map/all_to_all | solution.py:139
  55.3 17.2 %all-to-all-start.1 = ((bf16[64,4,256]{2,1,0:T(4,128)(2,1)}), bf16[64,4,256]{2,1,0:T(4,128)(2,1)S(1)}, u32[]{:S(2)}, u32[]{:S(2)}) async-start(bf16[64,4,256]{2,1,0:T(4,128)(2,1)} %all_to_all.86), calls=%async_computation.1 | async-start | bytes 262144 | tf_op jit(solution)/shard_map/all_to_all | solution.py:140
  72.5 17.3 %all-to-all-start.2 = ((bf16[64,4,256]{2,1,0:T(4,128)(2,1)}), bf16[64,4,256]{2,1,0:T(4,128)(2,1)S(1)}, u32[]{:S(2)}, u32[]{:S(2)}) async-start(bf16[64,4,256]{2,1,0:T(4,128)(2,1)} %all_to_all.88), calls=%async_computation.2 | async-start | bytes 262144 | tf_op jit(solution)/shard_map/all_to_all | solution.py:141
  97.0 1.6 copy-start
  124.7 6.2 %copy-start.2 = (f32[4,128,256]{2,1,0:T(8,128)S(1)}, f32[4,128,256]{2,1,0:T(8,128)}, u32[]{:S(2)}) copy-start(f32[4,128,256]{2,1,0:T(8,128)} %fusion.83) | copy-start | bytes 1572868
  125.4 17.9 %all-to-all-start.7 = ((bf16[4,64,256]{2,0,1:T(4,128)(2,1)}), bf16[4,64,256]{2,0,1:T(4,128)(2,1)}, u32[]{:S(2)}, u32[]{:S(2)}) async-start(bf16[4,64,256]{2,0,1:T(4,128)(2,1)} %copy.117), calls=%async_computation.7 | async-start | bytes 262144 | tf_op jit(solution)/shard_map/all_to_all | solution.py:159
  134.1 0.7 copy-start.12
  135.2 1.5 copy-start.1
  143.4 22.2 %all-to-all-start.5 = ((bf16[4,64,256]{2,0,1:T(4,128)(2,1)}), bf16[4,64,256]{2,0,1:T(4,128)(2,1)S(1)}, u32[]{:S(2)}, u32[]{:S(2)}) async-start(bf16[4,64,256]{2,0,1:T(4,128)(2,1)} %copy.113), calls=%async_computation.5 | async-start | bytes 262144 | tf_op jit(solution)/shard_map/all_to_all | solution.py:155
  165.6 17.4 %all-to-all-start.6 = ((bf16[4,64,256]{2,0,1:T(4,128)(2,1)}), bf16[4,64,256]{2,0,1:T(4,128)(2,1)S(1)}, u32[]{:S(2)}, u32[]{:S(2)}) async-start(bf16[4,64,256]{2,0,1:T(4,128)(2,1)} %copy.114), calls=%async_computation.6 | async-start | bytes 262144 | tf_op jit(solution)/shard_map/all_to_all | solution.py:156
  170.2 1.0 copy-start.13
  171.2 16.3 %copy-start.7 = (f32[256,16]{1,0:T(8,128)S(1)}, f32[256,16]{1,0:T(8,128)}, u32[]{:S(2)}) copy-start(f32[256,16]{1,0:T(8,128)} %copy.118) | copy-start | bytes 49156
  182.9 17.2 %all-to-all-start.3 = ((bf16[4,64,256]{2,0,1:T(4,128)(2,1)}), bf16[4,64,256]{2,0,1:T(4,128)(2,1)S(1)}, u32[]{:S(2)}, u32[]{:S(2)}) async-start(bf16[4,64,256]{2,0,1:T(4,128)(2,1)} %copy.108), calls=%async_computation.3 | async-start | bytes 262144 | tf_op jit(solution)/shard_map/all_to_all | solution.py:154
  190.6 10.3 %copy-start.11 = (f32[256]{0:T(256)S(1)}, f32[256]{0:T(256)}, u32[]{:S(2)}) copy-start(f32[256]{0:T(256)} %multiply_reduce_fusion.3) | copy-start | bytes 3076
  190.6 382.1 %copy-start.10 = (f32[256,16]{0,1:T(8,128)S(1)}, f32[256,16]{0,1:T(8,128)}, u32[]{:S(2)}) copy-start(f32[256,16]{0,1:T(8,128)} %param.11) | copy-start | bytes 49156
where the time goes:
time: 582 us; the launch traced here: 574 us
  blocking collectives  372 us (64%)
  waiting for transfers between devices  65.9 us (11%)
  starting transfers between devices  60.3 us (10%)
  matrix products  55.3 us (10%)
  local copies, waits for them, and re-layouts  11.6 us (2%)
  other arithmetic  7.27 us (1%)
    psum x1, blocking collectives, shards(): lax.psum((proj_part, tproj_part, skip_part_sum), 'seq')  372 us
    dot_general x3, matrix products, forward_dft(): jnp.einsum('ckt,tm->ckm', b_real, sin_two, precision=high)  14.6 us
    all_to_all x1, starting transfers between devices, shards(): lax.all_to_all(upstream.T, 'seq', split_axis=0, concat_axis=1, tiled=True)  13.7 us
    all_to_all x1, starting transfers between devices, shards(): lax.all_to_all(queries.T, 'seq', split_axis=0, concat_axis=1, tiled=True)  13 us
  transfers between devices with their start and end apart: 8, of which 7 were waited for; matrix products, arithmetic and copies ran while one was open for 6% of the time, Pallas kernels for 0%

commit v1 on v0

v1 whole, which is shorter than its diff:
```python
import functools

import jax
import jax.numpy as jnp
from jax import lax
from jax.experimental import pallas as pl
from jax.experimental.pallas import tpu as pltpu
from jax.sharding import PartitionSpec as P

F32 = jnp.float32
BF16 = jnp.bfloat16
VMEM = pltpu.VMEM
SEGS = 8
LANES = 128
GROUP = 4


def product(a, b):
    return (a.astype(F32) * b.astype(F32)).astype(BF16).astype(F32)


def lanes_of(i):
    return pl.ds(pl.multiple_of(i * LANES, LANES), LANES)


def rows_of(i, n):
    return pl.ds(pl.multiple_of(i * n, n), n)


def fetch(sems, *pairs):
    copies = [pltpu.make_async_copy(a, b, sems.at[i]) for i, (a, b) in enumerate(pairs)]
    for copy in copies:
        copy.start()
    return copies


def summary_kernel(
    dec_hbm, k_hbm, v_hbm, u_hbm, q_hbm,
    z_ref, gated_ref, grad_ref, pre_ref, post_ref, dec_t_ref, k_ref, v_ref, u_ref, q_ref,
    w_ref, e_ref, e1_ref, g_ref, g1_ref, p_ref, t_ref, sems,
):
    copies = fetch(sems, (dec_hbm, dec_t_ref), (k_hbm, k_ref), (v_hbm, v_ref), (u_hbm, u_ref), (q_hbm, q_ref))
    rows, width = q_ref.shape
    modes = dec_t_ref.shape[0]
    steps = rows // SEGS
    tiles = width // LANES
    copies[0].wait()
    dec_t = dec_t_ref[...]
    w_all = jnp.exp(-dec_t)
    for i in range(tiles):
        for m in range(modes):
            row = w_all[m : m + 1, i * LANES : (i + 1) * LANES]
            w_ref[i, pl.ds(m * SEGS, SEGS), :] = jnp.broadcast_to(row, (SEGS, LANES))
    for copy in copies[1:]:
        copy.wait()
    skip = jnp.zeros((8, width), F32)
    for seg in range(SEGS):
        for part in range(steps // 16):
            at = pl.ds(seg * steps + part * 16, 16)
            gated = product(k_ref[at, :], v_ref[at, :])
            grad = product(u_ref[at, :], q_ref[at, :])
            both = gated * grad
            skip = skip + both[:8] + both[8:]
            to = pl.ds(part * 16 * SEGS + seg, 16, stride=SEGS)
            for i in range(tiles):
                ln = slice(i * LANES, (i + 1) * LANES)
                gated_ref[i, to, :] = gated[:, ln]
                grad_ref[i, to, :] = grad[:, ln]
    skip = jnp.sum(skip, axis=0, keepdims=True)

    groups = modes // GROUP

    def one(i, _):
        ln = lax.div(i, groups)
        base = lax.rem(i, groups) * GROUP
        at = [rows_of(base + m, SEGS) for m in range(GROUP)]
        w = [w_ref[ln, a, :] for a in at]
        zero = jnp.zeros((SEGS, LANES), F32)
        h, h1, p, t, r, r1 = ([zero] * GROUP for _ in range(6))
        for j in range(steps):
            x = gated_ref[ln, pl.ds(j * SEGS, SEGS), :]
            y = grad_ref[ln, pl.ds(j * SEGS, SEGS), :]
            back = grad_ref[ln, pl.ds((steps - 1 - j) * SEGS, SEGS), :]
            for m in range(GROUP):
                wh = w[m] * h[m]
                h1[m] = w[m] * h1[m] + wh
                h[m] = wh + x
                p[m] = p[m] + y * h[m]
                t[m] = t[m] + y * h1[m]
                wr = w[m] * r[m]
                r1[m] = w[m] * r1[m] + wr
                r[m] = wr + back
        for m in range(GROUP):
            e_ref[ln, at[m], :] = w[m] * h[m]
            e1_ref[ln, at[m], :] = w[m] * (h1[m] + h[m])
            g_ref[ln, at[m], :] = r[m]
            g1_ref[ln, at[m], :] = r1[m]
            p_ref[ln, at[m], :] = p[m]
            t_ref[ln, at[m], :] = t[m]
        return 0

    lax.fori_loop(0, groups * tiles, one, 0)

    for i in range(tiles):
        ln = slice(i * LANES, (i + 1) * LANES)
        dec = dec_t[:, ln]
        w_seg = jnp.exp(dec * (-float(steps)))
        zero = jnp.zeros((modes, LANES), F32)
        s, s1, p, t = zero, zero, zero, zero
        for seg in range(SEGS):
            at = pl.ds(seg, modes, stride=SEGS)
            g, g1 = g_ref[i, at, :], g1_ref[i, at, :]
            pre_ref[i, at, :] = s
            p = p + p_ref[i, at, :] + s * g
            t = t + t_ref[i, at, :] + s1 * g + s * g1
            s1 = w_seg * (s1 + float(steps) * s) + e1_ref[i, at, :]
            s = w_seg * s + e_ref[i, at, :]
        r, r1 = zero, zero
        for seg in range(SEGS - 1, -1, -1):
            at = pl.ds(seg, modes, stride=SEGS)
            post_ref[i, at, :] = r
            r1 = w_seg * (r1 + float(steps) * r) + g1_ref[i, at, :]
            r = w_seg * r + g_ref[i, at, :]
        parts = (s, 0.25 * s - dec * s1, r, 0.25 * r - dec * r1, p, 0.5 * p - dec * t)
        for n, part in enumerate(parts):
            z_ref[n * modes : (n + 1) * modes, ln] = part.astype(BF16)
    z_ref[6 * modes : 6 * modes + 16, :] = jnp.broadcast_to(skip, (16, width)).astype(BF16)


def conv_kernel(
    res_hbm, skip_hbm, gated_ref, grad_ref, dec_t_ref, pre_ref, post_ref,
    fwd_ref, bwd_ref, in_ref, out_ref, in0_ref, out0_ref, res_t_ref, skip_ref, w_ref, a_ref, sems,
):
    copies = fetch(sems, (res_hbm, res_t_ref), (skip_hbm, skip_ref))
    tiles, rows, _ = gated_ref.shape
    modes = dec_t_ref.shape[0]
    steps = rows // SEGS
    for copy in copies:
        copy.wait()
    dec_t = dec_t_ref[...]
    scale = res_t_ref[...] * jnp.sqrt(dec_t)
    seg_at = lax.broadcasted_iota(jnp.int32, (SEGS, LANES), 0).astype(F32) * float(steps)
    for i in range(tiles):
        ln = slice(i * LANES, (i + 1) * LANES)
        for m in range(modes):
            at = pl.ds(m * SEGS, SEGS)
            d = jnp.broadcast_to(dec_t[m : m + 1, ln], (SEGS, LANES))
            a = jnp.broadcast_to(scale[m : m + 1, ln], (SEGS, LANES))
            w = jnp.exp(-d)
            w_ref[i, at, :] = w
            a_ref[i, at, :] = a
            in_ref[i, at, :] = a * jnp.exp(-d * seg_at)
            out_ref[i, at, :] = a * jnp.exp(-d * (float(rows - steps + 1) - seg_at))
            in0_ref[i, at, :] = a * pre_ref[i, at, :]
            out0_ref[i, at, :] = a * w * post_ref[i, at, :]

    def one(i, _):
        for base in range(0, modes, GROUP):
            at = [pl.ds((base + m) * SEGS, SEGS) for m in range(GROUP)]
            w = [w_ref[i, x, :] for x in at]
            a = [a_ref[i, x, :] for x in at]
            zero = jnp.zeros((SEGS, LANES), F32)
            h, r = [zero] * GROUP, [zero] * GROUP
            for j in range(steps):
                at_f = pl.ds(j * SEGS, SEGS)
                at_b = pl.ds((steps - 1 - j) * SEGS, SEGS)
                x, y = gated_ref[i, at_f, :], grad_ref[i, at_b, :]
                f = fwd_ref[i, at_f, :] if base else zero
                b = bwd_ref[i, at_b, :] if base else zero
                for m in range(GROUP):
                    h[m] = w[m] * h[m] + x
                    r[m] = w[m] * r[m] + y
                    f = f + a[m] * h[m]
                    b = b + a[m] * r[m]
                fwd_ref[i, at_f, :] = f
                bwd_ref[i, at_b, :] = b
        return 0

    lax.fori_loop(0, tiles, one, 0)


def combine(level, count, own, got, dec_t, s, r):
    modes = dec_t.shape[0]
    at = lax.axis_index("seq")
    right = lax.rem(lax.div(at, 2**level), 2) == 1
    offset = lax.rem(at, 2**level).astype(F32)
    span = float(count * 2**level)

    def half(i, n=modes):
        mine = own[pl.ds(i * modes, n), :].astype(F32)
        other = got[pl.ds(i * modes, n), :].astype(F32)
        return jnp.where(right, other, mine), jnp.where(right, mine, other)

    e_l, e_r = half(0)
    f_l, f_r = half(1)
    g_l, g_r = half(2)
    h_l, h_r = half(3)
    p_l, p_r = half(4)
    d_l, d_r = half(5)
    k_l, k_r = half(6, 16)
    decay = jnp.exp(-dec_t * span)
    ds = dec_t * span
    block = (
        decay * e_l + e_r,
        decay * (f_l - ds * e_l) + f_r,
        g_l + decay * g_r,
        h_l + decay * (h_r - ds * g_r),
        p_l + p_r + e_l * g_r,
        d_l + d_r + f_l * g_r + e_l * h_r,
        k_l + k_r,
    )
    into = jnp.exp(dec_t * (-float(count) * offset)) * e_l
    back = jnp.exp(dec_t * (-float(count) * (float(2**level - 1) - offset))) * g_r
    return block, s + jnp.where(right, into, 0.0), r + jnp.where(right, 0.0, back)


def combine_kernel(level, count, own, got, dec_t_ref, s_ref, r_ref, z_ref, s_out, r_out):
    modes = dec_t_ref.shape[0]
    block, s, r = combine(level, count, own, got, dec_t_ref[...], s_ref[...], r_ref[...])
    for i, part in enumerate(block):
        z_ref[pl.ds(i * modes, part.shape[0]), :] = part.astype(BF16)
    s_out[...] = s
    r_out[...] = r


def finish_kernel(
    level, count,
    own, got, dec_t_ref, s_ref, r_ref, res_t_ref, skip_ref,
    q_ref, k_ref, v_ref, u_ref, fwd_ref, bwd_ref, in_ref, out_ref, in0_ref, out0_ref,
    dq_ref, dk_ref, dv_ref, dres_ref, ddec_ref, dskip_ref,
    f_ref, b_ref, sv_ref, rv_ref, w_ref,
):
    rows, width = q_ref.shape
    modes = dec_t_ref.shape[0]
    steps = rows // SEGS
    dec_t = dec_t_ref[...]
    block, s, r = combine(level, count, own, got, dec_t, s_ref[...], r_ref[...])
    roots = jnp.sqrt(dec_t)
    dres_ref[...] = roots * block[4]
    ddec_ref[...] = res_t_ref[...] / roots * block[5]
    dskip_ref[...] = block[6][:1]
    sv_ref[...] = s
    rv_ref[...] = r
    w_ref[...] = jnp.exp(-dec_t)

    def one(i, _):
        ln = lanes_of(i)

        def spread(ref, m):
            return jnp.broadcast_to(ref[pl.ds(m, 1), ln], (SEGS, LANES))

        w = [spread(w_ref, m) for m in range(modes)]
        at = [pl.ds(m * SEGS, SEGS) for m in range(modes)]
        c = [in_ref[i, at[m], :] * spread(sv_ref, m) + in0_ref[i, at[m], :] for m in range(modes)]
        for j in range(steps):
            here = pl.ds(j * SEGS, SEGS)
            f = fwd_ref[i, here, :]
            for m in range(modes):
                f = f + c[m]
                c[m] = c[m] * w[m]
            f_ref[i, here, :] = f
        c = [out_ref[i, at[m], :] * spread(rv_ref, m) + out0_ref[i, at[m], :] for m in range(modes)]
        for j in range(steps - 1, -1, -1):
            here = pl.ds(j * SEGS, SEGS)
            b = bwd_ref[i, here, :]
            for m in range(modes):
                b = b + c[m]
                c[m] = c[m] * w[m]
            b_ref[i, here, :] = b
        return 0

    lax.fori_loop(0, width // LANES, one, 0)

    for i in range(width // LANES):
        ln = slice(i * LANES, (i + 1) * LANES)
        skip = skip_ref[:, ln]
        for seg in range(SEGS):
            for part in range(steps // 16):
                at = slice(seg * steps + part * 16, seg * steps + part * 16 + 16)
                frm = pl.ds(part * 16 * SEGS + seg, 16, stride=SEGS)
                q, k, v, u = (ref[at, ln].astype(F32) for ref in (q_ref, k_ref, v_ref, u_ref))
                gated = (k * v).astype(BF16).astype(F32)
                grad = (u * q).astype(BF16).astype(F32)
                conv = (f_ref[i, frm, :] + skip * gated).astype(BF16).astype(F32)
                dq_ref[at, ln] = (u * conv).astype(BF16)
                gg = (b_ref[i, frm, :] + skip * grad).astype(BF16).astype(F32)
                dk_ref[at, ln] = (gg * v).astype(BF16)
                dv_ref[at, ln] = (gg * k).astype(BF16)


def kept(array, space=VMEM):
    return pltpu.with_memory_space_constraint(array, space)


def call(kernel, outs, args, scratch=(), flops=0, name=None, hbm=0):
    return pl.pallas_call(
        kernel,
        out_shape=outs,
        in_specs=[pl.BlockSpec(memory_space=pltpu.HBM)] * hbm + [pl.BlockSpec(memory_space=VMEM)] * (len(args) - hbm),
        out_specs=[pl.BlockSpec(memory_space=VMEM)] * len(outs),
        scratch_shapes=list(scratch),
        cost_estimate=pl.CostEstimate(flops=flops, bytes_accessed=1 << 19, transcendentals=0),
        compiler_params=pltpu.CompilerParams(vmem_limit_bytes=24 << 20),
        name=name,
    )(*[kept(a, pltpu.HBM) for a in args[:hbm]], *[kept(a) for a in args[hbm:]])


def exchange(array, mask, size):
    return lax.ppermute(array, "seq", [(i, i ^ mask) for i in range(size)])


def shards(queries, keys, values, upstream, residues, decay, skip):
    rows, width = queries.shape
    modes = residues.shape[1]
    size = lax.axis_size("seq")
    masks = (1, 3, 4, 12, 16, 48)
    seg_rows = modes * SEGS
    z_rows = 6 * modes + 16
    tiles = width // LANES
    big = VMEM((tiles, rows, LANES), F32)
    state = VMEM((modes, width), F32)
    spread = VMEM((tiles, seg_rows, LANES), F32)
    block = VMEM((z_rows, width), BF16)
    local = VMEM((rows, width), BF16)
    z, gated, grad, pre, post, dec_t, keys, values, upstream, queries = call(
        summary_kernel,
        [block, big, big, spread, spread, state] + [local] * 4,
        [decay.T, keys, values, upstream, queries],
        [spread] * 7 + [pltpu.SemaphoreType.DMA((5,))],
        flops=12 * rows * width * modes,
        name="summary",
        hbm=5,
    )
    fwd, bwd, in_w, out_w, in_0, out_0, res_t, skip = call(
        conv_kernel,
        [big, big, spread, spread, spread, spread, state, VMEM((1, width), F32)],
        [residues.T, skip.reshape(1, width), gated, grad, dec_t, pre, post],
        [spread] * 2 + [pltpu.SemaphoreType.DMA((2,))],
        flops=8 * rows * width * modes,
        name="conv",
        hbm=2,
    )
    s = jnp.zeros((modes, width), F32)
    r = jnp.zeros((modes, width), F32)
    for level, mask in enumerate(masks[:-1]):
        got = exchange(z, mask, size)
        z, s, r = call(
            functools.partial(combine_kernel, level, rows),
            [block, state, state],
            [z, got, dec_t, s, r],
            name=f"combine{level}",
        )
    got = exchange(z, masks[-1], size)
    outs = [jax.ShapeDtypeStruct((rows, width), BF16)] * 3
    outs += [jax.ShapeDtypeStruct((modes, width), F32)] * 2
    outs += [jax.ShapeDtypeStruct((1, width), F32)]
    dq, dk, dv, dres, ddec, dskip = call(
        functools.partial(finish_kernel, len(masks) - 1, rows),
        outs,
        [z, got, dec_t, s, r, res_t, skip, queries, keys, values, upstream, fwd, bwd, in_w, out_w, in_0, out_0],
        [big, big, state, state, state],
        name="finish",
    )
    return dq, dk, dv, dres.T, ddec.T, dskip.reshape(width)


def solution(mesh):
    tokens = P("seq", "chan")
    return jax.shard_map(
        shards,
        mesh=mesh,
        in_specs=(tokens, tokens, tokens, tokens, P("chan", None), P("chan", None), P("chan")),
        out_specs=(tokens, tokens, tokens, P("chan", None), P("chan", None), P("chan")),
        check_vma=False,
    )
```

time: 582 us -> 40.1 us (0.07)
  the two profiles are of different devices: /device:TPU:32 before, /device:TPU:6 now
where the time goes in v1:
time: 40.1 us; the launch traced here: 39.8 us
  starting transfers between devices  18 us (45%)
  waiting for transfers between devices  14.1 us (35%)
  Pallas kernels  7.1 us (18%)
  between operations  0.69 us (2%)
    ppermute x6, starting transfers between devices, exchange(): return lax.ppermute(array, 'seq', [(i, i ^ mask) for i in range(size)])  18 us
    ppermute x6, waiting for transfers between devices, exchange(): return lax.ppermute(array, 'seq', [(i, i ^ mask) for i in range(size)])  14.1 us
    pallas_call x8, Pallas kernels, call(): pl.pallas_call(kernel, out_shape=outs, in_specs=[pl.BlockSpec(memory_spac...  7.1 us
  transfers between devices with their start and end apart: 6, of which 6 were waited for; matrix products, arithmetic and copies ran while one was open for 0% of the time, Pallas kernels for 5%

profile of v1, /device:TPU:6, one launch (start us, length us, event | category | flops | bytes accessed | tf_op | source)
XLA Modules:
  0.0 39.8 jit_solution(1394619360357087214)
XLA Ops:
  0.6 3.3 %summary.1 = (bf16[112,256]{1,0:T(8,128)(2,1)S(1)}, f32[2,256,128]{2,1,0:T(8,128)S(1)}, f32[2,256,128]{2,1,0:T(8,128)S(1)}, f32[2,128,128]{2,1,0:T(8,128)S(1)}, ...) custom-call(f32[16,256]{1,0:T(8,128)} %bitcast.6, ...), custom_call_target="tpu_custom_call" | custom-call | flops 12582912 | bytes 524288 | tf_op jit(solution)/shard_map/summary/pallas_call | solution.py:296
  4.0 0.9 %collective-permute-start = (bf16[112,256]{1,0:T(8,128)(2,1)S(1)}, bf16[112,256]{1,0:T(8,128)(2,1)S(1)}, u32[]{:S(2)}, u32[]{:S(2)}) collective-permute-start(bf16[112,256]{1,0:T(8,128)(2,1)S(1)} %get-tuple-element.45.own), channel_id=1, source_target_pairs={{0,4},{4,0},{8,12},{12,8},{16,20},{20,16},{24,28},{28,24},{32,36},... | collective-permute-start | bytes 172040 | tf_op jit(solution)/shard_map/ppermute | solution.py:309
  4.9 3.3 %collective-permute-done.got = bf16[112,256]{1,0:T(8,128)(2,1)S(1)} collective-permute-done((bf16[112,256]{1,0:T(8,128)(2,1)S(1)}, bf16[112,256]{1,0:T(8,128)(2,1)S(1)}, u32[]{:S(2)}, u32[]{:S(2)}) %collective-permute-start) | collective-permute-done | bytes 57376 | tf_op jit(solution)/shard_map/ppermute | solution.py:309
  8.2 0.1 combine0.1
  8.3 2.3 %collective-permute-start.1 = (bf16[112,256]{1,0:T(8,128)(2,1)S(1)}, bf16[112,256]{1,0:T(8,128)(2,1)S(1)}, u32[]{:S(2)}, u32[]{:S(2)}) collective-permute-start(bf16[112,256]{1,0:T(8,128)(2,1)S(1)} %get-tuple-element.47.own), channel_id=1, source_target_pairs={{0,12},{4,8},{8,4},{12,0},{16,28},{20,24},{24,20},{28,16},{32,44},... | collective-permute-start | bytes 172040 | tf_op jit(solution)/shard_map/ppermute | solution.py:309
  10.6 3.2 %collective-permute-done.1.got = bf16[112,256]{1,0:T(8,128)(2,1)S(1)} collective-permute-done((bf16[112,256]{1,0:T(8,128)(2,1)S(1)}, bf16[112,256]{1,0:T(8,128)(2,1)S(1)}, u32[]{:S(2)}, u32[]{:S(2)}) %collective-permute-start.1) | collective-permute-done | bytes 57376 | tf_op jit(solution)/shard_map/ppermute | solution.py:309
  13.8 0.1 combine1.1
  13.8 1.7 %collective-permute-start.2 = (bf16[112,256]{1,0:T(8,128)(2,1)S(1)}, bf16[112,256]{1,0:T(8,128)(2,1)S(1)}, u32[]{:S(2)}, u32[]{:S(2)}) collective-permute-start(bf16[112,256]{1,0:T(8,128)(2,1)S(1)} %get-tuple-element.50.own), channel_id=1, source_target_pairs={{0,16},{4,20},{8,24},{12,28},{16,0},{20,4},{24,8},{28,12},{32,48},... | collective-permute-start | bytes 172040 | tf_op jit(solution)/shard_map/ppermute | solution.py:309
  15.5 2.6 %collective-permute-done.2.got = bf16[112,256]{1,0:T(8,128)(2,1)S(1)} collective-permute-done((bf16[112,256]{1,0:T(8,128)(2,1)S(1)}, bf16[112,256]{1,0:T(8,128)(2,1)S(1)}, u32[]{:S(2)}, u32[]{:S(2)}) %collective-permute-start.2) | collective-permute-done | bytes 57376 | tf_op jit(solution)/shard_map/ppermute | solution.py:309
  18.1 0.1 combine2.1
  18.2 3.1 %collective-permute-start.3 = (bf16[112,256]{1,0:T(8,128)(2,1)S(1)}, bf16[112,256]{1,0:T(8,128)(2,1)S(1)}, u32[]{:S(2)}, u32[]{:S(2)}) collective-permute-start(bf16[112,256]{1,0:T(8,128)(2,1)S(1)} %get-tuple-element.53.own), channel_id=1, source_target_pairs={{0,48},{4,52},{8,56},{12,60},{16,32},{20,36},{24,40},{28,44},{32,1... | collective-permute-start | bytes 172040 | tf_op jit(solution)/shard_map/ppermute | solution.py:309
  21.3 2.4 %collective-permute-done.3.got = bf16[112,256]{1,0:T(8,128)(2,1)S(1)} collective-permute-done((bf16[112,256]{1,0:T(8,128)(2,1)S(1)}, bf16[112,256]{1,0:T(8,128)(2,1)S(1)}, u32[]{:S(2)}, u32[]{:S(2)}) %collective-permute-start.3) | collective-permute-done | bytes 57376 | tf_op jit(solution)/shard_map/ppermute | solution.py:309
  23.6 0.1 combine3.1
  23.7 3.4 %collective-permute-start.4 = (bf16[112,256]{1,0:T(8,128)(2,1)S(1)}, bf16[112,256]{1,0:T(8,128)(2,1)S(1)}, u32[]{:S(2)}, u32[]{:S(2)}) collective-permute-start(bf16[112,256]{1,0:T(8,128)(2,1)S(1)} %get-tuple-element.56.own), channel_id=1, source_target_pairs={{0,64},{4,68},{8,72},{12,76},{16,80},{20,84},{24,88},{28,92},{32,9... | collective-permute-start | bytes 172040 | tf_op jit(solution)/shard_map/ppermute | solution.py:309
  27.1 2.2 %collective-permute-done.4.got = bf16[112,256]{1,0:T(8,128)(2,1)S(1)} collective-permute-done((bf16[112,256]{1,0:T(8,128)(2,1)S(1)}, bf16[112,256]{1,0:T(8,128)(2,1)S(1)}, u32[]{:S(2)}, u32[]{:S(2)}) %collective-permute-start.4) | collective-permute-done | bytes 57376 | tf_op jit(solution)/shard_map/ppermute | solution.py:309
  29.2 0.1 combine4.1
  29.3 6.6 %collective-permute-start.5 = (bf16[112,256]{1,0:T(8,128)(2,1)S(1)}, bf16[112,256]{1,0:T(8,128)(2,1)S(1)}, u32[]{:S(2)}, u32[]{:S(2)}) collective-permute-start(bf16[112,256]{1,0:T(8,128)(2,1)S(1)} %get-tuple-element.59.own), channel_id=1, source_target_pairs={{0,192},{4,196},{8,200},{12,204},{16,208},{20,212},{24,216},{28,22... | collective-permute-start | bytes 172040 | tf_op jit(solution)/shard_map/ppermute | solution.py:309
  35.9 1.9 %conv.1 = (f32[2,256,128]{2,1,0:T(8,128)S(1)}, f32[2,256,128]{2,1,0:T(8,128)S(1)}, f32[2,128,128]{2,1,0:T(8,128)S(1)}, f32[2,128,128]{2,1,0:T(8,128)S(1)}, f32[2...) custom-call(f32[16,256]{1,0:T(8,128)} %bitcast.7, ...), custom_call_target="tpu_custom_call" | custom-call | flops 8388608 | bytes 524288 | tf_op jit(solution)/shard_map/conv/pallas_call | solution.py:296
  37.9 0.4 %collective-permute-done.5.got = bf16[112,256]{1,0:T(8,128)(2,1)S(1)} collective-permute-done((bf16[112,256]{1,0:T(8,128)(2,1)S(1)}, bf16[112,256]{1,0:T(8,128)(2,1)S(1)}, u32[]{:S(2)}, u32[]{:S(2)}) %collective-permute-start.5) | collective-permute-done | bytes 57376 | tf_op jit(solution)/shard_map/ppermute | solution.py:309
  38.3 1.6 %finish.1 = (bf16[256,256]{1,0:T(8,128)(2,1)}, bf16[256,256]{1,0:T(8,128)(2,1)}, bf16[256,256]{1,0:T(8,128)(2,1)}, f32[16,256]{1,0:T(8,128)}, f32[16,256]{1,0:T(8,128)}, /*index=5*/f32[1,256]{1,0:T(1,128)}) custom-call(bf16[112,256]{1,0:T(8,128)(2,1)S(1)} %get-tuple-element.59.own, bf16[112,256]{1,0:T(8,128)(2,1)S(1)} %collective-permute-done.5.got, ...), custom_call_target="tpu_custom_call" | custom-call | bytes 524288 | tf_op jit(solution)/shard_map/finish/pallas_call | solution.py:296
  (1 shorter events, 0.0 us)
Async XLA Ops:
  4.0 4.3 %collective-permute-start = (bf16[112,256]{1,0:T(8,128)(2,1)S(1)}, bf16[112,256]{1,0:T(8,128)(2,1)S(1)}, u32[]{:S(2)}, u32[]{:S(2)}) collective-permute-start(bf16[112,256]{1,0:T(8,128)(2,1)S(1)} %get-tuple-element.45.own), channel_id=1, source_target_pairs={{0,4},{4,0},{8,12},{12,8},{16,20},{20,16},{24,28},{28,24},{32,36},... | collective-permute-start | bytes 172040 | tf_op jit(solution)/shard_map/ppermute | solution.py:309
  8.3 5.5 %collective-permute-start.1 = (bf16[112,256]{1,0:T(8,128)(2,1)S(1)}, bf16[112,256]{1,0:T(8,128)(2,1)S(1)}, u32[]{:S(2)}, u32[]{:S(2)}) collective-permute-start(bf16[112,256]{1,0:T(8,128)(2,1)S(1)} %get-tuple-element.47.own), channel_id=1, source_target_pairs={{0,12},{4,8},{8,4},{12,0},{16,28},{20,24},{24,20},{28,16},{32,44},... | collective-permute-start | bytes 172040 | tf_op jit(solution)/shard_map/ppermute | solution.py:309
  13.8 4.3 %collective-permute-start.2 = (bf16[112,256]{1,0:T(8,128)(2,1)S(1)}, bf16[112,256]{1,0:T(8,128)(2,1)S(1)}, u32[]{:S(2)}, u32[]{:S(2)}) collective-permute-start(bf16[112,256]{1,0:T(8,128)(2,1)S(1)} %get-tuple-element.50.own), channel_id=1, source_target_pairs={{0,16},{4,20},{8,24},{12,28},{16,0},{20,4},{24,8},{28,12},{32,48},... | collective-permute-start | bytes 172040 | tf_op jit(solution)/shard_map/ppermute | solution.py:309
  18.2 5.5 %collective-permute-start.3 = (bf16[112,256]{1,0:T(8,128)(2,1)S(1)}, bf16[112,256]{1,0:T(8,128)(2,1)S(1)}, u32[]{:S(2)}, u32[]{:S(2)}) collective-permute-start(bf16[112,256]{1,0:T(8,128)(2,1)S(1)} %get-tuple-element.53.own), channel_id=1, source_target_pairs={{0,48},{4,52},{8,56},{12,60},{16,32},{20,36},{24,40},{28,44},{32,1... | collective-permute-start | bytes 172040 | tf_op jit(solution)/shard_map/ppermute | solution.py:309
  23.7 5.5 %collective-permute-start.4 = (bf16[112,256]{1,0:T(8,128)(2,1)S(1)}, bf16[112,256]{1,0:T(8,128)(2,1)S(1)}, u32[]{:S(2)}, u32[]{:S(2)}) collective-permute-start(bf16[112,256]{1,0:T(8,128)(2,1)S(1)} %get-tuple-element.56.own), channel_id=1, source_target_pairs={{0,64},{4,68},{8,72},{12,76},{16,80},{20,84},{24,88},{28,92},{32,9... | collective-permute-start | bytes 172040 | tf_op jit(solution)/shard_map/ppermute | solution.py:309
  29.3 9.0 %collective-permute-start.5 = (bf16[112,256]{1,0:T(8,128)(2,1)S(1)}, bf16[112,256]{1,0:T(8,128)(2,1)S(1)}, u32[]{:S(2)}, u32[]{:S(2)}) collective-permute-start(bf16[112,256]{1,0:T(8,128)(2,1)S(1)} %get-tuple-element.59.own), channel_id=1, source_target_pairs={{0,192},{4,196},{8,200},{12,204},{16,208},{20,212},{24,216},{28,22... | collective-permute-start | bytes 172040 | tf_op jit(solution)/shard_map/ppermute | solution.py:309

commit v2 on v1

--- a/solution.py
+++ b/solution.py
@@ -179,44 +179,51 @@
     lax.fori_loop(0, tiles, one, 0)
 
 
-def combine(level, count, own, got, dec_t, s, r):
+def combine(level, count, parts, dec_t, s, r):
     modes = dec_t.shape[0]
     at = lax.axis_index("seq")
-    right = lax.rem(lax.div(at, 2**level), 2) == 1
-    offset = lax.rem(at, 2**level).astype(F32)
-    span = float(count * 2**level)
-
-    def half(i, n=modes):
-        mine = own[pl.ds(i * modes, n), :].astype(F32)
-        other = got[pl.ds(i * modes, n), :].astype(F32)
-        return jnp.where(right, other, mine), jnp.where(right, mine, other)
-
-    e_l, e_r = half(0)
-    f_l, f_r = half(1)
-    g_l, g_r = half(2)
-    h_l, h_r = half(3)
-    p_l, p_r = half(4)
-    d_l, d_r = half(5)
-    k_l, k_r = half(6, 16)
-    decay = jnp.exp(-dec_t * span)
-    ds = dec_t * span
-    block = (
-        decay * e_l + e_r,
-        decay * (f_l - ds * e_l) + f_r,
-        g_l + decay * g_r,
-        h_l + decay * (h_r - ds * g_r),
-        p_l + p_r + e_l * g_r,
-        d_l + d_r + f_l * g_r + e_l * h_r,
-        k_l + k_r,
-    )
-    into = jnp.exp(dec_t * (-float(count) * offset)) * e_l
-    back = jnp.exp(dec_t * (-float(count) * (float(2**level - 1) - offset))) * g_r
-    return block, s + jnp.where(right, into, 0.0), r + jnp.where(right, 0.0, back)
-
-
-def combine_kernel(level, count, own, got, dec_t_ref, s_ref, r_ref, z_ref, s_out, r_out):
+    digit = lax.rem(lax.div(at, 4**level), 4)
+    offset = lax.rem(at, 4**level).astype(F32)
+    span = float(count * 4**level)
+
+    def gather(i, n=modes):
+        have = [part[pl.ds(i * modes, n), :].astype(F32) for part in parts]
+        pick = []
+        for j in range(4):
+            away = digit ^ j
+            pick.append(
+                jnp.where(away >= 2, jnp.where(away == 2, have[2], have[3]), jnp.where(away == 0, have[0], have[1]))
+            )
+        return pick
+
+    e, f, g, h, p, d = (gather(i) for i in range(6))
+    k = gather(6, 16)
+    one = dec_t * span
+    w = [jnp.exp(one * (-float(j))) for j in range(4)]
+    e_t, f_t, g_t, h_t, p_t, d_t, k_t = e[0], f[0], g[0], h[0], p[0], d[0], k[0]
+    enter = jnp.zeros_like(s)
+    for j in range(1, 4):
+        enter = jnp.where(digit == j, e_t, enter)
+        p_t = p_t + p[j] + e_t * g[j]
+        d_t = d_t + d[j] + f_t * g[j] + e_t * h[j]
+        f_t = w[1] * (f_t - one * e_t) + f[j]
+        e_t = w[1] * e_t + e[j]
+        h_t = h_t + w[j] * (h[j] - one * float(j) * g[j])
+        g_t = g_t + w[j] * g[j]
+        k_t = k_t + k[j]
+    leave = jnp.zeros_like(r)
+    tail = g[3]
+    for j in range(2, -1, -1):
+        leave = jnp.where(digit == j, tail, leave)
+        tail = g[j] + w[1] * tail
+    s = s + jnp.exp(dec_t * (-float(count) * offset)) * enter
+    r = r + jnp.exp(dec_t * (-float(count) * (float(4**level - 1) - offset))) * leave
+    return (e_t, f_t, g_t, h_t, p_t, d_t, k_t), s, r
+
+
+def combine_kernel(level, count, z0, z1, z2, z3, dec_t_ref, s_ref, r_ref, z_ref, s_out, r_out):
     modes = dec_t_ref.shape[0]
-    block, s, r = combine(level, count, own, got, dec_t_ref[...], s_ref[...], r_ref[...])
+    block, s, r = combine(level, count, (z0, z1, z2, z3), dec_t_ref[...], s_ref[...], r_ref[...])
     for i, part in enumerate(block):
         z_ref[pl.ds(i * modes, part.shape[0]), :] = part.astype(BF16)
     s_out[...] = s
@@ -225,7 +232,7 @@
 
 def finish_kernel(
     level, count,
-    own, got, dec_t_ref, s_ref, r_ref, res_t_ref, skip_ref,
+    z0, z1, z2, z3, dec_t_ref, s_ref, r_ref, res_t_ref, skip_ref,
     q_ref, k_ref, v_ref, u_ref, fwd_ref, bwd_ref, in_ref, out_ref, in0_ref, out0_ref,
     dq_ref, dk_ref, dv_ref, dres_ref, ddec_ref, dskip_ref,
     f_ref, b_ref, sv_ref, rv_ref, w_ref,
@@ -234,7 +241,7 @@
     modes = dec_t_ref.shape[0]
     steps = rows // SEGS
     dec_t = dec_t_ref[...]
-    block, s, r = combine(level, count, own, got, dec_t, s_ref[...], r_ref[...])
+    block, s, r = combine(level, count, (z0, z1, z2, z3), dec_t, s_ref[...], r_ref[...])
     roots = jnp.sqrt(dec_t)
     dres_ref[...] = roots * block[4]
     ddec_ref[...] = res_t_ref[...] / roots * block[5]
@@ -305,15 +312,18 @@
     )(*[kept(a, pltpu.HBM) for a in args[:hbm]], *[kept(a) for a in args[hbm:]])
 
 
-def exchange(array, mask, size):
-    return lax.ppermute(array, "seq", [(i, i ^ mask) for i in range(size)])
+def exchange(array, level, size):
+    got = {}
+    for k in (2, 3, 1):
+        got[k] = lax.ppermute(array, "seq", [(i, i ^ (k * 4**level)) for i in range(size)])
+    return [array, got[1], got[2], got[3]]
 
 
 def shards(queries, keys, values, upstream, residues, decay, skip):
     rows, width = queries.shape
     modes = residues.shape[1]
     size = lax.axis_size("seq")
-    masks = (1, 3, 4, 12, 16, 48)
+    levels = 3
     seg_rows = modes * SEGS
     z_rows = 6 * modes + 16
     tiles = width // LANES
@@ -342,22 +352,20 @@
     )
     s = jnp.zeros((modes, width), F32)
     r = jnp.zeros((modes, width), F32)
-    for level, mask in enumerate(masks[:-1]):
-        got = exchange(z, mask, size)
+    for level in range(levels - 1):
         z, s, r = call(
             functools.partial(combine_kernel, level, rows),
             [block, state, state],
-            [z, got, dec_t, s, r],
+            [*exchange(z, level, size), dec_t, s, r],
             name=f"combine{level}",
         )
-    got = exchange(z, masks[-1], size)
     outs = [jax.ShapeDtypeStruct((rows, width), BF16)] * 3
     outs += [jax.ShapeDtypeStruct((modes, width), F32)] * 2
     outs += [jax.ShapeDtypeStruct((1, width), F32)]
     dq, dk, dv, dres, ddec, dskip = call(
-        functools.partial(finish_kernel, len(masks) - 1, rows),
+        functools.partial(finish_kernel, levels - 1, rows),
         outs,
-        [z, got, dec_t, s, r, res_t, skip, queries, keys, values, upstream, fwd, bwd, in_w, out_w, in_0, out_0],
+        [*exchange(z, levels - 1, size), dec_t, s, r, res_t, skip, queries, keys, values, upstream, fwd, bwd, in_w, out_w, in_0, out_0],
         [big, big, state, state, state],
         name="finish",
     )

time: 40.1 us -> 37.1 us (0.925)
  the two profiles are of different devices: /device:TPU:6 before, /device:TPU:32 now
where the time goes in v2:
time: 37.1 us; the launch traced here: 36.7 us
  starting transfers between devices  16.3 us (44%)
  waiting for transfers between devices  12.6 us (34%)
  Pallas kernels  7.15 us (19%)
  between operations  0.68 us (2%)
    ppermute x9, starting transfers between devices, exchange(): lax.ppermute(array, 'seq', [(i, i ^ k * 4 ** level) for i in range(size)])  16.3 us
    ppermute x9, waiting for transfers between devices, exchange(): lax.ppermute(array, 'seq', [(i, i ^ k * 4 ** level) for i in range(size)])  12.6 us
    pallas_call x5, Pallas kernels, call(): pl.pallas_call(kernel, out_shape=outs, in_specs=[pl.BlockSpec(memory_spac...  7.15 us
  transfers between devices with their start and end apart: 9, of which 5 were waited for; matrix products, arithmetic and copies ran while one was open for 0% of the time, Pallas kernels for 5%

profile of v2, /device:TPU:32, one launch (start us, length us, event | category | flops | bytes accessed | tf_op | source)
XLA Modules:
  0.0 36.7 jit_solution(10541911083935143540)
XLA Ops:
  0.6 3.3 %summary.1 = (bf16[112,256]{1,0:T(8,128)(2,1)S(1)}, f32[2,256,128]{2,1,0:T(8,128)S(1)}, f32[2,256,128]{2,1,0:T(8,128)S(1)}, f32[2,128,128]{2,1,0:T(8,128)S(1)}, ...) custom-call(f32[16,256]{1,0:T(8,128)} %bitcast.6, ...), custom_call_target="tpu_custom_call" | custom-call | flops 12582912 | bytes 524288 | tf_op jit(solution)/shard_map/summary/pallas_call | solution.py:303
  3.9 2.8 %collective-permute-start.2 = (bf16[112,256]{1,0:T(8,128)(2,1)S(1)}, bf16[112,256]{1,0:T(8,128)(2,1)S(1)}, u32[]{:S(2)}, u32[]{:S(2)}) collective-permute-start(bf16[112,256]{1,0:T(8,128)(2,1)S(1)} %get-tuple-element.36.z0), channel_id=1, source_target_pairs={{0,12},{4,8},{8,4},{12,0},{16,28},{20,24},{24,20},{28,16},{32,44},... | collective-permute-start | bytes 172040 | tf_op jit(solution)/shard_map/ppermute | solution.py:318
  6.8 0.8 %collective-permute-start.1 = (bf16[112,256]{1,0:T(8,128)(2,1)S(1)}, bf16[112,256]{1,0:T(8,128)(2,1)S(1)}, u32[]{:S(2)}, u32[]{:S(2)}) collective-permute-start(bf16[112,256]{1,0:T(8,128)(2,1)S(1)} %get-tuple-element.36.z0), channel_id=1, source_target_pairs={{0,8},{4,12},{8,0},{12,4},{16,24},{20,28},{24,16},{28,20},{32,40},... | collective-permute-start | bytes 172040 | tf_op jit(solution)/shard_map/ppermute | solution.py:318
  7.6 0.5 %collective-permute-start = (bf16[112,256]{1,0:T(8,128)(2,1)S(1)}, bf16[112,256]{1,0:T(8,128)(2,1)S(1)}, u32[]{:S(2)}, u32[]{:S(2)}) collective-permute-start(bf16[112,256]{1,0:T(8,128)(2,1)S(1)} %get-tuple-element.36.z0), channel_id=1, source_target_pairs={{0,4},{4,0},{8,12},{12,8},{16,20},{20,16},{24,28},{28,24},{32,36},... | collective-permute-start | bytes 172040 | tf_op jit(solution)/shard_map/ppermute | solution.py:318
  8.1 1.3 %collective-permute-done.2.z3 = bf16[112,256]{1,0:T(8,128)(2,1)S(1)} collective-permute-done((bf16[112,256]{1,0:T(8,128)(2,1)S(1)}, bf16[112,256]{1,0:T(8,128)(2,1)S(1)}, u32[]{:S(2)}, u32[]{:S(2)}) %collective-permute-start.2) | collective-permute-done | bytes 57376 | tf_op jit(solution)/shard_map/ppermute | solution.py:318
  9.4 3.1 %collective-permute-done.1.z2 = bf16[112,256]{1,0:T(8,128)(2,1)S(1)} collective-permute-done((bf16[112,256]{1,0:T(8,128)(2,1)S(1)}, bf16[112,256]{1,0:T(8,128)(2,1)S(1)}, u32[]{:S(2)}, u32[]{:S(2)}) %collective-permute-start.1) | collective-permute-done | bytes 57376 | tf_op jit(solution)/shard_map/ppermute | solution.py:318
  12.5 0.0 collective-permute-done.z1
  12.5 0.1 combine0.1
  12.6 3.1 %collective-permute-start.5 = (bf16[112,256]{1,0:T(8,128)(2,1)S(1)}, bf16[112,256]{1,0:T(8,128)(2,1)S(1)}, u32[]{:S(2)}, u32[]{:S(2)}) collective-permute-start(bf16[112,256]{1,0:T(8,128)(2,1)S(1)} %get-tuple-element.38.z0), channel_id=1, source_target_pairs={{0,48},{4,52},{8,56},{12,60},{16,32},{20,36},{24,40},{28,44},{32,1... | collective-permute-start | bytes 172040 | tf_op jit(solution)/shard_map/ppermute | solution.py:318
  15.7 0.6 %collective-permute-start.4 = (bf16[112,256]{1,0:T(8,128)(2,1)S(1)}, bf16[112,256]{1,0:T(8,128)(2,1)S(1)}, u32[]{:S(2)}, u32[]{:S(2)}) collective-permute-start(bf16[112,256]{1,0:T(8,128)(2,1)S(1)} %get-tuple-element.38.z0), channel_id=1, source_target_pairs={{0,32},{4,36},{8,40},{12,44},{16,48},{20,52},{24,56},{28,60},{32,0... | collective-permute-start | bytes 172040 | tf_op jit(solution)/shard_map/ppermute | solution.py:318
  16.3 0.5 %collective-permute-start.3 = (bf16[112,256]{1,0:T(8,128)(2,1)S(1)}, bf16[112,256]{1,0:T(8,128)(2,1)S(1)}, u32[]{:S(2)}, u32[]{:S(2)}) collective-permute-start(bf16[112,256]{1,0:T(8,128)(2,1)S(1)} %get-tuple-element.38.z0), channel_id=1, source_target_pairs={{0,16},{4,20},{8,24},{12,28},{16,0},{20,4},{24,8},{28,12},{32,48},... | collective-permute-start | bytes 172040 | tf_op jit(solution)/shard_map/ppermute | solution.py:318
  16.8 1.9 %collective-permute-done.5.z3 = bf16[112,256]{1,0:T(8,128)(2,1)S(1)} collective-permute-done((bf16[112,256]{1,0:T(8,128)(2,1)S(1)}, bf16[112,256]{1,0:T(8,128)(2,1)S(1)}, u32[]{:S(2)}, u32[]{:S(2)}) %collective-permute-start.5) | collective-permute-done | bytes 57376 | tf_op jit(solution)/shard_map/ppermute | solution.py:318
  18.7 2.7 %collective-permute-done.4.z2 = bf16[112,256]{1,0:T(8,128)(2,1)S(1)} collective-permute-done((bf16[112,256]{1,0:T(8,128)(2,1)S(1)}, bf16[112,256]{1,0:T(8,128)(2,1)S(1)}, u32[]{:S(2)}, u32[]{:S(2)}) %collective-permute-start.4) | collective-permute-done | bytes 57376 | tf_op jit(solution)/shard_map/ppermute | solution.py:318
  21.4 0.0 collective-permute-done.3.z1
  21.4 0.1 combine1.1
  21.5 5.5 %collective-permute-start.8 = (bf16[112,256]{1,0:T(8,128)(2,1)S(1)}, bf16[112,256]{1,0:T(8,128)(2,1)S(1)}, u32[]{:S(2)}, u32[]{:S(2)}) collective-permute-start(bf16[112,256]{1,0:T(8,128)(2,1)S(1)} %get-tuple-element.41.z0), channel_id=1, source_target_pairs={{0,192},{4,196},{8,200},{12,204},{16,208},{20,212},{24,216},{28,22... | collective-permute-start | bytes 172040 | tf_op jit(solution)/shard_map/ppermute | solution.py:318
  27.0 1.4 %collective-permute-start.7 = (bf16[112,256]{1,0:T(8,128)(2,1)S(1)}, bf16[112,256]{1,0:T(8,128)(2,1)S(1)}, u32[]{:S(2)}, u32[]{:S(2)}) collective-permute-start(bf16[112,256]{1,0:T(8,128)(2,1)S(1)} %get-tuple-element.41.z0), channel_id=1, source_target_pairs={{0,128},{4,132},{8,136},{12,140},{16,144},{20,148},{24,152},{28,15... | collective-permute-start | bytes 172040 | tf_op jit(solution)/shard_map/ppermute | solution.py:318
  28.5 1.0 %collective-permute-start.6 = (bf16[112,256]{1,0:T(8,128)(2,1)S(1)}, bf16[112,256]{1,0:T(8,128)(2,1)S(1)}, u32[]{:S(2)}, u32[]{:S(2)}) collective-permute-start(bf16[112,256]{1,0:T(8,128)(2,1)S(1)} %get-tuple-element.41.z0), channel_id=1, source_target_pairs={{0,64},{4,68},{8,72},{12,76},{16,80},{20,84},{24,88},{28,92},{32,9... | collective-permute-start | bytes 172040 | tf_op jit(solution)/shard_map/ppermute | solution.py:318
  29.5 2.0 %conv.1 = (f32[2,256,128]{2,1,0:T(8,128)S(1)}, f32[2,256,128]{2,1,0:T(8,128)S(1)}, f32[2,128,128]{2,1,0:T(8,128)S(1)}, f32[2,128,128]{2,1,0:T(8,128)S(1)}, f32[2...) custom-call(f32[16,256]{1,0:T(8,128)} %bitcast.7, ...), custom_call_target="tpu_custom_call" | custom-call | flops 8388608 | bytes 524288 | tf_op jit(solution)/shard_map/conv/pallas_call | solution.py:303
  31.5 0.0 collective-permute-done.8.z3
  31.5 3.6 %collective-permute-done.7.z2 = bf16[112,256]{1,0:T(8,128)(2,1)S(1)} collective-permute-done((bf16[112,256]{1,0:T(8,128)(2,1)S(1)}, bf16[112,256]{1,0:T(8,128)(2,1)S(1)}, u32[]{:S(2)}, u32[]{:S(2)}) %collective-permute-start.7) | collective-permute-done | bytes 57376 | tf_op jit(solution)/shard_map/ppermute | solution.py:318
  35.1 0.0 collective-permute-done.6.z1
  35.1 1.6 %finish.1 = (bf16[256,256]{1,0:T(8,128)(2,1)}, bf16[256,256]{1,0:T(8,128)(2,1)}, bf16[256,256]{1,0:T(8,128)(2,1)}, f32[16,256]{1,0:T(8,128)}, f32[16,256]{1,0:T(8,128)}, /*index=5*/f32[1,256]{1,0:T(1,128)}) custom-call(bf16[112,256]{1,0:T(8,128)(2,1)S(1)} %get-tuple-element.41.z0, bf16[112,256]{1,0:T(8,128)(2,1)S(1)} %collective-permute-done.6.z1, ...), custom_call_target="tpu_custom_call" | custom-call | bytes 524288 | tf_op jit(solution)/shard_map/finish/pallas_call | solution.py:303
  (1 shorter events, 0.0 us)
Async XLA Ops:
  3.9 5.5 %collective-permute-start.2 = (bf16[112,256]{1,0:T(8,128)(2,1)S(1)}, bf16[112,256]{1,0:T(8,128)(2,1)S(1)}, u32[]{:S(2)}, u32[]{:S(2)}) collective-permute-start(bf16[112,256]{1,0:T(8,128)(2,1)S(1)} %get-tuple-element.36.z0), channel_id=1, source_target_pairs={{0,12},{4,8},{8,4},{12,0},{16,28},{20,24},{24,20},{28,16},{32,44},... | collective-permute-start | bytes 172040 | tf_op jit(solution)/shard_map/ppermute | solution.py:318
  6.8 5.7 %collective-permute-start.1 = (bf16[112,256]{1,0:T(8,128)(2,1)S(1)}, bf16[112,256]{1,0:T(8,128)(2,1)S(1)}, u32[]{:S(2)}, u32[]{:S(2)}) collective-permute-start(bf16[112,256]{1,0:T(8,128)(2,1)S(1)} %get-tuple-element.36.z0), channel_id=1, source_target_pairs={{0,8},{4,12},{8,0},{12,4},{16,24},{20,28},{24,16},{28,20},{32,40},... | collective-permute-start | bytes 172040 | tf_op jit(solution)/shard_map/ppermute | solution.py:318
  7.6 4.9 %collective-permute-start = (bf16[112,256]{1,0:T(8,128)(2,1)S(1)}, bf16[112,256]{1,0:T(8,128)(2,1)S(1)}, u32[]{:S(2)}, u32[]{:S(2)}) collective-permute-start(bf16[112,256]{1,0:T(8,128)(2,1)S(1)} %get-tuple-element.36.z0), channel_id=1, source_target_pairs={{0,4},{4,0},{8,12},{12,8},{16,20},{20,16},{24,28},{28,24},{32,36},... | collective-permute-start | bytes 172040 | tf_op jit(solution)/shard_map/ppermute | solution.py:318
  12.6 6.1 %collective-permute-start.5 = (bf16[112,256]{1,0:T(8,128)(2,1)S(1)}, bf16[112,256]{1,0:T(8,128)(2,1)S(1)}, u32[]{:S(2)}, u32[]{:S(2)}) collective-permute-start(bf16[112,256]{1,0:T(8,128)(2,1)S(1)} %get-tuple-element.38.z0), channel_id=1, source_target_pairs={{0,48},{4,52},{8,56},{12,60},{16,32},{20,36},{24,40},{28,44},{32,1... | collective-permute-start | bytes 172040 | tf_op jit(solution)/shard_map/ppermute | solution.py:318
  15.7 5.7 %collective-permute-start.4 = (bf16[112,256]{1,0:T(8,128)(2,1)S(1)}, bf16[112,256]{1,0:T(8,128)(2,1)S(1)}, u32[]{:S(2)}, u32[]{:S(2)}) collective-permute-start(bf16[112,256]{1,0:T(8,128)(2,1)S(1)} %get-tuple-element.38.z0), channel_id=1, source_target_pairs={{0,32},{4,36},{8,40},{12,44},{16,48},{20,52},{24,56},{28,60},{32,0... | collective-permute-start | bytes 172040 | tf_op jit(solution)/shard_map/ppermute | solution.py:318
  16.3 5.1 %collective-permute-start.3 = (bf16[112,256]{1,0:T(8,128)(2,1)S(1)}, bf16[112,256]{1,0:T(8,128)(2,1)S(1)}, u32[]{:S(2)}, u32[]{:S(2)}) collective-permute-start(bf16[112,256]{1,0:T(8,128)(2,1)S(1)} %get-tuple-element.38.z0), channel_id=1, source_target_pairs={{0,16},{4,20},{8,24},{12,28},{16,0},{20,4},{24,8},{28,12},{32,48},... | collective-permute-start | bytes 172040 | tf_op jit(solution)/shard_map/ppermute | solution.py:318
  21.5 9.9 %collective-permute-start.8 = (bf16[112,256]{1,0:T(8,128)(2,1)S(1)}, bf16[112,256]{1,0:T(8,128)(2,1)S(1)}, u32[]{:S(2)}, u32[]{:S(2)}) collective-permute-start(bf16[112,256]{1,0:T(8,128)(2,1)S(1)} %get-tuple-element.41.z0), channel_id=1, source_target_pairs={{0,192},{4,196},{8,200},{12,204},{16,208},{20,212},{24,216},{28,22... | collective-permute-start | bytes 172040 | tf_op jit(solution)/shard_map/ppermute | solution.py:318
  27.0 8.1 %collective-permute-start.7 = (bf16[112,256]{1,0:T(8,128)(2,1)S(1)}, bf16[112,256]{1,0:T(8,128)(2,1)S(1)}, u32[]{:S(2)}, u32[]{:S(2)}) collective-permute-start(bf16[112,256]{1,0:T(8,128)(2,1)S(1)} %get-tuple-element.41.z0), channel_id=1, source_target_pairs={{0,128},{4,132},{8,136},{12,140},{16,144},{20,148},{24,152},{28,15... | collective-permute-start | bytes 172040 | tf_op jit(solution)/shard_map/ppermute | solution.py:318
  28.5 6.6 %collective-permute-start.6 = (bf16[112,256]{1,0:T(8,128)(2,1)S(1)}, bf16[112,256]{1,0:T(8,128)(2,1)S(1)}, u32[]{:S(2)}, u32[]{:S(2)}) collective-permute-start(bf16[112,256]{1,0:T(8,128)(2,1)S(1)} %get-tuple-element.41.z0), channel_id=1, source_target_pairs={{0,64},{4,68},{8,72},{12,76},{16,80},{20,84},{24,88},{28,92},{32,9... | collective-permute-start | bytes 172040 | tf_op jit(solution)/shard_map/ppermute | solution.py:318

commit v3 on v2

--- a/solution.py
+++ b/solution.py
@@ -13,6 +13,7 @@
 SEGS = 8
 LANES = 128
 GROUP = 4
+HALF = 8
 
 
 def product(a, b):
@@ -27,8 +28,8 @@
     return pl.ds(pl.multiple_of(i * n, n), n)
 
 
-def fetch(sems, *pairs):
-    copies = [pltpu.make_async_copy(a, b, sems.at[i]) for i, (a, b) in enumerate(pairs)]
+def fetch(sems, *pairs, first=0):
+    copies = [pltpu.make_async_copy(a, b, sems.at[first + i]) for i, (a, b) in enumerate(pairs)]
     for copy in copies:
         copy.start()
     return copies
@@ -39,11 +40,15 @@
     z_ref, gated_ref, grad_ref, pre_ref, post_ref, dec_t_ref, k_ref, v_ref, u_ref, q_ref,
     w_ref, e_ref, e1_ref, g_ref, g1_ref, p_ref, t_ref, sems,
 ):
-    copies = fetch(sems, (dec_hbm, dec_t_ref), (k_hbm, k_ref), (v_hbm, v_ref), (u_hbm, u_ref), (q_hbm, q_ref))
     rows, width = q_ref.shape
     modes = dec_t_ref.shape[0]
     steps = rows // SEGS
     tiles = width // LANES
+    columns = [pl.ds(i * LANES, LANES) for i in range(tiles)]
+    pairs = [(dec_hbm, dec_t_ref)]
+    for ln in columns:
+        pairs += [(a.at[:, ln], b.at[:, ln]) for a, b in ((k_hbm, k_ref), (v_hbm, v_ref), (u_hbm, u_ref), (q_hbm, q_ref))]
+    copies = fetch(sems, *pairs)
     copies[0].wait()
     dec_t = dec_t_ref[...]
     w_all = jnp.exp(-dec_t)
@@ -51,55 +56,49 @@
         for m in range(modes):
             row = w_all[m : m + 1, i * LANES : (i + 1) * LANES]
             w_ref[i, pl.ds(m * SEGS, SEGS), :] = jnp.broadcast_to(row, (SEGS, LANES))
-    for copy in copies[1:]:
-        copy.wait()
-    skip = jnp.zeros((8, width), F32)
-    for seg in range(SEGS):
-        for part in range(steps // 16):
-            at = pl.ds(seg * steps + part * 16, 16)
-            gated = product(k_ref[at, :], v_ref[at, :])
-            grad = product(u_ref[at, :], q_ref[at, :])
-            both = gated * grad
-            skip = skip + both[:8] + both[8:]
-            to = pl.ds(part * 16 * SEGS + seg, 16, stride=SEGS)
-            for i in range(tiles):
-                ln = slice(i * LANES, (i + 1) * LANES)
-                gated_ref[i, to, :] = gated[:, ln]
-                grad_ref[i, to, :] = grad[:, ln]
-    skip = jnp.sum(skip, axis=0, keepdims=True)
-
-    groups = modes // GROUP
-
-    def one(i, _):
-        ln = lax.div(i, groups)
-        base = lax.rem(i, groups) * GROUP
-        at = [rows_of(base + m, SEGS) for m in range(GROUP)]
-        w = [w_ref[ln, a, :] for a in at]
+
+    def one(base, i):
+        at = [pl.ds((base * GROUP + m) * SEGS, SEGS) for m in range(GROUP)]
+        w = [w_ref[i, a, :] for a in at]
         zero = jnp.zeros((SEGS, LANES), F32)
         h, h1, p, t, r, r1 = ([zero] * GROUP for _ in range(6))
         for j in range(steps):
-            x = gated_ref[ln, pl.ds(j * SEGS, SEGS), :]
-            y = grad_ref[ln, pl.ds(j * SEGS, SEGS), :]
-            back = grad_ref[ln, pl.ds((steps - 1 - j) * SEGS, SEGS), :]
+            x = gated_ref[i, pl.ds(j * SEGS, SEGS), :]
+            y = grad_ref[i, pl.ds(j * SEGS, SEGS), :]
+            back = grad_ref[i, pl.ds((steps - 1 - j) * SEGS, SEGS), :]
             for m in range(GROUP):
-                wh = w[m] * h[m]
-                h1[m] = w[m] * h1[m] + wh
-                h[m] = wh + x
+                h[m] = w[m] * h[m] + x
+                h1[m] = w[m] * h1[m] + h[m]
                 p[m] = p[m] + y * h[m]
                 t[m] = t[m] + y * h1[m]
-                wr = w[m] * r[m]
-                r1[m] = w[m] * r1[m] + wr
-                r[m] = wr + back
+                r[m] = w[m] * r[m] + back
+                r1[m] = w[m] * r1[m] + r[m]
         for m in range(GROUP):
-            e_ref[ln, at[m], :] = w[m] * h[m]
-            e1_ref[ln, at[m], :] = w[m] * (h1[m] + h[m])
-            g_ref[ln, at[m], :] = r[m]
-            g1_ref[ln, at[m], :] = r1[m]
-            p_ref[ln, at[m], :] = p[m]
-            t_ref[ln, at[m], :] = t[m]
-        return 0
-
-    lax.fori_loop(0, groups * tiles, one, 0)
+            e_ref[i, at[m], :] = w[m] * h[m]
+            e1_ref[i, at[m], :] = w[m] * h1[m]
+            g_ref[i, at[m], :] = r[m]
+            g1_ref[i, at[m], :] = r1[m] - r[m]
+            p_ref[i, at[m], :] = p[m]
+            t_ref[i, at[m], :] = t[m] - p[m]
+
+    for i, ln in enumerate(columns):
+        for copy in copies[1 + 4 * i : 5 + 4 * i]:
+            copy.wait()
+        skip = jnp.zeros((8, LANES), F32)
+        for seg in range(SEGS):
+            for part in range(steps // 16):
+                at = pl.ds(seg * steps + part * 16, 16)
+                gated = product(k_ref[at, ln], v_ref[at, ln])
+                grad = product(u_ref[at, ln], q_ref[at, ln])
+                both = gated * grad
+                skip = skip + both[:8] + both[8:]
+                to = pl.ds(part * 16 * SEGS + seg, 16, stride=SEGS)
+                gated_ref[i, to, :] = gated
+                grad_ref[i, to, :] = grad
+        skip = jnp.sum(skip, axis=0, keepdims=True)
+        z_ref[6 * modes :, ln] = jnp.broadcast_to(skip, (8, LANES)).astype(BF16)
+        for base in range(modes // GROUP):
+            one(base, i)
 
     for i in range(tiles):
         ln = slice(i * LANES, (i + 1) * LANES)
@@ -124,7 +123,6 @@
         parts = (s, 0.25 * s - dec * s1, r, 0.25 * r - dec * r1, p, 0.5 * p - dec * t)
         for n, part in enumerate(parts):
             z_ref[n * modes : (n + 1) * modes, ln] = part.astype(BF16)
-    z_ref[6 * modes : 6 * modes + 16, :] = jnp.broadcast_to(skip, (16, width)).astype(BF16)
 
 
 def conv_kernel(
@@ -155,6 +153,7 @@
             out0_ref[i, at, :] = a * w * post_ref[i, at, :]
 
     def one(i, _):
+        direct = jnp.broadcast_to(skip_ref[:, lanes_of(i)], (SEGS, LANES))
         for base in range(0, modes, GROUP):
             at = [pl.ds((base + m) * SEGS, SEGS) for m in range(GROUP)]
             w = [w_ref[i, x, :] for x in at]
@@ -165,8 +164,8 @@
                 at_f = pl.ds(j * SEGS, SEGS)
                 at_b = pl.ds((steps - 1 - j) * SEGS, SEGS)
                 x, y = gated_ref[i, at_f, :], grad_ref[i, at_b, :]
-                f = fwd_ref[i, at_f, :] if base else zero
-                b = bwd_ref[i, at_b, :] if base else zero
+                f = fwd_ref[i, at_f, :] if base else direct * x
+                b = bwd_ref[i, at_b, :] if base else direct * y
                 for m in range(GROUP):
                     h[m] = w[m] * h[m] + x
                     r[m] = w[m] * r[m] + y
@@ -197,7 +196,7 @@
         return pick
 
     e, f, g, h, p, d = (gather(i) for i in range(6))
-    k = gather(6, 16)
+    k = gather(6, 8)
     one = dec_t * span
     w = [jnp.exp(one * (-float(j))) for j in range(4)]
     e_t, f_t, g_t, h_t, p_t, d_t, k_t = e[0], f[0], g[0], h[0], p[0], d[0], k[0]
@@ -221,7 +220,7 @@
     return (e_t, f_t, g_t, h_t, p_t, d_t, k_t), s, r
 
 
-def combine_kernel(level, count, z0, z1, z2, z3, dec_t_ref, s_ref, r_ref, z_ref, s_out, r_out):
+def combine_kernel(level, count, z0, z1, z3, z2, dec_t_ref, s_ref, r_ref, z_ref, s_out, r_out):
     modes = dec_t_ref.shape[0]
     block, s, r = combine(level, count, (z0, z1, z2, z3), dec_t_ref[...], s_ref[...], r_ref[...])
     for i, part in enumerate(block):
@@ -232,23 +231,24 @@
 
 def finish_kernel(
     level, count,
-    z0, z1, z2, z3, dec_t_ref, s_ref, r_ref, res_t_ref, skip_ref,
-    q_ref, k_ref, v_ref, u_ref, fwd_ref, bwd_ref, in_ref, out_ref, in0_ref, out0_ref,
-    dq_ref, dk_ref, dv_ref, dres_ref, ddec_ref, dskip_ref,
-    f_ref, b_ref, sv_ref, rv_ref, w_ref,
+    z0, z1, z3, z2, dec_t_ref, s_ref, r_ref, res_t_ref,
+    k_ref, v_ref, u_ref, fwd_ref, bwd_ref, in_ref, out_ref, in0_ref, out0_ref,
+    dq_hbm, dk_hbm, dv_hbm, dres_hbm, ddec_hbm, dskip_hbm,
+    dq_ref, dk_ref, dv_ref, dres_ref, ddec_ref, dskip_ref, f_ref, b_ref, sv_ref, rv_ref, w_ref, sems,
 ):
-    rows, width = q_ref.shape
+    rows, width = k_ref.shape
     modes = dec_t_ref.shape[0]
     steps = rows // SEGS
     dec_t = dec_t_ref[...]
     block, s, r = combine(level, count, (z0, z1, z2, z3), dec_t, s_ref[...], r_ref[...])
+    sv_ref[...] = s
+    rv_ref[...] = r
+    w_ref[...] = jnp.exp(-dec_t)
     roots = jnp.sqrt(dec_t)
     dres_ref[...] = roots * block[4]
     ddec_ref[...] = res_t_ref[...] / roots * block[5]
     dskip_ref[...] = block[6][:1]
-    sv_ref[...] = s
-    rv_ref[...] = r
-    w_ref[...] = jnp.exp(-dec_t)
+    copies = fetch(sems, (dres_ref, dres_hbm), (ddec_ref, ddec_hbm), (dskip_ref, dskip_hbm))
 
     def one(i, _):
         ln = lanes_of(i)
@@ -256,55 +256,64 @@
         def spread(ref, m):
             return jnp.broadcast_to(ref[pl.ds(m, 1), ln], (SEGS, LANES))
 
-        w = [spread(w_ref, m) for m in range(modes)]
-        at = [pl.ds(m * SEGS, SEGS) for m in range(modes)]
-        c = [in_ref[i, at[m], :] * spread(sv_ref, m) + in0_ref[i, at[m], :] for m in range(modes)]
-        for j in range(steps):
-            here = pl.ds(j * SEGS, SEGS)
-            f = fwd_ref[i, here, :]
-            for m in range(modes):
-                f = f + c[m]
-                c[m] = c[m] * w[m]
-            f_ref[i, here, :] = f
-        c = [out_ref[i, at[m], :] * spread(rv_ref, m) + out0_ref[i, at[m], :] for m in range(modes)]
-        for j in range(steps - 1, -1, -1):
-            here = pl.ds(j * SEGS, SEGS)
-            b = bwd_ref[i, here, :]
-            for m in range(modes):
-                b = b + c[m]
-                c[m] = c[m] * w[m]
-            b_ref[i, here, :] = b
+        for half in range(0, modes, HALF):
+            w = [spread(w_ref, half + m) for m in range(HALF)]
+            powers = [[x, x * x, x * x * x, (x * x) * (x * x)] for x in w]
+            at = [pl.ds((half + m) * SEGS, SEGS) for m in range(HALF)]
+            sides = (
+                (in_ref, in0_ref, sv_ref, fwd_ref, f_ref, range(steps)),
+                (out_ref, out0_ref, rv_ref, bwd_ref, b_ref, range(steps - 1, -1, -1)),
+            )
+            for scale, extra, state, local, total, order in sides:
+                c = [scale[i, at[m], :] * spread(state, half + m) + extra[i, at[m], :] for m in range(HALF)]
+                source = total if half else local
+                for first in range(0, steps, 4):
+                    here = [pl.ds(j * SEGS, SEGS) for j in order[first : first + 4]]
+                    y = [source[i, x, :] for x in here]
+                    for m in range(HALF):
+                        w1, w2, w3, w4 = powers[m]
+                        y[0] = y[0] + c[m]
+                        y[1] = y[1] + c[m] * w1
+                        y[2] = y[2] + c[m] * w2
+                        y[3] = y[3] + c[m] * w3
+                        if first < steps - 4:
+                            c[m] = c[m] * w4
+                    for x, value in zip(here, y):
+                        total[i, x, :] = value
         return 0
 
     lax.fori_loop(0, width // LANES, one, 0)
 
-    for i in range(width // LANES):
-        ln = slice(i * LANES, (i + 1) * LANES)
-        skip = skip_ref[:, ln]
-        for seg in range(SEGS):
-            for part in range(steps // 16):
-                at = slice(seg * steps + part * 16, seg * steps + part * 16 + 16)
-                frm = pl.ds(part * 16 * SEGS + seg, 16, stride=SEGS)
-                q, k, v, u = (ref[at, ln].astype(F32) for ref in (q_ref, k_ref, v_ref, u_ref))
-                gated = (k * v).astype(BF16).astype(F32)
-                grad = (u * q).astype(BF16).astype(F32)
-                conv = (f_ref[i, frm, :] + skip * gated).astype(BF16).astype(F32)
-                dq_ref[at, ln] = (u * conv).astype(BF16)
-                gg = (b_ref[i, frm, :] + skip * grad).astype(BF16).astype(F32)
-                dk_ref[at, ln] = (gg * v).astype(BF16)
-                dv_ref[at, ln] = (gg * k).astype(BF16)
+    done = 0
+    for seg in range(SEGS):
+        for part in range(steps // 16):
+            to = pl.ds(seg * steps + part * 16, 16)
+            frm = pl.ds(part * 16 * SEGS + seg, 16, stride=SEGS)
+            for i in range(width // LANES):
+                ln = pl.ds(i * LANES, LANES)
+                conv = f_ref[i, frm, :].astype(BF16).astype(F32)
+                gg = b_ref[i, frm, :].astype(BF16).astype(F32)
+                dq_ref[to, ln] = (u_ref[to, ln].astype(F32) * conv).astype(BF16)
+                dk_ref[to, ln] = (gg * v_ref[to, ln].astype(F32)).astype(BF16)
+                dv_ref[to, ln] = (gg * k_ref[to, ln].astype(F32)).astype(BF16)
+        if seg % 2:
+            block_rows = pl.ds((seg - 1) * steps, 2 * steps)
+            pairs = ((dq_ref, dq_hbm), (dk_ref, dk_hbm), (dv_ref, dv_hbm))
+            copies += fetch(sems, *[(a.at[block_rows], b.at[block_rows]) for a, b in pairs], first=3 + 3 * (seg // 2))
+    for copy in copies:
+        copy.wait()
 
 
 def kept(array, space=VMEM):
     return pltpu.with_memory_space_constraint(array, space)
 
 
-def call(kernel, outs, args, scratch=(), flops=0, name=None, hbm=0):
+def call(kernel, outs, args, scratch=(), flops=0, name=None, hbm=0, out_space=VMEM):
     return pl.pallas_call(
         kernel,
         out_shape=outs,
         in_specs=[pl.BlockSpec(memory_space=pltpu.HBM)] * hbm + [pl.BlockSpec(memory_space=VMEM)] * (len(args) - hbm),
-        out_specs=[pl.BlockSpec(memory_space=VMEM)] * len(outs),
+        out_specs=[pl.BlockSpec(memory_space=out_space)] * len(outs),
         scratch_shapes=list(scratch),
         cost_estimate=pl.CostEstimate(flops=flops, bytes_accessed=1 << 19, transcendentals=0),
         compiler_params=pltpu.CompilerParams(vmem_limit_bytes=24 << 20),
@@ -314,9 +323,9 @@
 
 def exchange(array, level, size):
     got = {}
-    for k in (2, 3, 1):
+    for k in (1, 3, 2):
         got[k] = lax.ppermute(array, "seq", [(i, i ^ (k * 4**level)) for i in range(size)])
-    return [array, got[1], got[2], got[3]]
+    return [array, got[1], got[3], got[2]]
 
 
 def shards(queries, keys, values, upstream, residues, decay, skip):
@@ -325,7 +334,7 @@
     size = lax.axis_size("seq")
     levels = 3
     seg_rows = modes * SEGS
-    z_rows = 6 * modes + 16
+    z_rows = 6 * modes + 8
     tiles = width // LANES
     big = VMEM((tiles, rows, LANES), F32)
     state = VMEM((modes, width), F32)
@@ -336,7 +345,7 @@
         summary_kernel,
         [block, big, big, spread, spread, state] + [local] * 4,
         [decay.T, keys, values, upstream, queries],
-        [spread] * 7 + [pltpu.SemaphoreType.DMA((5,))],
+        [spread] * 7 + [pltpu.SemaphoreType.DMA((1 + 4 * tiles,))],
         flops=12 * rows * width * modes,
         name="summary",
         hbm=5,
@@ -365,9 +374,10 @@
     dq, dk, dv, dres, ddec, dskip = call(
         functools.partial(finish_kernel, levels - 1, rows),
         outs,
-        [*exchange(z, levels - 1, size), dec_t, s, r, res_t, skip, queries, keys, values, upstream, fwd, bwd, in_w, out_w, in_0, out_0],
-        [big, big, state, state, state],
+        [*exchange(z, levels - 1, size), dec_t, s, r, res_t, keys, values, upstream, fwd, bwd, in_w, out_w, in_0, out_0],
+        [local] * 3 + [state] * 2 + [VMEM((1, width), F32), big, big, state, state, state, pltpu.SemaphoreType.DMA((3 + 3 * SEGS // 2,))],
         name="finish",
+        out_space=pltpu.HBM,
     )
     return dq, dk, dv, dres.T, ddec.T, dskip.reshape(width)
 

time: 37.1 us -> 36 us (0.970)
  waiting for transfers between devices: 12.6 us -> 11.9 us
  Pallas kernels: 7.15 us -> 6.76 us
    ppermute x9, waiting for transfers between devices: 12.6 us -> 11.9 us  [exchange(): lax.ppermute(array, 'seq', [(i, i ^ k * 4 ** level) for i in range(size)])]
    pallas_call x5, Pallas kernels: 7.15 us -> 6.76 us  [call(): pl.pallas_call(kernel, out_shape=outs, in_specs=[pl.BlockSpec(memory_spac...]
where the time goes in v3:
time: 36 us; the launch traced here: 35.8 us
  starting transfers between devices  16.4 us (46%)
  waiting for transfers between devices  11.9 us (33%)
  Pallas kernels  6.76 us (19%)
  between operations  0.67 us (2%)
    ppermute x9, starting transfers between devices, exchange(): lax.ppermute(array, 'seq', [(i, i ^ k * 4 ** level) for i in range(size)])  16.4 us
    ppermute x9, waiting for transfers between devices, exchange(): lax.ppermute(array, 'seq', [(i, i ^ k * 4 ** level) for i in range(size)])  11.9 us
    pallas_call x5, Pallas kernels, call(): pl.pallas_call(kernel, out_shape=outs, in_specs=[pl.BlockSpec(memory_spac...  6.76 us
  transfers between devices with their start and end apart: 9, of which 5 were waited for; matrix products, arithmetic and copies ran while one was open for 0% of the time, Pallas kernels for 5%

profile of v3, /device:TPU:32, one launch (start us, length us, event | category | flops | bytes accessed | tf_op | source)
XLA Modules:
  0.0 35.8 jit_solution(15652589194007552301)
XLA Ops:
  0.6 3.0 %summary.1 = (bf16[104,256]{1,0:T(8,128)(2,1)S(1)}, f32[2,256,128]{2,1,0:T(8,128)S(1)}, f32[2,256,128]{2,1,0:T(8,128)S(1)}, f32[2,128,128]{2,1,0:T(8,128)S(1)}, ...) custom-call(f32[16,256]{1,0:T(8,128)} %bitcast.6, ...), custom_call_target="tpu_custom_call" | custom-call | flops 12582912 | bytes 524288 | tf_op jit(solution)/shard_map/summary/pallas_call | solution.py:312
  3.6 3.1 %collective-permute-start.2 = (bf16[104,256]{1,0:T(8,128)(2,1)S(1)}, bf16[104,256]{1,0:T(8,128)(2,1)S(1)}, u32[]{:S(2)}, u32[]{:S(2)}) collective-permute-start(bf16[104,256]{1,0:T(8,128)(2,1)S(1)} %get-tuple-element.34.z0), channel_id=1, source_target_pairs={{0,8},{4,12},{8,0},{12,4},{16,24},{20,28},{24,16},{28,20},{32,40},... | collective-permute-start | bytes 159752 | tf_op jit(solution)/shard_map/ppermute | solution.py:327
  6.7 1.1 %collective-permute-start.1 = (bf16[104,256]{1,0:T(8,128)(2,1)S(1)}, bf16[104,256]{1,0:T(8,128)(2,1)S(1)}, u32[]{:S(2)}, u32[]{:S(2)}) collective-permute-start(bf16[104,256]{1,0:T(8,128)(2,1)S(1)} %get-tuple-element.34.z0), channel_id=1, source_target_pairs={{0,12},{4,8},{8,4},{12,0},{16,28},{20,24},{24,20},{28,16},{32,44},... | collective-permute-start | bytes 159752 | tf_op jit(solution)/shard_map/ppermute | solution.py:327
  7.9 0.0 collective-permute-start
  7.9 1.5 %collective-permute-done.2.z2 = bf16[104,256]{1,0:T(8,128)(2,1)S(1)} collective-permute-done((bf16[104,256]{1,0:T(8,128)(2,1)S(1)}, bf16[104,256]{1,0:T(8,128)(2,1)S(1)}, u32[]{:S(2)}, u32[]{:S(2)}) %collective-permute-start.2) | collective-permute-done | bytes 53280 | tf_op jit(solution)/shard_map/ppermute | solution.py:327
  9.4 2.7 %collective-permute-done.1.z3 = bf16[104,256]{1,0:T(8,128)(2,1)S(1)} collective-permute-done((bf16[104,256]{1,0:T(8,128)(2,1)S(1)}, bf16[104,256]{1,0:T(8,128)(2,1)S(1)}, u32[]{:S(2)}, u32[]{:S(2)}) %collective-permute-start.1) | collective-permute-done | bytes 53280 | tf_op jit(solution)/shard_map/ppermute | solution.py:327
  12.1 0.0 collective-permute-done.z1
  12.1 0.1 combine0.1
  12.2 3.3 %collective-permute-start.5 = (bf16[104,256]{1,0:T(8,128)(2,1)S(1)}, bf16[104,256]{1,0:T(8,128)(2,1)S(1)}, u32[]{:S(2)}, u32[]{:S(2)}) collective-permute-start(bf16[104,256]{1,0:T(8,128)(2,1)S(1)} %get-tuple-element.36.z0), channel_id=1, source_target_pairs={{0,32},{4,36},{8,40},{12,44},{16,48},{20,52},{24,56},{28,60},{32,0... | collective-permute-start | bytes 159752 | tf_op jit(solution)/shard_map/ppermute | solution.py:327
  15.5 1.1 %collective-permute-start.4 = (bf16[104,256]{1,0:T(8,128)(2,1)S(1)}, bf16[104,256]{1,0:T(8,128)(2,1)S(1)}, u32[]{:S(2)}, u32[]{:S(2)}) collective-permute-start(bf16[104,256]{1,0:T(8,128)(2,1)S(1)} %get-tuple-element.36.z0), channel_id=1, source_target_pairs={{0,48},{4,52},{8,56},{12,60},{16,32},{20,36},{24,40},{28,44},{32,1... | collective-permute-start | bytes 159752 | tf_op jit(solution)/shard_map/ppermute | solution.py:327
  16.6 0.0 collective-permute-start.3
  16.6 1.4 %collective-permute-done.5.z2 = bf16[104,256]{1,0:T(8,128)(2,1)S(1)} collective-permute-done((bf16[104,256]{1,0:T(8,128)(2,1)S(1)}, bf16[104,256]{1,0:T(8,128)(2,1)S(1)}, u32[]{:S(2)}, u32[]{:S(2)}) %collective-permute-start.5) | collective-permute-done | bytes 53280 | tf_op jit(solution)/shard_map/ppermute | solution.py:327
  18.0 2.8 %collective-permute-done.4.z3 = bf16[104,256]{1,0:T(8,128)(2,1)S(1)} collective-permute-done((bf16[104,256]{1,0:T(8,128)(2,1)S(1)}, bf16[104,256]{1,0:T(8,128)(2,1)S(1)}, u32[]{:S(2)}, u32[]{:S(2)}) %collective-permute-start.4) | collective-permute-done | bytes 53280 | tf_op jit(solution)/shard_map/ppermute | solution.py:327
  20.8 0.0 collective-permute-done.3.z1
  20.9 0.1 combine1.1
  21.0 6.4 %collective-permute-start.8 = (bf16[104,256]{1,0:T(8,128)(2,1)S(1)}, bf16[104,256]{1,0:T(8,128)(2,1)S(1)}, u32[]{:S(2)}, u32[]{:S(2)}) collective-permute-start(bf16[104,256]{1,0:T(8,128)(2,1)S(1)} %get-tuple-element.39.z0), channel_id=1, source_target_pairs={{0,128},{4,132},{8,136},{12,140},{16,144},{20,148},{24,152},{28,15... | collective-permute-start | bytes 159752 | tf_op jit(solution)/shard_map/ppermute | solution.py:327
  27.4 0.6 %collective-permute-start.7 = (bf16[104,256]{1,0:T(8,128)(2,1)S(1)}, bf16[104,256]{1,0:T(8,128)(2,1)S(1)}, u32[]{:S(2)}, u32[]{:S(2)}) collective-permute-start(bf16[104,256]{1,0:T(8,128)(2,1)S(1)} %get-tuple-element.39.z0), channel_id=1, source_target_pairs={{0,192},{4,196},{8,200},{12,204},{16,208},{20,212},{24,216},{28,22... | collective-permute-start | bytes 159752 | tf_op jit(solution)/shard_map/ppermute | solution.py:327
  27.9 0.9 %collective-permute-start.6 = (bf16[104,256]{1,0:T(8,128)(2,1)S(1)}, bf16[104,256]{1,0:T(8,128)(2,1)S(1)}, u32[]{:S(2)}, u32[]{:S(2)}) collective-permute-start(bf16[104,256]{1,0:T(8,128)(2,1)S(1)} %get-tuple-element.39.z0), channel_id=1, source_target_pairs={{0,64},{4,68},{8,72},{12,76},{16,80},{20,84},{24,88},{28,92},{32,9... | collective-permute-start | bytes 159752 | tf_op jit(solution)/shard_map/ppermute | solution.py:327
  28.8 1.9 %conv.1 = (f32[2,256,128]{2,1,0:T(8,128)S(1)}, f32[2,256,128]{2,1,0:T(8,128)S(1)}, f32[2,128,128]{2,1,0:T(8,128)S(1)}, f32[2,128,128]{2,1,0:T(8,128)S(1)}, f32[2...) custom-call(f32[16,256]{1,0:T(8,128)} %bitcast.7, ...), custom_call_target="tpu_custom_call" | custom-call | flops 8388608 | bytes 524288 | tf_op jit(solution)/shard_map/conv/pallas_call | solution.py:312
  30.8 0.0 collective-permute-done.8.z2
  30.8 3.4 %collective-permute-done.7.z3 = bf16[104,256]{1,0:T(8,128)(2,1)S(1)} collective-permute-done((bf16[104,256]{1,0:T(8,128)(2,1)S(1)}, bf16[104,256]{1,0:T(8,128)(2,1)S(1)}, u32[]{:S(2)}, u32[]{:S(2)}) %collective-permute-start.7) | collective-permute-done | bytes 53280 | tf_op jit(solution)/shard_map/ppermute | solution.py:327
  34.2 0.0 collective-permute-done.6.z1
  34.2 1.6 %finish.1 = (bf16[256,256]{1,0:T(8,128)(2,1)}, bf16[256,256]{1,0:T(8,128)(2,1)}, bf16[256,256]{1,0:T(8,128)(2,1)}, f32[16,256]{1,0:T(8,128)}, f32[16,256]{1,0:T(8,128)}, /*index=5*/f32[1,256]{1,0:T(1,128)}) custom-call(bf16[104,256]{1,0:T(8,128)(2,1)S(1)} %get-tuple-element.39.z0, bf16[104,256]{1,0:T(8,128)(2,1)S(1)} %collective-permute-done.6.z1, ...), custom_call_target="tpu_custom_call" | custom-call | bytes 524288 | tf_op jit(solution)/shard_map/finish/pallas_call | solution.py:312
  (1 shorter events, 0.0 us)
Async XLA Ops:
  3.6 5.7 %collective-permute-start.2 = (bf16[104,256]{1,0:T(8,128)(2,1)S(1)}, bf16[104,256]{1,0:T(8,128)(2,1)S(1)}, u32[]{:S(2)}, u32[]{:S(2)}) collective-permute-start(bf16[104,256]{1,0:T(8,128)(2,1)S(1)} %get-tuple-element.34.z0), channel_id=1, source_target_pairs={{0,8},{4,12},{8,0},{12,4},{16,24},{20,28},{24,16},{28,20},{32,40},... | collective-permute-start | bytes 159752 | tf_op jit(solution)/shard_map/ppermute | solution.py:327
  6.7 5.3 %collective-permute-start.1 = (bf16[104,256]{1,0:T(8,128)(2,1)S(1)}, bf16[104,256]{1,0:T(8,128)(2,1)S(1)}, u32[]{:S(2)}, u32[]{:S(2)}) collective-permute-start(bf16[104,256]{1,0:T(8,128)(2,1)S(1)} %get-tuple-element.34.z0), channel_id=1, source_target_pairs={{0,12},{4,8},{8,4},{12,0},{16,28},{20,24},{24,20},{28,16},{32,44},... | collective-permute-start | bytes 159752 | tf_op jit(solution)/shard_map/ppermute | solution.py:327
  7.9 4.2 %collective-permute-start = (bf16[104,256]{1,0:T(8,128)(2,1)S(1)}, bf16[104,256]{1,0:T(8,128)(2,1)S(1)}, u32[]{:S(2)}, u32[]{:S(2)}) collective-permute-start(bf16[104,256]{1,0:T(8,128)(2,1)S(1)} %get-tuple-element.34.z0), channel_id=1, source_target_pairs={{0,4},{4,0},{8,12},{12,8},{16,20},{20,16},{24,28},{28,24},{32,36},... | collective-permute-start | bytes 159752 | tf_op jit(solution)/shard_map/ppermute | solution.py:327
  12.2 5.8 %collective-permute-start.5 = (bf16[104,256]{1,0:T(8,128)(2,1)S(1)}, bf16[104,256]{1,0:T(8,128)(2,1)S(1)}, u32[]{:S(2)}, u32[]{:S(2)}) collective-permute-start(bf16[104,256]{1,0:T(8,128)(2,1)S(1)} %get-tuple-element.36.z0), channel_id=1, source_target_pairs={{0,32},{4,36},{8,40},{12,44},{16,48},{20,52},{24,56},{28,60},{32,0... | collective-permute-start | bytes 159752 | tf_op jit(solution)/shard_map/ppermute | solution.py:327
  15.5 5.3 %collective-permute-start.4 = (bf16[104,256]{1,0:T(8,128)(2,1)S(1)}, bf16[104,256]{1,0:T(8,128)(2,1)S(1)}, u32[]{:S(2)}, u32[]{:S(2)}) collective-permute-start(bf16[104,256]{1,0:T(8,128)(2,1)S(1)} %get-tuple-element.36.z0), channel_id=1, source_target_pairs={{0,48},{4,52},{8,56},{12,60},{16,32},{20,36},{24,40},{28,44},{32,1... | collective-permute-start | bytes 159752 | tf_op jit(solution)/shard_map/ppermute | solution.py:327
  16.6 4.3 %collective-permute-start.3 = (bf16[104,256]{1,0:T(8,128)(2,1)S(1)}, bf16[104,256]{1,0:T(8,128)(2,1)S(1)}, u32[]{:S(2)}, u32[]{:S(2)}) collective-permute-start(bf16[104,256]{1,0:T(8,128)(2,1)S(1)} %get-tuple-element.36.z0), channel_id=1, source_target_pairs={{0,16},{4,20},{8,24},{12,28},{16,0},{20,4},{24,8},{28,12},{32,48},... | collective-permute-start | bytes 159752 | tf_op jit(solution)/shard_map/ppermute | solution.py:327
  21.0 9.8 %collective-permute-start.8 = (bf16[104,256]{1,0:T(8,128)(2,1)S(1)}, bf16[104,256]{1,0:T(8,128)(2,1)S(1)}, u32[]{:S(2)}, u32[]{:S(2)}) collective-permute-start(bf16[104,256]{1,0:T(8,128)(2,1)S(1)} %get-tuple-element.39.z0), channel_id=1, source_target_pairs={{0,128},{4,132},{8,136},{12,140},{16,144},{20,148},{24,152},{28,15... | collective-permute-start | bytes 159752 | tf_op jit(solution)/shard_map/ppermute | solution.py:327
  27.4 6.8 %collective-permute-start.7 = (bf16[104,256]{1,0:T(8,128)(2,1)S(1)}, bf16[104,256]{1,0:T(8,128)(2,1)S(1)}, u32[]{:S(2)}, u32[]{:S(2)}) collective-permute-start(bf16[104,256]{1,0:T(8,128)(2,1)S(1)} %get-tuple-element.39.z0), channel_id=1, source_target_pairs={{0,192},{4,196},{8,200},{12,204},{16,208},{20,212},{24,216},{28,22... | collective-permute-start | bytes 159752 | tf_op jit(solution)/shard_map/ppermute | solution.py:327
  27.9 6.3 %collective-permute-start.6 = (bf16[104,256]{1,0:T(8,128)(2,1)S(1)}, bf16[104,256]{1,0:T(8,128)(2,1)S(1)}, u32[]{:S(2)}, u32[]{:S(2)}) collective-permute-start(bf16[104,256]{1,0:T(8,128)(2,1)S(1)} %get-tuple-element.39.z0), channel_id=1, source_target_pairs={{0,64},{4,68},{8,72},{12,76},{16,80},{20,84},{24,88},{28,92},{32,9... | collective-permute-start | bytes 159752 | tf_op jit(solution)/shard_map/ppermute | solution.py:327

commit v4 on v3

v4 whole, which is shorter than its diff:
```python
import functools

import jax
import jax.numpy as jnp
from jax import lax
from jax.experimental import pallas as pl
from jax.experimental.pallas import tpu as pltpu
from jax.sharding import PartitionSpec as P

F32 = jnp.float32
BF16 = jnp.bfloat16
VMEM = pltpu.VMEM
SEGS = 8
LANES = 128
GROUP = 4


def product(a, b):
    return (a.astype(F32) * b.astype(F32)).astype(BF16).astype(F32)


def lanes_of(i):
    return pl.ds(pl.multiple_of(i * LANES, LANES), LANES)


def rows_of(i, n):
    return pl.ds(pl.multiple_of(i * n, n), n)


def fetch(sems, *pairs, first=0):
    copies = [pltpu.make_async_copy(a, b, sems.at[first + i]) for i, (a, b) in enumerate(pairs)]
    for copy in copies:
        copy.start()
    return copies


def summary_kernel(
    dec_hbm, k_hbm, v_hbm, u_hbm, q_hbm,
    z_ref, gated_ref, grad_ref, pre_ref, post_ref, dec_t_ref, k_ref, v_ref, u_ref, q_ref,
    w_ref, e_ref, e1_ref, g_ref, g1_ref, p_ref, t_ref, sems,
):
    rows, width = q_ref.shape
    modes = dec_t_ref.shape[0]
    steps = rows // SEGS
    tiles = width // LANES
    columns = [pl.ds(i * LANES, LANES) for i in range(tiles)]
    pairs = [(dec_hbm, dec_t_ref)]
    for ln in columns:
        pairs += [(a.at[:, ln], b.at[:, ln]) for a, b in ((k_hbm, k_ref), (v_hbm, v_ref), (u_hbm, u_ref), (q_hbm, q_ref))]
    copies = fetch(sems, *pairs)
    copies[0].wait()
    dec_t = dec_t_ref[...]
    w_all = jnp.exp(-dec_t)
    for i in range(tiles):
        for m in range(modes):
            row = w_all[m : m + 1, i * LANES : (i + 1) * LANES]
            w_ref[i, pl.ds(m * SEGS, SEGS), :] = jnp.broadcast_to(row, (SEGS, LANES))

    def one(base, i):
        at = [pl.ds((base * GROUP + m) * SEGS, SEGS) for m in range(GROUP)]
        w = [w_ref[i, a, :] for a in at]
        zero = jnp.zeros((SEGS, LANES), F32)
        h, h1, p, t, r, r1 = ([zero] * GROUP for _ in range(6))
        for j in range(steps):
            x = gated_ref[i, pl.ds(j * SEGS, SEGS), :]
            y = grad_ref[i, pl.ds(j * SEGS, SEGS), :]
            back = grad_ref[i, pl.ds((steps - 1 - j) * SEGS, SEGS), :]
            for m in range(GROUP):
                h[m] = w[m] * h[m] + x
                h1[m] = w[m] * h1[m] + h[m]
                p[m] = p[m] + y * h[m]
                t[m] = t[m] + y * h1[m]
                r[m] = w[m] * r[m] + back
                r1[m] = w[m] * r1[m] + r[m]
        for m in range(GROUP):
            e_ref[i, at[m], :] = w[m] * h[m]
            e1_ref[i, at[m], :] = w[m] * h1[m]
            g_ref[i, at[m], :] = r[m]
            g1_ref[i, at[m], :] = r1[m] - r[m]
            p_ref[i, at[m], :] = p[m]
            t_ref[i, at[m], :] = t[m] - p[m]

    for i, ln in enumerate(columns):
        for copy in copies[1 + 4 * i : 5 + 4 * i]:
            copy.wait()
        skip = jnp.zeros((8, LANES), F32)
        for seg in range(SEGS):
            for part in range(steps // 16):
                at = pl.ds(seg * steps + part * 16, 16)
                gated = product(k_ref[at, ln], v_ref[at, ln])
                grad = product(u_ref[at, ln], q_ref[at, ln])
                both = gated * grad
                skip = skip + both[:8] + both[8:]
                to = pl.ds(part * 16 * SEGS + seg, 16, stride=SEGS)
                gated_ref[i, to, :] = gated
                grad_ref[i, to, :] = grad
        skip = jnp.sum(skip, axis=0, keepdims=True)
        z_ref[6 * modes :, ln] = jnp.broadcast_to(skip, (8, LANES)).astype(BF16)
        for base in range(modes // GROUP):
            one(base, i)

    for i in range(tiles):
        ln = slice(i * LANES, (i + 1) * LANES)
        dec = dec_t[:, ln]
        w_seg = jnp.exp(dec * (-float(steps)))
        zero = jnp.zeros((modes, LANES), F32)
        s, s1, p, t = zero, zero, zero, zero
        for seg in range(SEGS):
            at = pl.ds(seg, modes, stride=SEGS)
            g, g1 = g_ref[i, at, :], g1_ref[i, at, :]
            pre_ref[i, at, :] = s
            p = p + p_ref[i, at, :] + s * g
            t = t + t_ref[i, at, :] + s1 * g + s * g1
            s1 = w_seg * (s1 + float(steps) * s) + e1_ref[i, at, :]
            s = w_seg * s + e_ref[i, at, :]
        r, r1 = zero, zero
        for seg in range(SEGS - 1, -1, -1):
            at = pl.ds(seg, modes, stride=SEGS)
            post_ref[i, at, :] = r
            r1 = w_seg * (r1 + float(steps) * r) + g1_ref[i, at, :]
            r = w_seg * r + g_ref[i, at, :]
        parts = (s, 0.25 * s - dec * s1, r, 0.25 * r - dec * r1, p, 0.5 * p - dec * t)
        for n, part in enumerate(parts):
            z_ref[n * modes : (n + 1) * modes, ln] = part.astype(BF16)


def place(stride, radix):
    at = lax.axis_index("seq")
    return lax.rem(lax.div(at, stride), radix), lax.rem(at, stride)


def conv_kernel(
    stride, count,
    res_hbm, skip_hbm, gated_ref, grad_ref, dec_t_ref, pre_ref, post_ref, s_ref, r_ref, k_ref, v_ref, u_ref,
    fwd_ref, bwd_ref, scale_ref, roots_ref, ratio_ref, dq_ref, dk_ref, dv_ref,
    res_t_ref, skip_ref, w_ref, a_ref, h_ref, b_ref, sems,
):
    copies = fetch(sems, (res_hbm, res_t_ref), (skip_hbm, skip_ref))
    tiles, rows, _ = gated_ref.shape
    modes = dec_t_ref.shape[0]
    steps = rows // SEGS
    digit, offset = place(stride, 2)
    right = digit == 1
    chunks = jnp.where(right, offset, stride - 1 - offset).astype(F32)
    for copy in copies:
        copy.wait()
    dec_t = dec_t_ref[...]
    roots = jnp.sqrt(dec_t)
    scale = res_t_ref[...] * roots
    roots_ref[...] = roots
    ratio_ref[...] = res_t_ref[...] / roots
    far = scale * jnp.exp(dec_t * (-float(count) * chunks))
    s, r = s_ref[...], r_ref[...]
    seg_at = lax.broadcasted_iota(jnp.int32, (SEGS, LANES), 0).astype(F32) * float(steps)
    away = jnp.where(right, seg_at, float(rows - steps + 1) - seg_at)
    for i in range(tiles):
        ln = slice(i * LANES, (i + 1) * LANES)
        for m in range(modes):
            at = pl.ds(m * SEGS, SEGS)

            def spread(x):
                return jnp.broadcast_to(x[m : m + 1, ln], (SEGS, LANES))

            d = spread(dec_t)
            w_ref[i, at, :] = jnp.exp(-d)
            a_ref[i, at, :] = spread(scale)
            scale_ref[i, at, :] = spread(far) * jnp.exp(-d * away)
            h_ref[i, at, :] = pre_ref[i, at, :] + jnp.exp(-d * seg_at) * spread(s)
            b_ref[i, at, :] = post_ref[i, at, :] + jnp.exp(-d * (float(rows - steps) - seg_at)) * spread(r)

    def one(i, _):
        direct = jnp.broadcast_to(skip_ref[:, lanes_of(i)], (SEGS, LANES))
        for base in range(0, modes, GROUP):
            at = [pl.ds((base + m) * SEGS, SEGS) for m in range(GROUP)]
            w = [w_ref[i, x, :] for x in at]
            a = [a_ref[i, x, :] for x in at]
            h = [h_ref[i, x, :] for x in at]
            r = [b_ref[i, x, :] for x in at]
            for j in range(steps):
                at_f = pl.ds(j * SEGS, SEGS)
                at_b = pl.ds((steps - 1 - j) * SEGS, SEGS)
                x, y = gated_ref[i, at_f, :], grad_ref[i, at_b, :]
                f = fwd_ref[i, at_f, :] if base else direct * x
                b = bwd_ref[i, at_b, :] if base else direct * y
                for m in range(GROUP):
                    h[m] = (w[m] * h[m] if j else h[m]) + x
                    r[m] = w[m] * r[m] + y
                    f = f + a[m] * h[m]
                    b = b + a[m] * r[m]
                fwd_ref[i, at_f, :] = f
                bwd_ref[i, at_b, :] = b
        return 0

    lax.fori_loop(0, tiles, one, 0)
    for seg in range(SEGS):
        for part in range(steps // 16):
            to, frm = rows_in(seg, part, steps)
            for i in range(tiles):
                ln = pl.ds(i * LANES, LANES)
                query_rows(u_ref, fwd_ref, dq_ref, i, frm, to, ln)
                pair_rows(k_ref, v_ref, bwd_ref, dk_ref, dv_ref, i, frm, to, ln)


def rows_in(seg, part, steps):
    return pl.ds(seg * steps + part * 16, 16), pl.ds(part * 16 * SEGS + seg, 16, stride=SEGS)


def query_rows(u_ref, total_ref, dq_ref, i, frm, to, ln):
    conv = total_ref[i, frm, :].astype(BF16).astype(F32)
    dq_ref[to, ln] = (u_ref[to, ln].astype(F32) * conv).astype(BF16)


def pair_rows(k_ref, v_ref, total_ref, dk_ref, dv_ref, i, frm, to, ln):
    gg = total_ref[i, frm, :].astype(BF16).astype(F32)
    dk_ref[to, ln] = (gg * v_ref[to, ln].astype(F32)).astype(BF16)
    dv_ref[to, ln] = (gg * k_ref[to, ln].astype(F32)).astype(BF16)


def four_kernel(stride, count, z0, z1, z3, z2, *refs):
    combine_kernel(stride, 4, count, False, z0, z1, z2, z3, *refs)


def combine_kernel(stride, radix, count, last, *refs):
    parts = refs[:radix]
    dec_t_ref, s_ref, r_ref, z_ref, s_out, r_out = refs[radix : radix + 6]
    dec_t = dec_t_ref[...]
    modes = dec_t.shape[0]
    digit, offset = place(stride, radix)
    offset = offset.astype(F32)

    def gather(i, n=modes):
        have = [part[pl.ds(i * modes, n), :].astype(F32) for part in parts]
        pick = []
        for j in range(radix):
            k = digit ^ j
            first = jnp.where(k == 0, have[0], have[1])
            if radix == 4:
                first = jnp.where(k >= 2, jnp.where(k == 2, have[2], have[3]), first)
            pick.append(first)
        return pick

    e, f, g, h, p, d = (gather(i) for i in range(6))
    k = gather(6, 8)
    one = dec_t * float(count * stride)
    w = [jnp.exp(one * (-float(j))) for j in range(radix)]
    e_t, f_t, g_t, h_t, p_t, d_t, k_t = e[0], f[0], g[0], h[0], p[0], d[0], k[0]
    enter = jnp.zeros_like(dec_t)
    for j in range(1, radix):
        enter = jnp.where(digit == j, e_t, enter)
        p_t = p_t + p[j] + e_t * g[j]
        d_t = d_t + d[j] + f_t * g[j] + e_t * h[j]
        f_t = w[1] * (f_t - one * e_t) + f[j]
        e_t = w[1] * e_t + e[j]
        h_t = h_t + w[j] * (h[j] - one * float(j) * g[j])
        g_t = g_t + w[j] * g[j]
        k_t = k_t + k[j]
    leave = jnp.zeros_like(dec_t)
    tail = g[-1]
    for j in range(radix - 2, -1, -1):
        leave = jnp.where(digit == j, tail, leave)
        tail = g[j] + w[1] * tail
    s_out[...] = s_ref[...] + jnp.exp(dec_t * (-float(count) * offset)) * enter
    r_out[...] = r_ref[...] + jnp.exp(dec_t * (-float(count) * (float(stride - 1) - offset))) * leave
    block = [x.astype(BF16) for x in (e_t, f_t, g_t, h_t, p_t, d_t, k_t)]
    for i, part in enumerate(block):
        z_ref[pl.ds(i * modes, part.shape[0]), :] = part
    if last:
        side = place(stride * radix, 2)[0] == 1
        send = refs[radix + 6]
        send[pl.ds(0, modes), :] = jnp.where(side, block[2].astype(F32), block[0].astype(F32)).astype(BF16)
        send[pl.ds(modes, modes), :] = jnp.where(side, block[3].astype(F32), block[1].astype(F32)).astype(BF16)
        for i, part in enumerate(block[4:]):
            send[pl.ds((2 + i) * modes, part.shape[0]), :] = part


def finish_kernel(
    stride,
    own_ref, got_ref, dec_t_ref, roots_ref, ratio_ref, scale_ref, fwd_ref, bwd_ref,
    k_ref, v_ref, u_ref, dq_old, dk_old, dv_old,
    dq_hbm, dk_hbm, dv_hbm, dres_hbm, ddec_hbm, dskip_hbm,
    dq_ref, dk_ref, dv_ref, dres_ref, ddec_ref, dskip_ref, total_ref, w_ref, c_ref, sems,
):
    rows, width = k_ref.shape
    modes = dec_t_ref.shape[0]
    steps = rows // SEGS
    tiles = width // LANES
    right = place(stride, 2)[0] == 1
    outs = ((dq_old, dq_ref, dq_hbm), (dk_old, dk_ref, dk_hbm), (dv_old, dv_ref, dv_hbm))

    @pl.when(right)
    def _():
        fetch(sems, *[(old, hbm) for old, _, hbm in outs[1:]])

    @pl.when(jnp.logical_not(right))
    def _():
        fetch(sems, *[(old, hbm) for old, _, hbm in outs[:1]])

    def half(ref, i, n=modes):
        return ref[pl.ds(i * modes, n), :].astype(F32)

    got = half(got_ref, 0), half(got_ref, 1)
    e_l, g_r = jnp.where(right, got[0], half(own_ref, 0)), jnp.where(right, half(own_ref, 2), got[0])
    f_l, h_r = jnp.where(right, got[1], half(own_ref, 1)), jnp.where(right, half(own_ref, 3), got[1])
    proj = half(own_ref, 4) + half(got_ref, 2) + e_l * g_r
    diff = half(own_ref, 5) + half(got_ref, 3) + (f_l * g_r + e_l * h_r)
    dres_ref[...] = roots_ref[...] * proj
    ddec_ref[...] = ratio_ref[...] * diff
    dskip_ref[...] = (half(own_ref, 6, 8) + half(got_ref, 4, 8))[:1]
    copies = fetch(sems, (dres_ref, dres_hbm), (ddec_ref, ddec_hbm), (dskip_ref, dskip_hbm), first=2)
    w_ref[...] = jnp.exp(-dec_t_ref[...])
    c_ref[...] = got[0]

    def add(local_ref, order):
        def one(i, _):
            ln = lanes_of(i)

            def spread(ref, m):
                return jnp.broadcast_to(ref[pl.ds(m, 1), ln], (SEGS, LANES))

            w = [spread(w_ref, m) for m in range(modes)]
            c = [scale_ref[i, pl.ds(m * SEGS, SEGS), :] * spread(c_ref, m) for m in range(modes)]
            for n, j in enumerate(order):
                here = pl.ds(j * SEGS, SEGS)
                y = local_ref[i, here, :]
                for m in range(modes):
                    y = y + c[m]
                    if n < steps - 1:
                        c[m] = c[m] * w[m]
                total_ref[i, here, :] = y
            return 0

        lax.fori_loop(0, tiles, one, 0)

    def rest(work, pairs):
        for seg in range(SEGS):
            for part in range(steps // 16):
                to, frm = rows_in(seg, part, steps)
                for i in range(tiles):
                    work(i, frm, to, pl.ds(i * LANES, LANES))
        done = fetch(sems, *pairs, first=5)
        for copy in done:
            copy.wait()

    @pl.when(right)
    def _():
        add(fwd_ref, range(steps))
        rest(
            lambda i, frm, to, ln: query_rows(u_ref, total_ref, dq_ref, i, frm, to, ln),
            [(new, hbm) for _, new, hbm in outs[:1]],
        )
        for i, (old, _, hbm) in enumerate(outs[1:]):
            pltpu.make_async_copy(old, hbm, sems.at[i]).wait()

    @pl.when(jnp.logical_not(right))
    def _():
        add(bwd_ref, range(steps - 1, -1, -1))
        rest(
            lambda i, frm, to, ln: pair_rows(k_ref, v_ref, total_ref, dk_ref, dv_ref, i, frm, to, ln),
            [(new, hbm) for _, new, hbm in outs[1:]],
        )
        pltpu.make_async_copy(dq_old, dq_hbm, sems.at[0]).wait()

    for copy in copies:
        copy.wait()


def kept(array, space=VMEM):
    return pltpu.with_memory_space_constraint(array, space)


def call(kernel, outs, args, scratch=(), flops=0, name=None, hbm=0, out_space=VMEM):
    return pl.pallas_call(
        kernel,
        out_shape=outs,
        in_specs=[pl.BlockSpec(memory_space=pltpu.HBM)] * hbm + [pl.BlockSpec(memory_space=VMEM)] * (len(args) - hbm),
        out_specs=[pl.BlockSpec(memory_space=out_space)] * len(outs),
        scratch_shapes=list(scratch),
        cost_estimate=pl.CostEstimate(flops=flops, bytes_accessed=1 << 19, transcendentals=0),
        compiler_params=pltpu.CompilerParams(vmem_limit_bytes=24 << 20),
        name=name,
    )(*[kept(a, pltpu.HBM) for a in args[:hbm]], *[kept(a) for a in args[hbm:]])


def exchange(array, mask, size):
    return lax.ppermute(array, "seq", [(i, i ^ mask) for i in range(size)])


def shards(queries, keys, values, upstream, residues, decay, skip):
    rows, width = queries.shape
    modes = residues.shape[1]
    size = lax.axis_size("seq")
    seg_rows = modes * SEGS
    z_rows = 6 * modes + 8
    tiles = width // LANES
    big = VMEM((tiles, rows, LANES), F32)
    state = VMEM((modes, width), F32)
    spread = VMEM((tiles, seg_rows, LANES), F32)
    block = VMEM((z_rows, width), BF16)
    local = VMEM((rows, width), BF16)
    z, gated, grad, pre, post, dec_t, keys, values, upstream, queries = call(
        summary_kernel,
        [block, big, big, spread, spread, state] + [local] * 4,
        [decay.T, keys, values, upstream, queries],
        [spread] * 7 + [pltpu.SemaphoreType.DMA((1 + 4 * tiles,))],
        flops=12 * rows * width * modes,
        name="summary",
        hbm=5,
    )
    s = r = jnp.zeros((modes, width), F32)
    for stride in (1, 4):
        parts = [z] + [exchange(z, k * stride, size) for k in (1, 3, 2)]
        z, s, r = call(
            functools.partial(four_kernel, stride, rows),
            [block, state, state],
            [*parts, dec_t, s, r],
            name=f"combine{stride}",
        )
    z, s, r, send = call(
        functools.partial(combine_kernel, 16, 2, rows, True),
        [block, state, state, VMEM((4 * modes + 8, width), BF16)],
        [z, exchange(z, 16, size), dec_t, s, r],
        name="combine16",
    )
    got = exchange(send, 48, size)
    fwd, bwd, scale, roots, ratio, dq, dk, dv = call(
        functools.partial(conv_kernel, 32, rows),
        [big, big, spread, state, state] + [local] * 3,
        [residues.T, skip.reshape(1, width), gated, grad, dec_t, pre, post, s, r, keys, values, upstream],
        [state, VMEM((1, width), F32)] + [spread] * 4 + [pltpu.SemaphoreType.DMA((2,))],
        flops=8 * rows * width * modes,
        name="conv",
        hbm=2,
    )
    outs = [jax.ShapeDtypeStruct((rows, width), BF16)] * 3
    outs += [jax.ShapeDtypeStruct((modes, width), F32)] * 2
    outs += [jax.ShapeDtypeStruct((1, width), F32)]
    dq, dk, dv, dres, ddec, dskip = call(
        functools.partial(finish_kernel, 32),
        outs,
        [z, got, dec_t, roots, ratio, scale, fwd, bwd, keys, values, upstream, dq, dk, dv],
        [local] * 3 + [state] * 2 + [VMEM((1, width), F32), big, state, state, pltpu.SemaphoreType.DMA((7,))],
        name="finish",
        out_space=pltpu.HBM,
    )
    return dq, dk, dv, dres.T, ddec.T, dskip.reshape(width)


def solution(mesh):
    tokens = P("seq", "chan")
    return jax.shard_map(
        shards,
        mesh=mesh,
        in_specs=(tokens, tokens, tokens, tokens, P("chan", None), P("chan", None), P("chan")),
        out_specs=(tokens, tokens, tokens, P("chan", None), P("chan", None), P("chan")),
        check_vma=False,
    )
```

time: 36 us -> 36 us (level)
  starting transfers between devices: 16.4 us -> 17.7 us
  waiting for transfers between devices: 11.9 us -> 10.8 us
    ppermute x9 -> x8, starting transfers between devices: 16.4 us -> 17.7 us  [exchange(): return lax.ppermute(array, 'seq', [(i, i ^ mask) for i in range(size)])]
    ppermute x9 -> x8, waiting for transfers between devices: 11.9 us -> 10.8 us  [exchange(): return lax.ppermute(array, 'seq', [(i, i ^ mask) for i in range(size)])]
    pallas_call x5 -> x6, Pallas kernels: 6.76 us -> 6.56 us  [call(): pl.pallas_call(kernel, out_shape=outs, in_specs=[pl.BlockSpec(memory_spac...]
  transfers between devices with their start and end apart: 9 -> 8, of which waited for: 5 -> 6; matrix products, arithmetic and copies ran while one was open for 0% -> 0% of each run, Pallas kernels for 5% -> 6%
where the time goes in v4:
time: 36 us; the launch traced here: 35.7 us
  starting transfers between devices  17.7 us (49%)
  waiting for transfers between devices  10.8 us (30%)
  Pallas kernels  6.56 us (18%)
  between operations  0.67 us (2%)
    ppermute x8, starting transfers between devices, exchange(): return lax.ppermute(array, 'seq', [(i, i ^ mask) for i in range(size)])  17.7 us
    ppermute x8, waiting for transfers between devices, exchange(): return lax.ppermute(array, 'seq', [(i, i ^ mask) for i in range(size)])  10.8 us
    pallas_call x6, Pallas kernels, call(): pl.pallas_call(kernel, out_shape=outs, in_specs=[pl.BlockSpec(memory_spac...  6.56 us
  transfers between devices with their start and end apart: 8, of which 6 were waited for; matrix products, arithmetic and copies ran while one was open for 0% of the time, Pallas kernels for 6%

profile of v4, /device:TPU:32, one launch (start us, length us, event | category | flops | bytes accessed | tf_op | source)
XLA Modules:
  0.0 35.7 jit_solution(8748526644618308115)
XLA Ops:
  0.6 3.0 %summary.1 = (bf16[104,256]{1,0:T(8,128)(2,1)S(1)}, f32[2,256,128]{2,1,0:T(8,128)S(1)}, f32[2,256,128]{2,1,0:T(8,128)S(1)}, f32[2,128,128]{2,1,0:T(8,128)S(1)}, ...) custom-call(f32[16,256]{1,0:T(8,128)} %bitcast.7, ...), custom_call_target="tpu_custom_call" | custom-call | flops 12582912 | bytes 524288 | tf_op jit(solution)/shard_map/summary/pallas_call | solution.py:372
  3.6 3.1 %collective-permute-start.2 = (bf16[104,256]{1,0:T(8,128)(2,1)S(1)}, bf16[104,256]{1,0:T(8,128)(2,1)S(1)}, u32[]{:S(2)}, u32[]{:S(2)}) collective-permute-start(bf16[104,256]{1,0:T(8,128)(2,1)S(1)} %get-tuple-element.39.z0), channel_id=1, source_target_pairs={{0,8},{4,12},{8,0},{12,4},{16,24},{20,28},{24,16},{28,20},{32,40},... | collective-permute-start | bytes 159752 | tf_op jit(solution)/shard_map/ppermute | solution.py:385
  6.7 1.1 %collective-permute-start.1 = (bf16[104,256]{1,0:T(8,128)(2,1)S(1)}, bf16[104,256]{1,0:T(8,128)(2,1)S(1)}, u32[]{:S(2)}, u32[]{:S(2)}) collective-permute-start(bf16[104,256]{1,0:T(8,128)(2,1)S(1)} %get-tuple-element.39.z0), channel_id=1, source_target_pairs={{0,12},{4,8},{8,4},{12,0},{16,28},{20,24},{24,20},{28,16},{32,44},... | collective-permute-start | bytes 159752 | tf_op jit(solution)/shard_map/ppermute | solution.py:385
  7.9 0.0 collective-permute-start
  7.9 1.5 %collective-permute-done.2.z2 = bf16[104,256]{1,0:T(8,128)(2,1)S(1)} collective-permute-done((bf16[104,256]{1,0:T(8,128)(2,1)S(1)}, bf16[104,256]{1,0:T(8,128)(2,1)S(1)}, u32[]{:S(2)}, u32[]{:S(2)}) %collective-permute-start.2) | collective-permute-done | bytes 53280 | tf_op jit(solution)/shard_map/ppermute | solution.py:385
  9.4 2.7 %collective-permute-done.1.z3 = bf16[104,256]{1,0:T(8,128)(2,1)S(1)} collective-permute-done((bf16[104,256]{1,0:T(8,128)(2,1)S(1)}, bf16[104,256]{1,0:T(8,128)(2,1)S(1)}, u32[]{:S(2)}, u32[]{:S(2)}) %collective-permute-start.1) | collective-permute-done | bytes 53280 | tf_op jit(solution)/shard_map/ppermute | solution.py:385
  12.1 0.0 collective-permute-done.z1
  12.1 0.1 combine1.1
  12.2 3.3 %collective-permute-start.5 = (bf16[104,256]{1,0:T(8,128)(2,1)S(1)}, bf16[104,256]{1,0:T(8,128)(2,1)S(1)}, u32[]{:S(2)}, u32[]{:S(2)}) collective-permute-start(bf16[104,256]{1,0:T(8,128)(2,1)S(1)} %get-tuple-element.41.z0), channel_id=1, source_target_pairs={{0,32},{4,36},{8,40},{12,44},{16,48},{20,52},{24,56},{28,60},{32,0... | collective-permute-start | bytes 159752 | tf_op jit(solution)/shard_map/ppermute | solution.py:385
  15.5 1.1 %collective-permute-start.4 = (bf16[104,256]{1,0:T(8,128)(2,1)S(1)}, bf16[104,256]{1,0:T(8,128)(2,1)S(1)}, u32[]{:S(2)}, u32[]{:S(2)}) collective-permute-start(bf16[104,256]{1,0:T(8,128)(2,1)S(1)} %get-tuple-element.41.z0), channel_id=1, source_target_pairs={{0,48},{4,52},{8,56},{12,60},{16,32},{20,36},{24,40},{28,44},{32,1... | collective-permute-start | bytes 159752 | tf_op jit(solution)/shard_map/ppermute | solution.py:385
  16.6 0.0 collective-permute-start.3
  16.6 1.4 %collective-permute-done.5.z2 = bf16[104,256]{1,0:T(8,128)(2,1)S(1)} collective-permute-done((bf16[104,256]{1,0:T(8,128)(2,1)S(1)}, bf16[104,256]{1,0:T(8,128)(2,1)S(1)}, u32[]{:S(2)}, u32[]{:S(2)}) %collective-permute-start.5) | collective-permute-done | bytes 53280 | tf_op jit(solution)/shard_map/ppermute | solution.py:385
  18.0 2.8 %collective-permute-done.4.z3 = bf16[104,256]{1,0:T(8,128)(2,1)S(1)} collective-permute-done((bf16[104,256]{1,0:T(8,128)(2,1)S(1)}, bf16[104,256]{1,0:T(8,128)(2,1)S(1)}, u32[]{:S(2)}, u32[]{:S(2)}) %collective-permute-start.4) | collective-permute-done | bytes 53280 | tf_op jit(solution)/shard_map/ppermute | solution.py:385
  20.8 0.0 collective-permute-done.3.z1
  20.8 0.1 combine4.1
  21.0 3.4 %collective-permute-start.6 = (bf16[104,256]{1,0:T(8,128)(2,1)S(1)}, bf16[104,256]{1,0:T(8,128)(2,1)S(1)}, u32[]{:S(2)}, u32[]{:S(2)}) collective-permute-start(bf16[104,256]{1,0:T(8,128)(2,1)S(1)} %get-tuple-element.44.refs_0_), channel_id=1, source_target_pairs={{0,64},{4,68},{8,72},{12,76},{16,80},{20,84},{24,88},{28,92},{32,9... | collective-permute-start | bytes 159752 | tf_op jit(solution)/shard_map/ppermute | solution.py:385
  24.3 2.1 %collective-permute-done.6.refs_1_ = bf16[104,256]{1,0:T(8,128)(2,1)S(1)} collective-permute-done((bf16[104,256]{1,0:T(8,128)(2,1)S(1)}, bf16[104,256]{1,0:T(8,128)(2,1)S(1)}, u32[]{:S(2)}, u32[]{:S(2)}) %collective-permute-start.6) | collective-permute-done | bytes 53280 | tf_op jit(solution)/shard_map/ppermute | solution.py:385
  26.4 0.1 combine16.1
  26.5 5.7 %collective-permute-start.7 = (bf16[72,256]{1,0:T(8,128)(2,1)S(1)}, bf16[72,256]{1,0:T(8,128)(2,1)S(1)}, u32[]{:S(2)}, u32[]{:S(2)}) collective-permute-start(bf16[72,256]{1,0:T(8,128)(2,1)S(1)} %get-tuple-element.48), channel_id=1, source_target_pairs={{0,192},{4,196},{8,200},{12,204},{16,208},{20,212},{24,216},{28,22... | collective-permute-start | bytes 110600 | tf_op jit(solution)/shard_map/ppermute | solution.py:385
  32.2 2.1 %conv.1 = (f32[2,256,128]{2,1,0:T(8,128)S(1)}, f32[2,256,128]{2,1,0:T(8,128)S(1)}, f32[2,128,128]{2,1,0:T(8,128)S(1)}, f32[16,256]{1,0:T(8,128)S(1)}, f32[16,256...) custom-call(f32[16,256]{1,0:T(8,128)} %bitcast.6, ...), custom_call_target="tpu_custom_call" | custom-call | flops 8388608 | bytes 524288 | tf_op jit(solution)/shard_map/conv/pallas_call | solution.py:372
  34.3 0.2 collective-permute-done.7.got_ref
  34.5 1.1 %finish.1 = (bf16[256,256]{1,0:T(8,128)(2,1)}, bf16[256,256]{1,0:T(8,128)(2,1)}, bf16[256,256]{1,0:T(8,128)(2,1)}, f32[16,256]{1,0:T(8,128)}, f32[16,256]{1,0:T(8,128)}, /*index=5*/f32[1,256]{1,0:T(1,128)}) custom-call(bf16[104,256]{1,0:T(8,128)(2,1)S(1)} %get-tuple-element.47.own_ref, bf16[72,256]{1,0:T(8,128)(2,1)S(1)} %collective-permute-done.7.got_ref, ...), custom_call_target="tpu_custom_call" | custom-call | bytes 524288 | tf_op jit(solution)/shard_map/finish/pallas_call | solution.py:372
  (1 shorter events, 0.0 us)
Async XLA Ops:
  3.6 5.7 %collective-permute-start.2 = (bf16[104,256]{1,0:T(8,128)(2,1)S(1)}, bf16[104,256]{1,0:T(8,128)(2,1)S(1)}, u32[]{:S(2)}, u32[]{:S(2)}) collective-permute-start(bf16[104,256]{1,0:T(8,128)(2,1)S(1)} %get-tuple-element.39.z0), channel_id=1, source_target_pairs={{0,8},{4,12},{8,0},{12,4},{16,24},{20,28},{24,16},{28,20},{32,40},... | collective-permute-start | bytes 159752 | tf_op jit(solution)/shard_map/ppermute | solution.py:385
  6.7 5.3 %collective-permute-start.1 = (bf16[104,256]{1,0:T(8,128)(2,1)S(1)}, bf16[104,256]{1,0:T(8,128)(2,1)S(1)}, u32[]{:S(2)}, u32[]{:S(2)}) collective-permute-start(bf16[104,256]{1,0:T(8,128)(2,1)S(1)} %get-tuple-element.39.z0), channel_id=1, source_target_pairs={{0,12},{4,8},{8,4},{12,0},{16,28},{20,24},{24,20},{28,16},{32,44},... | collective-permute-start | bytes 159752 | tf_op jit(solution)/shard_map/ppermute | solution.py:385
  7.9 4.2 %collective-permute-start = (bf16[104,256]{1,0:T(8,128)(2,1)S(1)}, bf16[104,256]{1,0:T(8,128)(2,1)S(1)}, u32[]{:S(2)}, u32[]{:S(2)}) collective-permute-start(bf16[104,256]{1,0:T(8,128)(2,1)S(1)} %get-tuple-element.39.z0), channel_id=1, source_target_pairs={{0,4},{4,0},{8,12},{12,8},{16,20},{20,16},{24,28},{28,24},{32,36},... | collective-permute-start | bytes 159752 | tf_op jit(solution)/shard_map/ppermute | solution.py:385
  12.2 5.8 %collective-permute-start.5 = (bf16[104,256]{1,0:T(8,128)(2,1)S(1)}, bf16[104,256]{1,0:T(8,128)(2,1)S(1)}, u32[]{:S(2)}, u32[]{:S(2)}) collective-permute-start(bf16[104,256]{1,0:T(8,128)(2,1)S(1)} %get-tuple-element.41.z0), channel_id=1, source_target_pairs={{0,32},{4,36},{8,40},{12,44},{16,48},{20,52},{24,56},{28,60},{32,0... | collective-permute-start | bytes 159752 | tf_op jit(solution)/shard_map/ppermute | solution.py:385
  15.5 5.3 %collective-permute-start.4 = (bf16[104,256]{1,0:T(8,128)(2,1)S(1)}, bf16[104,256]{1,0:T(8,128)(2,1)S(1)}, u32[]{:S(2)}, u32[]{:S(2)}) collective-permute-start(bf16[104,256]{1,0:T(8,128)(2,1)S(1)} %get-tuple-element.41.z0), channel_id=1, source_target_pairs={{0,48},{4,52},{8,56},{12,60},{16,32},{20,36},{24,40},{28,44},{32,1... | collective-permute-start | bytes 159752 | tf_op jit(solution)/shard_map/ppermute | solution.py:385
  16.6 4.3 %collective-permute-start.3 = (bf16[104,256]{1,0:T(8,128)(2,1)S(1)}, bf16[104,256]{1,0:T(8,128)(2,1)S(1)}, u32[]{:S(2)}, u32[]{:S(2)}) collective-permute-start(bf16[104,256]{1,0:T(8,128)(2,1)S(1)} %get-tuple-element.41.z0), channel_id=1, source_target_pairs={{0,16},{4,20},{8,24},{12,28},{16,0},{20,4},{24,8},{28,12},{32,48},... | collective-permute-start | bytes 159752 | tf_op jit(solution)/shard_map/ppermute | solution.py:385
  21.0 5.5 %collective-permute-start.6 = (bf16[104,256]{1,0:T(8,128)(2,1)S(1)}, bf16[104,256]{1,0:T(8,128)(2,1)S(1)}, u32[]{:S(2)}, u32[]{:S(2)}) collective-permute-start(bf16[104,256]{1,0:T(8,128)(2,1)S(1)} %get-tuple-element.44.refs_0_), channel_id=1, source_target_pairs={{0,64},{4,68},{8,72},{12,76},{16,80},{20,84},{24,88},{28,92},{32,9... | collective-permute-start | bytes 159752 | tf_op jit(solution)/shard_map/ppermute | solution.py:385
  26.5 8.0 %collective-permute-start.7 = (bf16[72,256]{1,0:T(8,128)(2,1)S(1)}, bf16[72,256]{1,0:T(8,128)(2,1)S(1)}, u32[]{:S(2)}, u32[]{:S(2)}) collective-permute-start(bf16[72,256]{1,0:T(8,128)(2,1)S(1)} %get-tuple-element.48), channel_id=1, source_target_pairs={{0,192},{4,196},{8,200},{12,204},{16,208},{20,212},{24,216},{28,22... | collective-permute-start | bytes 110600 | tf_op jit(solution)/shard_map/ppermute | solution.py:385

commit v5 on v4

--- a/solution.py
+++ b/solution.py
@@ -13,6 +13,8 @@
 SEGS = 8
 LANES = 128
 GROUP = 4
+STEP = 8
+PAIR = 2
 
 
 def product(a, b):
@@ -56,48 +58,77 @@
             row = w_all[m : m + 1, i * LANES : (i + 1) * LANES]
             w_ref[i, pl.ds(m * SEGS, SEGS), :] = jnp.broadcast_to(row, (SEGS, LANES))
 
-    def one(base, i):
-        at = [pl.ds((base * GROUP + m) * SEGS, SEGS) for m in range(GROUP)]
-        w = [w_ref[i, a, :] for a in at]
+    blocks = range(0, steps, STEP)
+
+    def lag_sums(i):
+        lags = [None] * STEP
+        for first in blocks:
+            x = [gated_ref[i, pl.ds((first + j) * SEGS, SEGS), :] for j in range(STEP)]
+            y = [grad_ref[i, pl.ds((first + j) * SEGS, SEGS), :] for j in range(STEP)]
+            for j in range(STEP):
+                for back in range(j + 1):
+                    term = y[j] * x[j - back]
+                    lags[back] = term if lags[back] is None else lags[back] + term
+        return lags
+
+    def weighted(low, w):
+        part = w[STEP - 2] * low[STEP - 1]
+        slope = part
+        for j in range(STEP - 2, 0, -1):
+            part = part + w[j - 1] * low[j]
+            slope = slope + part
+        return part + low[0], slope
+
+    def one(base, i, lags):
+        at = [pl.ds((base * PAIR + m) * SEGS, SEGS) for m in range(PAIR)]
+        w = [[w_ref[i, a, :]] for a in at]
+        for powers in w:
+            for j in range(1, STEP):
+                powers.append(powers[0] * powers[j - 1])
         zero = jnp.zeros((SEGS, LANES), F32)
-        h, h1, p, t, r, r1 = ([zero] * GROUP for _ in range(6))
-        for j in range(steps):
-            x = gated_ref[i, pl.ds(j * SEGS, SEGS), :]
-            y = grad_ref[i, pl.ds(j * SEGS, SEGS), :]
-            back = grad_ref[i, pl.ds((steps - 1 - j) * SEGS, SEGS), :]
-            for m in range(GROUP):
-                h[m] = w[m] * h[m] + x
-                h1[m] = w[m] * h1[m] + h[m]
-                p[m] = p[m] + y * h[m]
-                t[m] = t[m] + y * h1[m]
-                r[m] = w[m] * r[m] + back
-                r1[m] = w[m] * r1[m] + r[m]
-        for m in range(GROUP):
-            e_ref[i, at[m], :] = w[m] * h[m]
-            e1_ref[i, at[m], :] = w[m] * h1[m]
-            g_ref[i, at[m], :] = r[m]
-            g1_ref[i, at[m], :] = r1[m] - r[m]
-            p_ref[i, at[m], :] = p[m]
-            t_ref[i, at[m], :] = t[m] - p[m]
+        h, h1, p, t, g, g1, below, power = ([zero] * PAIR for _ in range(8))
+        for first in blocks:
+            x = [gated_ref[i, pl.ds((first + j) * SEGS, SEGS), :] for j in range(STEP)]
+            y = [grad_ref[i, pl.ds((first + j) * SEGS, SEGS), :] for j in range(STEP)]
+            for m in range(PAIR):
+                into, into1 = weighted(x[::-1], w[m])
+                out, out1 = weighted(y, w[m])
+                if first == 0:
+                    h[m], h1[m], g[m], g1[m], power[m] = into, into1, out, out1, w[m][-1]
+                    continue
+                p[m] = p[m] + h[m] * out
+                t[m] = t[m] + (h1[m] * out + h[m] * out1)
+                wh = w[m][-1] * h[m]
+                h1[m] = (w[m][-1] * h1[m] + float(STEP) * wh) + into1
+                h[m] = wh + into
+                below[m] = below[m] + g[m]
+                g[m] = g[m] + power[m] * out
+                g1[m] = g1[m] + power[m] * out1
+                if first + STEP < steps:
+                    power[m] = power[m] * w[m][-1]
+        for m in range(PAIR):
+            inside, inside1 = weighted(lags, w[m])
+            e_ref[i, at[m], :] = w[m][0] * h[m]
+            e1_ref[i, at[m], :] = w[m][0] * (h1[m] + h[m])
+            g_ref[i, at[m], :] = g[m]
+            g1_ref[i, at[m], :] = g1[m] + float(STEP) * (float(len(blocks) - 1) * g[m] - below[m])
+            p_ref[i, at[m], :] = w[m][0] * p[m] + inside
+            t_ref[i, at[m], :] = w[m][0] * (t[m] + p[m]) + inside1
 
     for i, ln in enumerate(columns):
         for copy in copies[1 + 4 * i : 5 + 4 * i]:
             copy.wait()
-        skip = jnp.zeros((8, LANES), F32)
         for seg in range(SEGS):
             for part in range(steps // 16):
                 at = pl.ds(seg * steps + part * 16, 16)
-                gated = product(k_ref[at, ln], v_ref[at, ln])
-                grad = product(u_ref[at, ln], q_ref[at, ln])
-                both = gated * grad
-                skip = skip + both[:8] + both[8:]
                 to = pl.ds(part * 16 * SEGS + seg, 16, stride=SEGS)
-                gated_ref[i, to, :] = gated
-                grad_ref[i, to, :] = grad
-        skip = jnp.sum(skip, axis=0, keepdims=True)
+                gated_ref[i, to, :] = product(k_ref[at, ln], v_ref[at, ln])
+                grad_ref[i, to, :] = product(u_ref[at, ln], q_ref[at, ln])
+        lags = lag_sums(i)
+        skip = jnp.sum(lags[0], axis=0, keepdims=True)
         z_ref[6 * modes :, ln] = jnp.broadcast_to(skip, (8, LANES)).astype(BF16)
-        for base in range(modes // GROUP):
-            one(base, i)
+        for base in range(modes // PAIR):
+            one(base, i, lags)
 
     for i in range(tiles):
         ln = slice(i * LANES, (i + 1) * LANES)
@@ -130,18 +161,14 @@
 
 
 def conv_kernel(
-    stride, count,
-    res_hbm, skip_hbm, gated_ref, grad_ref, dec_t_ref, pre_ref, post_ref, s_ref, r_ref, k_ref, v_ref, u_ref,
-    fwd_ref, bwd_ref, scale_ref, roots_ref, ratio_ref, dq_ref, dk_ref, dv_ref,
-    res_t_ref, skip_ref, w_ref, a_ref, h_ref, b_ref, sems,
+    res_hbm, skip_hbm, gated_ref, grad_ref, dec_t_ref, pre_ref, post_ref,
+    fwd_ref, bwd_ref, in_ref, out_ref, roots_ref, ratio_ref,
+    res_t_ref, skip_ref, w_ref, a_ref, sems,
 ):
     copies = fetch(sems, (res_hbm, res_t_ref), (skip_hbm, skip_ref))
     tiles, rows, _ = gated_ref.shape
     modes = dec_t_ref.shape[0]
     steps = rows // SEGS
-    digit, offset = place(stride, 2)
-    right = digit == 1
-    chunks = jnp.where(right, offset, stride - 1 - offset).astype(F32)
     for copy in copies:
         copy.wait()
     dec_t = dec_t_ref[...]
@@ -149,24 +176,17 @@
     scale = res_t_ref[...] * roots
     roots_ref[...] = roots
     ratio_ref[...] = res_t_ref[...] / roots
-    far = scale * jnp.exp(dec_t * (-float(count) * chunks))
-    s, r = s_ref[...], r_ref[...]
     seg_at = lax.broadcasted_iota(jnp.int32, (SEGS, LANES), 0).astype(F32) * float(steps)
-    away = jnp.where(right, seg_at, float(rows - steps + 1) - seg_at)
     for i in range(tiles):
         ln = slice(i * LANES, (i + 1) * LANES)
         for m in range(modes):
             at = pl.ds(m * SEGS, SEGS)
-
-            def spread(x):
-                return jnp.broadcast_to(x[m : m + 1, ln], (SEGS, LANES))
-
-            d = spread(dec_t)
+            d = jnp.broadcast_to(dec_t[m : m + 1, ln], (SEGS, LANES))
+            a = jnp.broadcast_to(scale[m : m + 1, ln], (SEGS, LANES))
             w_ref[i, at, :] = jnp.exp(-d)
-            a_ref[i, at, :] = spread(scale)
-            scale_ref[i, at, :] = spread(far) * jnp.exp(-d * away)
-            h_ref[i, at, :] = pre_ref[i, at, :] + jnp.exp(-d * seg_at) * spread(s)
-            b_ref[i, at, :] = post_ref[i, at, :] + jnp.exp(-d * (float(rows - steps) - seg_at)) * spread(r)
+            a_ref[i, at, :] = a
+            in_ref[i, at, :] = a * jnp.exp(-d * seg_at)
+            out_ref[i, at, :] = a * jnp.exp(-d * (float(rows - steps + 1) - seg_at))
 
     def one(i, _):
         direct = jnp.broadcast_to(skip_ref[:, lanes_of(i)], (SEGS, LANES))
@@ -174,8 +194,8 @@
             at = [pl.ds((base + m) * SEGS, SEGS) for m in range(GROUP)]
             w = [w_ref[i, x, :] for x in at]
             a = [a_ref[i, x, :] for x in at]
-            h = [h_ref[i, x, :] for x in at]
-            r = [b_ref[i, x, :] for x in at]
+            h = [pre_ref[i, x, :] for x in at]
+            r = [post_ref[i, x, :] for x in at]
             for j in range(steps):
                 at_f = pl.ds(j * SEGS, SEGS)
                 at_b = pl.ds((steps - 1 - j) * SEGS, SEGS)
@@ -192,6 +212,60 @@
         return 0
 
     lax.fori_loop(0, tiles, one, 0)
+
+
+def rows_in(seg, part, steps):
+    return pl.ds(seg * steps + part * 16, 16), pl.ds(part * 16 * SEGS + seg, 16, stride=SEGS)
+
+
+def query_rows(u_ref, total_ref, dq_ref, i, frm, to, ln):
+    conv = total_ref[i, frm, :].astype(BF16).astype(F32)
+    dq_ref[to, ln] = (u_ref[to, ln].astype(F32) * conv).astype(BF16)
+
+
+def pair_rows(k_ref, v_ref, total_ref, dk_ref, dv_ref, i, frm, to, ln):
+    gg = total_ref[i, frm, :].astype(BF16).astype(F32)
+    dk_ref[to, ln] = (gg * v_ref[to, ln].astype(F32)).astype(BF16)
+    dv_ref[to, ln] = (gg * k_ref[to, ln].astype(F32)).astype(BF16)
+
+
+def add_state(local_ref, total_ref, scale_ref, state_ref, w_ref, order, tiles, modes):
+    def one(i, _):
+        ln = lanes_of(i)
+
+        def spread(ref, m):
+            return jnp.broadcast_to(ref[pl.ds(m, 1), ln], (SEGS, LANES))
+
+        w = [spread(w_ref, m) for m in range(modes)]
+        c = [scale_ref[i, pl.ds(m * SEGS, SEGS), :] * spread(state_ref, m) for m in range(modes)]
+        for n, j in enumerate(order):
+            here = pl.ds(j * SEGS, SEGS)
+            y = local_ref[i, here, :]
+            for m in range(modes):
+                y = y + c[m]
+                if n < len(order) - 1:
+                    c[m] = c[m] * w[m]
+            total_ref[i, here, :] = y
+        return 0
+
+    lax.fori_loop(0, tiles, one, 0)
+
+
+def known_kernel(
+    stride, count,
+    dec_t_ref, s_ref, r_ref, in_ref, out_ref, fwd_old, bwd_old, k_ref, v_ref, u_ref,
+    fwd_ref, bwd_ref, far_ref, w_ref, dq_ref, dk_ref, dv_ref,
+):
+    tiles, rows, _ = fwd_ref.shape
+    modes = dec_t_ref.shape[0]
+    steps = rows // SEGS
+    digit, offset = place(stride, 2)
+    chunks = jnp.where(digit == 1, offset, stride - 1 - offset).astype(F32)
+    dec_t = dec_t_ref[...]
+    far_ref[...] = jnp.exp(dec_t * (-float(count) * chunks))
+    w_ref[...] = jnp.exp(-dec_t)
+    add_state(fwd_old, fwd_ref, in_ref, s_ref, w_ref, range(steps), tiles, modes)
+    add_state(bwd_old, bwd_ref, out_ref, r_ref, w_ref, range(steps - 1, -1, -1), tiles, modes)
     for seg in range(SEGS):
         for part in range(steps // 16):
             to, frm = rows_in(seg, part, steps)
@@ -201,23 +275,8 @@
                 pair_rows(k_ref, v_ref, bwd_ref, dk_ref, dv_ref, i, frm, to, ln)
 
 
-def rows_in(seg, part, steps):
-    return pl.ds(seg * steps + part * 16, 16), pl.ds(part * 16 * SEGS + seg, 16, stride=SEGS)
-
-
-def query_rows(u_ref, total_ref, dq_ref, i, frm, to, ln):
-    conv = total_ref[i, frm, :].astype(BF16).astype(F32)
-    dq_ref[to, ln] = (u_ref[to, ln].astype(F32) * conv).astype(BF16)
-
-
-def pair_rows(k_ref, v_ref, total_ref, dk_ref, dv_ref, i, frm, to, ln):
-    gg = total_ref[i, frm, :].astype(BF16).astype(F32)
-    dk_ref[to, ln] = (gg * v_ref[to, ln].astype(F32)).astype(BF16)
-    dv_ref[to, ln] = (gg * k_ref[to, ln].astype(F32)).astype(BF16)
-
-
-def four_kernel(stride, count, z0, z1, z3, z2, *refs):
-    combine_kernel(stride, 4, count, False, z0, z1, z2, z3, *refs)
+def four_kernel(stride, count, z0, z1, z3, z2, dec_t_ref, s_ref, r_ref, *refs):
+    combine_kernel(stride, 4, count, False, z0, z1, z2, z3, dec_t_ref, s_ref, r_ref, *refs[-3:])
 
 
 def combine_kernel(stride, radix, count, last, *refs):
@@ -275,13 +334,13 @@
 
 def finish_kernel(
     stride,
-    own_ref, got_ref, dec_t_ref, roots_ref, ratio_ref, scale_ref, fwd_ref, bwd_ref,
+    own_ref, got_ref, roots_ref, ratio_ref, in_ref, out_ref, far_ref, w_ref, fwd_ref, bwd_ref,
     k_ref, v_ref, u_ref, dq_old, dk_old, dv_old,
     dq_hbm, dk_hbm, dv_hbm, dres_hbm, ddec_hbm, dskip_hbm,
-    dq_ref, dk_ref, dv_ref, dres_ref, ddec_ref, dskip_ref, total_ref, w_ref, c_ref, sems,
+    dq_ref, dk_ref, dv_ref, dres_ref, ddec_ref, dskip_ref, total_ref, c_ref, sems,
 ):
     rows, width = k_ref.shape
-    modes = dec_t_ref.shape[0]
+    modes = w_ref.shape[0]
     steps = rows // SEGS
     tiles = width // LANES
     right = place(stride, 2)[0] == 1
@@ -307,29 +366,7 @@
     ddec_ref[...] = ratio_ref[...] * diff
     dskip_ref[...] = (half(own_ref, 6, 8) + half(got_ref, 4, 8))[:1]
     copies = fetch(sems, (dres_ref, dres_hbm), (ddec_ref, ddec_hbm), (dskip_ref, dskip_hbm), first=2)
-    w_ref[...] = jnp.exp(-dec_t_ref[...])
-    c_ref[...] = got[0]
-
-    def add(local_ref, order):
-        def one(i, _):
-            ln = lanes_of(i)
-
-            def spread(ref, m):
-                return jnp.broadcast_to(ref[pl.ds(m, 1), ln], (SEGS, LANES))
-
-            w = [spread(w_ref, m) for m in range(modes)]
-            c = [scale_ref[i, pl.ds(m * SEGS, SEGS), :] * spread(c_ref, m) for m in range(modes)]
-            for n, j in enumerate(order):
-                here = pl.ds(j * SEGS, SEGS)
-                y = local_ref[i, here, :]
-                for m in range(modes):
-                    y = y + c[m]
-                    if n < steps - 1:
-                        c[m] = c[m] * w[m]
-                total_ref[i, here, :] = y
-            return 0
-
-        lax.fori_loop(0, tiles, one, 0)
+    c_ref[...] = got[0] * far_ref[...]
 
     def rest(work, pairs):
         for seg in range(SEGS):
@@ -343,7 +380,7 @@
 
     @pl.when(right)
     def _():
-        add(fwd_ref, range(steps))
+        add_state(fwd_ref, total_ref, in_ref, c_ref, w_ref, range(steps), tiles, modes)
         rest(
             lambda i, frm, to, ln: query_rows(u_ref, total_ref, dq_ref, i, frm, to, ln),
             [(new, hbm) for _, new, hbm in outs[:1]],
@@ -353,7 +390,7 @@
 
     @pl.when(jnp.logical_not(right))
     def _():
-        add(bwd_ref, range(steps - 1, -1, -1))
+        add_state(bwd_ref, total_ref, out_ref, c_ref, w_ref, range(steps - 1, -1, -1), tiles, modes)
         rest(
             lambda i, frm, to, ln: pair_rows(k_ref, v_ref, total_ref, dk_ref, dv_ref, i, frm, to, ln),
             [(new, hbm) for _, new, hbm in outs[1:]],
@@ -406,13 +443,22 @@
         name="summary",
         hbm=5,
     )
+    fwd, bwd, in_w, out_w, roots, ratio = call(
+        conv_kernel,
+        [big, big, spread, spread, state, state],
+        [residues.T, skip.reshape(1, width), gated, grad, dec_t, pre, post],
+        [state, VMEM((1, width), F32)] + [spread] * 2 + [pltpu.SemaphoreType.DMA((2,))],
+        flops=8 * rows * width * modes,
+        name="conv",
+        hbm=2,
+    )
     s = r = jnp.zeros((modes, width), F32)
     for stride in (1, 4):
         parts = [z] + [exchange(z, k * stride, size) for k in (1, 3, 2)]
         z, s, r = call(
             functools.partial(four_kernel, stride, rows),
             [block, state, state],
-            [*parts, dec_t, s, r],
+            [*parts, dec_t, s, r] + [roots] * (stride == 1),
             name=f"combine{stride}",
         )
     z, s, r, send = call(
@@ -422,14 +468,12 @@
         name="combine16",
     )
     got = exchange(send, 48, size)
-    fwd, bwd, scale, roots, ratio, dq, dk, dv = call(
-        functools.partial(conv_kernel, 32, rows),
-        [big, big, spread, state, state] + [local] * 3,
-        [residues.T, skip.reshape(1, width), gated, grad, dec_t, pre, post, s, r, keys, values, upstream],
-        [state, VMEM((1, width), F32)] + [spread] * 4 + [pltpu.SemaphoreType.DMA((2,))],
-        flops=8 * rows * width * modes,
-        name="conv",
-        hbm=2,
+    fwd, bwd, far, w, dq, dk, dv = call(
+        functools.partial(known_kernel, 32, rows),
+        [big, big, state, state] + [local] * 3,
+        [dec_t, s, r, in_w, out_w, fwd, bwd, keys, values, upstream],
+        flops=4 * rows * width * modes,
+        name="known",
     )
     outs = [jax.ShapeDtypeStruct((rows, width), BF16)] * 3
     outs += [jax.ShapeDtypeStruct((modes, width), F32)] * 2
@@ -437,8 +481,8 @@
     dq, dk, dv, dres, ddec, dskip = call(
         functools.partial(finish_kernel, 32),
         outs,
-        [z, got, dec_t, roots, ratio, scale, fwd, bwd, keys, values, upstream, dq, dk, dv],
-        [local] * 3 + [state] * 2 + [VMEM((1, width), F32), big, state, state, pltpu.SemaphoreType.DMA((7,))],
+        [z, got, roots, ratio, in_w, out_w, far, w, fwd, bwd, keys, values, upstream, dq, dk, dv],
+        [local] * 3 + [state] * 2 + [VMEM((1, width), F32), big, state, pltpu.SemaphoreType.DMA((7,))],
         name="finish",
         out_space=pltpu.HBM,
     )

time: 36 us -> 35.5 us (0.986)
  waiting for transfers between devices: 10.8 us -> 10.2 us
    ppermute x8, waiting for transfers between devices: 10.8 us -> 10.2 us  [exchange(): return lax.ppermute(array, 'seq', [(i, i ^ mask) for i in range(size)])]
    pallas_call x6 -> x7, Pallas kernels: 6.56 us -> 6.62 us  [call(): pl.pallas_call(kernel, out_shape=outs, in_specs=[pl.BlockSpec(memory_spac...]
  transfers between devices with their start and end apart: 8 -> 8, of which waited for: 6 -> 5; matrix products, arithmetic and copies ran while one was open for 0% -> 0% of each run, Pallas kernels for 6% -> 8%
where the time goes in v5:
time: 35.5 us; the launch traced here: 35.2 us
  starting transfers between devices  17.7 us (50%)
  waiting for transfers between devices  10.2 us (29%)
  Pallas kernels  6.62 us (19%)
  between operations  0.68 us (2%)
    ppermute x8, starting transfers between devices, exchange(): return lax.ppermute(array, 'seq', [(i, i ^ mask) for i in range(size)])  17.7 us
    ppermute x8, waiting for transfers between devices, exchange(): return lax.ppermute(array, 'seq', [(i, i ^ mask) for i in range(size)])  10.2 us
    pallas_call x7, Pallas kernels, call(): pl.pallas_call(kernel, out_shape=outs, in_specs=[pl.BlockSpec(memory_spac...  6.62 us
  transfers between devices with their start and end apart: 8, of which 5 were waited for; matrix products, arithmetic and copies ran while one was open for 0% of the time, Pallas kernels for 8%

profile of v5, /device:TPU:32, one launch (start us, length us, event | category | flops | bytes accessed | tf_op | source)
XLA Modules:
  0.0 35.2 jit_solution(16564577784714120620)
XLA Ops:
  0.6 2.5 %summary.1 = (bf16[104,256]{1,0:T(8,128)(2,1)S(1)}, f32[2,256,128]{2,1,0:T(8,128)S(1)}, f32[2,256,128]{2,1,0:T(8,128)S(1)}, f32[2,128,128]{2,1,0:T(8,128)S(1)}, ...) custom-call(f32[16,256]{1,0:T(8,128)} %bitcast.6, ...), custom_call_target="tpu_custom_call" | custom-call | flops 12582912 | bytes 524288 | tf_op jit(solution)/shard_map/summary/pallas_call | solution.py:409
  3.1 3.1 %collective-permute-start.2 = (bf16[104,256]{1,0:T(8,128)(2,1)S(1)}, bf16[104,256]{1,0:T(8,128)(2,1)S(1)}, u32[]{:S(2)}, u32[]{:S(2)}) collective-permute-start(bf16[104,256]{1,0:T(8,128)(2,1)S(1)} %get-tuple-element.44.z0), channel_id=1, source_target_pairs={{0,8},{4,12},{8,0},{12,4},{16,24},{20,28},{24,16},{28,20},{32,40},... | collective-permute-start | bytes 159752 | tf_op jit(solution)/shard_map/ppermute | solution.py:422
  6.2 1.1 %collective-permute-start.1 = (bf16[104,256]{1,0:T(8,128)(2,1)S(1)}, bf16[104,256]{1,0:T(8,128)(2,1)S(1)}, u32[]{:S(2)}, u32[]{:S(2)}) collective-permute-start(bf16[104,256]{1,0:T(8,128)(2,1)S(1)} %get-tuple-element.44.z0), channel_id=1, source_target_pairs={{0,12},{4,8},{8,4},{12,0},{16,28},{20,24},{24,20},{28,16},{32,44},... | collective-permute-start | bytes 159752 | tf_op jit(solution)/shard_map/ppermute | solution.py:422
  7.4 0.0 collective-permute-start
  7.4 1.9 %conv.1 = (f32[2,256,128]{2,1,0:T(8,128)S(1)}, f32[2,256,128]{2,1,0:T(8,128)S(1)}, f32[2,128,128]{2,1,0:T(8,128)S(1)}, f32[2,128,128]{2,1,0:T(8,128)S(1)}, f32[16,256]{1,0:T(8,128)S(1)}, /*index=5*/f32[16,256]{1,0:T(8,128)S(1)}) custom-call(f32[16,256]{1,0:T(8,128)} %bitcast.7, f32[1,256]{1,0:T(1,128)} %bitcast.8, ...), custom_call_target="tpu_custom_call" | custom-call | flops 8388608 | bytes 524288 | tf_op jit(solution)/shard_map/conv/pallas_call | solution.py:409
  9.3 0.0 collective-permute-done.2.z2
  9.3 2.3 %collective-permute-done.1.z3 = bf16[104,256]{1,0:T(8,128)(2,1)S(1)} collective-permute-done((bf16[104,256]{1,0:T(8,128)(2,1)S(1)}, bf16[104,256]{1,0:T(8,128)(2,1)S(1)}, u32[]{:S(2)}, u32[]{:S(2)}) %collective-permute-start.1) | collective-permute-done | bytes 53280 | tf_op jit(solution)/shard_map/ppermute | solution.py:422
  11.6 0.0 collective-permute-done.z1
  11.6 0.1 combine1.1
  11.7 3.3 %collective-permute-start.5 = (bf16[104,256]{1,0:T(8,128)(2,1)S(1)}, bf16[104,256]{1,0:T(8,128)(2,1)S(1)}, u32[]{:S(2)}, u32[]{:S(2)}) collective-permute-start(bf16[104,256]{1,0:T(8,128)(2,1)S(1)} %get-tuple-element.51.z0), channel_id=1, source_target_pairs={{0,32},{4,36},{8,40},{12,44},{16,48},{20,52},{24,56},{28,60},{32,0... | collective-permute-start | bytes 159752 | tf_op jit(solution)/shard_map/ppermute | solution.py:422
  15.0 1.1 %collective-permute-start.4 = (bf16[104,256]{1,0:T(8,128)(2,1)S(1)}, bf16[104,256]{1,0:T(8,128)(2,1)S(1)}, u32[]{:S(2)}, u32[]{:S(2)}) collective-permute-start(bf16[104,256]{1,0:T(8,128)(2,1)S(1)} %get-tuple-element.51.z0), channel_id=1, source_target_pairs={{0,48},{4,52},{8,56},{12,60},{16,32},{20,36},{24,40},{28,44},{32,1... | collective-permute-start | bytes 159752 | tf_op jit(solution)/shard_map/ppermute | solution.py:422
  16.1 0.0 collective-permute-start.3
  16.1 1.4 %collective-permute-done.5.z2 = bf16[104,256]{1,0:T(8,128)(2,1)S(1)} collective-permute-done((bf16[104,256]{1,0:T(8,128)(2,1)S(1)}, bf16[104,256]{1,0:T(8,128)(2,1)S(1)}, u32[]{:S(2)}, u32[]{:S(2)}) %collective-permute-start.5) | collective-permute-done | bytes 53280 | tf_op jit(solution)/shard_map/ppermute | solution.py:422
  17.5 2.8 %collective-permute-done.4.z3 = bf16[104,256]{1,0:T(8,128)(2,1)S(1)} collective-permute-done((bf16[104,256]{1,0:T(8,128)(2,1)S(1)}, bf16[104,256]{1,0:T(8,128)(2,1)S(1)}, u32[]{:S(2)}, u32[]{:S(2)}) %collective-permute-start.4) | collective-permute-done | bytes 53280 | tf_op jit(solution)/shard_map/ppermute | solution.py:422
  20.3 0.0 collective-permute-done.3.z1
  20.3 0.1 combine4.1
  20.5 3.4 %collective-permute-start.6 = (bf16[104,256]{1,0:T(8,128)(2,1)S(1)}, bf16[104,256]{1,0:T(8,128)(2,1)S(1)}, u32[]{:S(2)}, u32[]{:S(2)}) collective-permute-start(bf16[104,256]{1,0:T(8,128)(2,1)S(1)} %get-tuple-element.54.refs_0_), channel_id=1, source_target_pairs={{0,64},{4,68},{8,72},{12,76},{16,80},{20,84},{24,88},{28,92},{32,9... | collective-permute-start | bytes 159752 | tf_op jit(solution)/shard_map/ppermute | solution.py:422
  23.8 2.1 %collective-permute-done.6.refs_1_ = bf16[104,256]{1,0:T(8,128)(2,1)S(1)} collective-permute-done((bf16[104,256]{1,0:T(8,128)(2,1)S(1)}, bf16[104,256]{1,0:T(8,128)(2,1)S(1)}, u32[]{:S(2)}, u32[]{:S(2)}) %collective-permute-start.6) | collective-permute-done | bytes 53280 | tf_op jit(solution)/shard_map/ppermute | solution.py:422
  26.0 0.1 combine16.1
  26.0 5.7 %collective-permute-start.7 = (bf16[72,256]{1,0:T(8,128)(2,1)S(1)}, bf16[72,256]{1,0:T(8,128)(2,1)S(1)}, u32[]{:S(2)}, u32[]{:S(2)}) collective-permute-start(bf16[72,256]{1,0:T(8,128)(2,1)S(1)} %get-tuple-element.58), channel_id=1, source_target_pairs={{0,192},{4,196},{8,200},{12,204},{16,208},{20,212},{24,216},{28,22... | collective-permute-start | bytes 110600 | tf_op jit(solution)/shard_map/ppermute | solution.py:422
  31.7 0.7 %known.1 = (f32[2,256,128]{2,1,0:T(8,128)S(1)}, f32[2,256,128]{2,1,0:T(8,128)S(1)}, f32[16,256]{1,0:T(8,128)S(1)}, f32[16,256]{1,0:T(8,128)S(1)}, bf16[256,256]{...) custom-call(f32[16,256]{1,0:T(8,128)S(1)} %get-tuple-element.45.dec_t_ref.refs_2_, ...), custom_call_target="tpu_custom_call" | custom-call | flops 4194304 | bytes 524288 | tf_op jit(solution)/shard_map/known/pallas_call | solution.py:409
  32.5 1.6 %collective-permute-done.7.got_ref = bf16[72,256]{1,0:T(8,128)(2,1)S(1)} collective-permute-done((bf16[72,256]{1,0:T(8,128)(2,1)S(1)}, bf16[72,256]{1,0:T(8,128)(2,1)S(1)}, u32[]{:S(2)}, u32[]{:S(2)}) %collective-permute-start.7) | collective-permute-done | bytes 36896 | tf_op jit(solution)/shard_map/ppermute | solution.py:422
  34.0 1.2 %finish.1 = (bf16[256,256]{1,0:T(8,128)(2,1)}, bf16[256,256]{1,0:T(8,128)(2,1)}, bf16[256,256]{1,0:T(8,128)(2,1)}, f32[16,256]{1,0:T(8,128)}, f32[16,256]{1,0:T(8,128)}, /*index=5*/f32[1,256]{1,0:T(1,128)}) custom-call(bf16[104,256]{1,0:T(8,128)(2,1)S(1)} %get-tuple-element.57.own_ref, bf16[72,256]{1,0:T(8,128)(2,1)S(1)} %collective-permute-done.7.got_ref, ...), custom_call_target="tpu_custom_call" | custom-call | bytes 524288 | tf_op jit(solution)/shard_map/finish/pallas_call | solution.py:409
  (1 shorter events, 0.0 us)
Async XLA Ops:
  3.1 6.2 %collective-permute-start.2 = (bf16[104,256]{1,0:T(8,128)(2,1)S(1)}, bf16[104,256]{1,0:T(8,128)(2,1)S(1)}, u32[]{:S(2)}, u32[]{:S(2)}) collective-permute-start(bf16[104,256]{1,0:T(8,128)(2,1)S(1)} %get-tuple-element.44.z0), channel_id=1, source_target_pairs={{0,8},{4,12},{8,0},{12,4},{16,24},{20,28},{24,16},{28,20},{32,40},... | collective-permute-start | bytes 159752 | tf_op jit(solution)/shard_map/ppermute | solution.py:422
  6.2 5.3 %collective-permute-start.1 = (bf16[104,256]{1,0:T(8,128)(2,1)S(1)}, bf16[104,256]{1,0:T(8,128)(2,1)S(1)}, u32[]{:S(2)}, u32[]{:S(2)}) collective-permute-start(bf16[104,256]{1,0:T(8,128)(2,1)S(1)} %get-tuple-element.44.z0), channel_id=1, source_target_pairs={{0,12},{4,8},{8,4},{12,0},{16,28},{20,24},{24,20},{28,16},{32,44},... | collective-permute-start | bytes 159752 | tf_op jit(solution)/shard_map/ppermute | solution.py:422
  7.4 4.2 %collective-permute-start = (bf16[104,256]{1,0:T(8,128)(2,1)S(1)}, bf16[104,256]{1,0:T(8,128)(2,1)S(1)}, u32[]{:S(2)}, u32[]{:S(2)}) collective-permute-start(bf16[104,256]{1,0:T(8,128)(2,1)S(1)} %get-tuple-element.44.z0), channel_id=1, source_target_pairs={{0,4},{4,0},{8,12},{12,8},{16,20},{20,16},{24,28},{28,24},{32,36},... | collective-permute-start | bytes 159752 | tf_op jit(solution)/shard_map/ppermute | solution.py:422
  11.7 5.8 %collective-permute-start.5 = (bf16[104,256]{1,0:T(8,128)(2,1)S(1)}, bf16[104,256]{1,0:T(8,128)(2,1)S(1)}, u32[]{:S(2)}, u32[]{:S(2)}) collective-permute-start(bf16[104,256]{1,0:T(8,128)(2,1)S(1)} %get-tuple-element.51.z0), channel_id=1, source_target_pairs={{0,32},{4,36},{8,40},{12,44},{16,48},{20,52},{24,56},{28,60},{32,0... | collective-permute-start | bytes 159752 | tf_op jit(solution)/shard_map/ppermute | solution.py:422
  15.0 5.3 %collective-permute-start.4 = (bf16[104,256]{1,0:T(8,128)(2,1)S(1)}, bf16[104,256]{1,0:T(8,128)(2,1)S(1)}, u32[]{:S(2)}, u32[]{:S(2)}) collective-permute-start(bf16[104,256]{1,0:T(8,128)(2,1)S(1)} %get-tuple-element.51.z0), channel_id=1, source_target_pairs={{0,48},{4,52},{8,56},{12,60},{16,32},{20,36},{24,40},{28,44},{32,1... | collective-permute-start | bytes 159752 | tf_op jit(solution)/shard_map/ppermute | solution.py:422
  16.1 4.3 %collective-permute-start.3 = (bf16[104,256]{1,0:T(8,128)(2,1)S(1)}, bf16[104,256]{1,0:T(8,128)(2,1)S(1)}, u32[]{:S(2)}, u32[]{:S(2)}) collective-permute-start(bf16[104,256]{1,0:T(8,128)(2,1)S(1)} %get-tuple-element.51.z0), channel_id=1, source_target_pairs={{0,16},{4,20},{8,24},{12,28},{16,0},{20,4},{24,8},{28,12},{32,48},... | collective-permute-start | bytes 159752 | tf_op jit(solution)/shard_map/ppermute | solution.py:422
  20.5 5.5 %collective-permute-start.6 = (bf16[104,256]{1,0:T(8,128)(2,1)S(1)}, bf16[104,256]{1,0:T(8,128)(2,1)S(1)}, u32[]{:S(2)}, u32[]{:S(2)}) collective-permute-start(bf16[104,256]{1,0:T(8,128)(2,1)S(1)} %get-tuple-element.54.refs_0_), channel_id=1, source_target_pairs={{0,64},{4,68},{8,72},{12,76},{16,80},{20,84},{24,88},{28,92},{32,9... | collective-permute-start | bytes 159752 | tf_op jit(solution)/shard_map/ppermute | solution.py:422
  26.0 8.0 %collective-permute-start.7 = (bf16[72,256]{1,0:T(8,128)(2,1)S(1)}, bf16[72,256]{1,0:T(8,128)(2,1)S(1)}, u32[]{:S(2)}, u32[]{:S(2)}) collective-permute-start(bf16[72,256]{1,0:T(8,128)(2,1)S(1)} %get-tuple-element.58), channel_id=1, source_target_pairs={{0,192},{4,196},{8,200},{12,204},{16,208},{20,212},{24,216},{28,22... | collective-permute-start | bytes 110600 | tf_op jit(solution)/shard_map/ppermute | solution.py:422

commit v6 on v5

--- a/solution.py
+++ b/solution.py
@@ -253,19 +253,22 @@
 
 def known_kernel(
     stride, count,
-    dec_t_ref, s_ref, r_ref, in_ref, out_ref, fwd_old, bwd_old, k_ref, v_ref, u_ref,
-    fwd_ref, bwd_ref, far_ref, w_ref, dq_ref, dk_ref, dv_ref,
+    pair_ref, dec_t_ref, s_ref, r_ref, in_ref, out_ref, fwd_old, bwd_old, k_ref, v_ref, u_ref,
+    fwd_ref, bwd_ref, s_out, r_out, w_ref, dq_ref, dk_ref, dv_ref,
 ):
     tiles, rows, _ = fwd_ref.shape
     modes = dec_t_ref.shape[0]
     steps = rows // SEGS
     digit, offset = place(stride, 2)
-    chunks = jnp.where(digit == 1, offset, stride - 1 - offset).astype(F32)
+    offset = offset.astype(F32)
     dec_t = dec_t_ref[...]
-    far_ref[...] = jnp.exp(dec_t * (-float(count) * chunks))
+    enter = jnp.exp(dec_t * (-float(count) * offset)) * pair_ref[pl.ds(0, modes), :].astype(F32)
+    leave = jnp.exp(dec_t * (-float(count) * (float(stride - 1) - offset))) * pair_ref[pl.ds(2 * modes, modes), :].astype(F32)
+    s_out[...] = s_ref[...] + jnp.where(digit == 1, enter, 0.0)
+    r_out[...] = r_ref[...] + jnp.where(digit == 1, 0.0, leave)
     w_ref[...] = jnp.exp(-dec_t)
-    add_state(fwd_old, fwd_ref, in_ref, s_ref, w_ref, range(steps), tiles, modes)
-    add_state(bwd_old, bwd_ref, out_ref, r_ref, w_ref, range(steps - 1, -1, -1), tiles, modes)
+    add_state(fwd_old, fwd_ref, in_ref, s_out, w_ref, range(steps), tiles, modes)
+    add_state(bwd_old, bwd_ref, out_ref, r_out, w_ref, range(steps - 1, -1, -1), tiles, modes)
     for seg in range(SEGS):
         for part in range(steps // 16):
             to, frm = rows_in(seg, part, steps)
@@ -275,36 +278,26 @@
                 pair_rows(k_ref, v_ref, bwd_ref, dk_ref, dv_ref, i, frm, to, ln)
 
 
-def four_kernel(stride, count, z0, z1, z3, z2, dec_t_ref, s_ref, r_ref, *refs):
-    combine_kernel(stride, 4, count, False, z0, z1, z2, z3, dec_t_ref, s_ref, r_ref, *refs[-3:])
-
-
-def combine_kernel(stride, radix, count, last, *refs):
-    parts = refs[:radix]
-    dec_t_ref, s_ref, r_ref, z_ref, s_out, r_out = refs[radix : radix + 6]
-    dec_t = dec_t_ref[...]
+def combine(stride, count, parts, dec_t, s, r):
     modes = dec_t.shape[0]
-    digit, offset = place(stride, radix)
+    digit, offset = place(stride, 4)
     offset = offset.astype(F32)
 
     def gather(i, n=modes):
-        have = [part[pl.ds(i * modes, n), :].astype(F32) for part in parts]
+        have = [parts(k, i, n) for k in range(4)]
         pick = []
-        for j in range(radix):
+        for j in range(4):
             k = digit ^ j
-            first = jnp.where(k == 0, have[0], have[1])
-            if radix == 4:
-                first = jnp.where(k >= 2, jnp.where(k == 2, have[2], have[3]), first)
-            pick.append(first)
+            pick.append(jnp.where(k >= 2, jnp.where(k == 2, have[2], have[3]), jnp.where(k == 0, have[0], have[1])))
         return pick
 
     e, f, g, h, p, d = (gather(i) for i in range(6))
     k = gather(6, 8)
     one = dec_t * float(count * stride)
-    w = [jnp.exp(one * (-float(j))) for j in range(radix)]
+    w = [jnp.exp(one * (-float(j))) for j in range(4)]
     e_t, f_t, g_t, h_t, p_t, d_t, k_t = e[0], f[0], g[0], h[0], p[0], d[0], k[0]
     enter = jnp.zeros_like(dec_t)
-    for j in range(1, radix):
+    for j in range(1, 4):
         enter = jnp.where(digit == j, e_t, enter)
         p_t = p_t + p[j] + e_t * g[j]
         d_t = d_t + d[j] + f_t * g[j] + e_t * h[j]
@@ -314,27 +307,31 @@
         g_t = g_t + w[j] * g[j]
         k_t = k_t + k[j]
     leave = jnp.zeros_like(dec_t)
-    tail = g[-1]
-    for j in range(radix - 2, -1, -1):
+    tail = g[3]
+    for j in range(2, -1, -1):
         leave = jnp.where(digit == j, tail, leave)
         tail = g[j] + w[1] * tail
-    s_out[...] = s_ref[...] + jnp.exp(dec_t * (-float(count) * offset)) * enter
-    r_out[...] = r_ref[...] + jnp.exp(dec_t * (-float(count) * (float(stride - 1) - offset))) * leave
-    block = [x.astype(BF16) for x in (e_t, f_t, g_t, h_t, p_t, d_t, k_t)]
+    s = s + jnp.exp(dec_t * (-float(count) * offset)) * enter
+    r = r + jnp.exp(dec_t * (-float(count) * (float(stride - 1) - offset))) * leave
+    return (e_t, f_t, g_t, h_t, p_t, d_t, k_t), s, r
+
+
+def combine_kernel(stride, count, z0, z2, z3, z1, dec_t_ref, s_ref, r_ref, *refs):
+    z_ref, s_out, r_out = refs[-3:]
+    modes = dec_t_ref.shape[0]
+
+    def parts(k, i, n):
+        return (z0, z1, z2, z3)[k][pl.ds(i * modes, n), :].astype(F32)
+
+    block, s_out[...], r_out[...] = combine(stride, count, parts, dec_t_ref[...], s_ref[...], r_ref[...])
     for i, part in enumerate(block):
-        z_ref[pl.ds(i * modes, part.shape[0]), :] = part
-    if last:
-        side = place(stride * radix, 2)[0] == 1
-        send = refs[radix + 6]
-        send[pl.ds(0, modes), :] = jnp.where(side, block[2].astype(F32), block[0].astype(F32)).astype(BF16)
-        send[pl.ds(modes, modes), :] = jnp.where(side, block[3].astype(F32), block[1].astype(F32)).astype(BF16)
-        for i, part in enumerate(block[4:]):
-            send[pl.ds((2 + i) * modes, part.shape[0]), :] = part
+        z_ref[pl.ds(i * modes, part.shape[0]), :] = part.astype(BF16)
 
 
 def finish_kernel(
-    stride,
-    own_ref, got_ref, roots_ref, ratio_ref, in_ref, out_ref, far_ref, w_ref, fwd_ref, bwd_ref,
+    stride, count,
+    own_ref, pair_ref, far_ref, near_ref, dec_t_ref, s_ref, r_ref, s_known, r_known,
+    roots_ref, ratio_ref, in_ref, out_ref, w_ref, fwd_ref, bwd_ref,
     k_ref, v_ref, u_ref, dq_old, dk_old, dv_old,
     dq_hbm, dk_hbm, dv_hbm, dres_hbm, ddec_hbm, dskip_hbm,
     dq_ref, dk_ref, dv_ref, dres_ref, ddec_ref, dskip_ref, total_ref, c_ref, sems,
@@ -343,7 +340,7 @@
     modes = w_ref.shape[0]
     steps = rows // SEGS
     tiles = width // LANES
-    right = place(stride, 2)[0] == 1
+    right = place(2 * stride, 2)[0] == 1
     outs = ((dq_old, dq_ref, dq_hbm), (dk_old, dk_ref, dk_hbm), (dv_old, dv_ref, dv_hbm))
 
     @pl.when(right)
@@ -354,19 +351,15 @@
     def _():
         fetch(sems, *[(old, hbm) for old, _, hbm in outs[:1]])
 
-    def half(ref, i, n=modes):
-        return ref[pl.ds(i * modes, n), :].astype(F32)
-
-    got = half(got_ref, 0), half(got_ref, 1)
-    e_l, g_r = jnp.where(right, got[0], half(own_ref, 0)), jnp.where(right, half(own_ref, 2), got[0])
-    f_l, h_r = jnp.where(right, got[1], half(own_ref, 1)), jnp.where(right, half(own_ref, 3), got[1])
-    proj = half(own_ref, 4) + half(got_ref, 2) + e_l * g_r
-    diff = half(own_ref, 5) + half(got_ref, 3) + (f_l * g_r + e_l * h_r)
-    dres_ref[...] = roots_ref[...] * proj
-    ddec_ref[...] = ratio_ref[...] * diff
-    dskip_ref[...] = (half(own_ref, 6, 8) + half(got_ref, 4, 8))[:1]
+    def parts(k, i, n):
+        return (own_ref, pair_ref, far_ref, near_ref)[k][pl.ds(i * modes, n), :].astype(F32)
+
+    block, s, r = combine(stride, count, parts, dec_t_ref[...], s_ref[...], r_ref[...])
+    c_ref[...] = jnp.where(right, s - s_known[...], r - r_known[...])
+    dres_ref[...] = roots_ref[...] * block[4]
+    ddec_ref[...] = ratio_ref[...] * block[5]
+    dskip_ref[...] = block[6][:1]
     copies = fetch(sems, (dres_ref, dres_hbm), (ddec_ref, ddec_hbm), (dskip_ref, dskip_hbm), first=2)
-    c_ref[...] = got[0] * far_ref[...]
 
     def rest(work, pairs):
         for seg in range(SEGS):
@@ -454,24 +447,20 @@
     )
     s = r = jnp.zeros((modes, width), F32)
     for stride in (1, 4):
-        parts = [z] + [exchange(z, k * stride, size) for k in (1, 3, 2)]
+        parts = [z] + [exchange(z, k * stride, size) for k in (2, 3, 1)]
         z, s, r = call(
-            functools.partial(four_kernel, stride, rows),
+            functools.partial(combine_kernel, stride, rows),
             [block, state, state],
             [*parts, dec_t, s, r] + [roots] * (stride == 1),
             name=f"combine{stride}",
         )
-    z, s, r, send = call(
-        functools.partial(combine_kernel, 16, 2, rows, True),
-        [block, state, state, VMEM((4 * modes + 8, width), BF16)],
-        [z, exchange(z, 16, size), dec_t, s, r],
-        name="combine16",
-    )
-    got = exchange(send, 48, size)
-    fwd, bwd, far, w, dq, dk, dv = call(
-        functools.partial(known_kernel, 32, rows),
-        [big, big, state, state] + [local] * 3,
-        [dec_t, s, r, in_w, out_w, fwd, bwd, keys, values, upstream],
+    near = exchange(z, 48, size)
+    pair = exchange(z, 16, size)
+    far = exchange(near, 16, size)
+    fwd, bwd, s_known, r_known, w, dq, dk, dv = call(
+        functools.partial(known_kernel, 16, rows),
+        [big, big, state, state, state] + [local] * 3,
+        [pair, dec_t, s, r, in_w, out_w, fwd, bwd, keys, values, upstream],
         flops=4 * rows * width * modes,
         name="known",
     )
@@ -479,9 +468,9 @@
     outs += [jax.ShapeDtypeStruct((modes, width), F32)] * 2
     outs += [jax.ShapeDtypeStruct((1, width), F32)]
     dq, dk, dv, dres, ddec, dskip = call(
-        functools.partial(finish_kernel, 32),
+        functools.partial(finish_kernel, 16, rows),
         outs,
-        [z, got, roots, ratio, in_w, out_w, far, w, fwd, bwd, keys, values, upstream, dq, dk, dv],
+        [z, pair, far, near, dec_t, s, r, s_known, r_known, roots, ratio, in_w, out_w, w, fwd, bwd, keys, values, upstream, dq, dk, dv],
         [local] * 3 + [state] * 2 + [VMEM((1, width), F32), big, state, pltpu.SemaphoreType.DMA((7,))],
         name="finish",
         out_space=pltpu.HBM,

time: 35.5 us -> 35.2 us (level)
  starting transfers between devices: 17.7 us -> 17 us
  waiting for transfers between devices: 10.2 us -> 10.6 us
    ppermute x8 -> x9, starting transfers between devices: 17.7 us -> 17 us  [exchange(): return lax.ppermute(array, 'seq', [(i, i ^ mask) for i in range(size)])]
    ppermute x8 -> x9, waiting for transfers between devices: 10.2 us -> 10.6 us  [exchange(): return lax.ppermute(array, 'seq', [(i, i ^ mask) for i in range(size)])]
    pallas_call x7 -> x6, Pallas kernels: 6.62 us -> 6.65 us  [call(): pl.pallas_call(kernel, out_shape=outs, in_specs=[pl.BlockSpec(memory_spac...]
  transfers between devices with their start and end apart: 8 -> 9, of which waited for: 5 -> 6; matrix products, arithmetic and copies ran while one was open for 0% -> 0% of each run, Pallas kernels for 8% -> 8%
where the time goes in v6:
time: 35.2 us; the launch traced here: 34.9 us
  starting transfers between devices  17 us (48%)
  waiting for transfers between devices  10.6 us (30%)
  Pallas kernels  6.65 us (19%)
  between operations  0.68 us (2%)
    ppermute x9, starting transfers between devices, exchange(): return lax.ppermute(array, 'seq', [(i, i ^ mask) for i in range(size)])  17 us
    ppermute x9, waiting for transfers between devices, exchange(): return lax.ppermute(array, 'seq', [(i, i ^ mask) for i in range(size)])  10.6 us
    pallas_call x6, Pallas kernels, call(): pl.pallas_call(kernel, out_shape=outs, in_specs=[pl.BlockSpec(memory_spac...  6.65 us
  transfers between devices with their start and end apart: 9, of which 6 were waited for; matrix products, arithmetic and copies ran while one was open for 0% of the time, Pallas kernels for 8%

profile of v6, /device:TPU:32, one launch (start us, length us, event | category | flops | bytes accessed | tf_op | source)
XLA Modules:
  0.0 34.9 jit_solution(492364838573184218)
XLA Ops:
  0.6 2.5 %summary.1 = (bf16[104,256]{1,0:T(8,128)(2,1)S(1)}, f32[2,256,128]{2,1,0:T(8,128)S(1)}, f32[2,256,128]{2,1,0:T(8,128)S(1)}, f32[2,128,128]{2,1,0:T(8,128)S(1)}, ...) custom-call(f32[16,256]{1,0:T(8,128)} %bitcast.6, ...), custom_call_target="tpu_custom_call" | custom-call | flops 12582912 | bytes 524288 | tf_op jit(solution)/shard_map/summary/pallas_call | solution.py:402
  3.1 3.1 %collective-permute-start = (bf16[104,256]{1,0:T(8,128)(2,1)S(1)}, bf16[104,256]{1,0:T(8,128)(2,1)S(1)}, u32[]{:S(2)}, u32[]{:S(2)}) collective-permute-start(bf16[104,256]{1,0:T(8,128)(2,1)S(1)} %get-tuple-element.41.z0), channel_id=1, source_target_pairs={{0,8},{4,12},{8,0},{12,4},{16,24},{20,28},{24,16},{28,20},{32,40},... | collective-permute-start | bytes 159752 | tf_op jit(solution)/shard_map/ppermute | solution.py:415
  6.2 1.1 %collective-permute-start.1 = (bf16[104,256]{1,0:T(8,128)(2,1)S(1)}, bf16[104,256]{1,0:T(8,128)(2,1)S(1)}, u32[]{:S(2)}, u32[]{:S(2)}) collective-permute-start(bf16[104,256]{1,0:T(8,128)(2,1)S(1)} %get-tuple-element.41.z0), channel_id=1, source_target_pairs={{0,12},{4,8},{8,4},{12,0},{16,28},{20,24},{24,20},{28,16},{32,44},... | collective-permute-start | bytes 159752 | tf_op jit(solution)/shard_map/ppermute | solution.py:415
  7.4 0.0 collective-permute-start.2
  7.4 1.9 %conv.1 = (f32[2,256,128]{2,1,0:T(8,128)S(1)}, f32[2,256,128]{2,1,0:T(8,128)S(1)}, f32[2,128,128]{2,1,0:T(8,128)S(1)}, f32[2,128,128]{2,1,0:T(8,128)S(1)}, f32[16,256]{1,0:T(8,128)S(1)}, /*index=5*/f32[16,256]{1,0:T(8,128)S(1)}) custom-call(f32[16,256]{1,0:T(8,128)} %bitcast.7, f32[1,256]{1,0:T(1,128)} %bitcast.8, ...), custom_call_target="tpu_custom_call" | custom-call | flops 8388608 | bytes 524288 | tf_op jit(solution)/shard_map/conv/pallas_call | solution.py:402
  9.3 0.0 collective-permute-done.z2
  9.3 2.3 %collective-permute-done.1.z3 = bf16[104,256]{1,0:T(8,128)(2,1)S(1)} collective-permute-done((bf16[104,256]{1,0:T(8,128)(2,1)S(1)}, bf16[104,256]{1,0:T(8,128)(2,1)S(1)}, u32[]{:S(2)}, u32[]{:S(2)}) %collective-permute-start.1) | collective-permute-done | bytes 53280 | tf_op jit(solution)/shard_map/ppermute | solution.py:415
  11.6 0.0 collective-permute-done.2.z1
  11.6 0.1 combine1.1
  11.7 3.3 %collective-permute-start.3 = (bf16[104,256]{1,0:T(8,128)(2,1)S(1)}, bf16[104,256]{1,0:T(8,128)(2,1)S(1)}, u32[]{:S(2)}, u32[]{:S(2)}) collective-permute-start(bf16[104,256]{1,0:T(8,128)(2,1)S(1)} %get-tuple-element.48.z0), channel_id=1, source_target_pairs={{0,32},{4,36},{8,40},{12,44},{16,48},{20,52},{24,56},{28,60},{32,0... | collective-permute-start | bytes 159752 | tf_op jit(solution)/shard_map/ppermute | solution.py:415
  15.0 1.1 %collective-permute-start.4 = (bf16[104,256]{1,0:T(8,128)(2,1)S(1)}, bf16[104,256]{1,0:T(8,128)(2,1)S(1)}, u32[]{:S(2)}, u32[]{:S(2)}) collective-permute-start(bf16[104,256]{1,0:T(8,128)(2,1)S(1)} %get-tuple-element.48.z0), channel_id=1, source_target_pairs={{0,48},{4,52},{8,56},{12,60},{16,32},{20,36},{24,40},{28,44},{32,1... | collective-permute-start | bytes 159752 | tf_op jit(solution)/shard_map/ppermute | solution.py:415
  16.1 0.0 collective-permute-start.5
  16.1 1.4 %collective-permute-done.3.z2 = bf16[104,256]{1,0:T(8,128)(2,1)S(1)} collective-permute-done((bf16[104,256]{1,0:T(8,128)(2,1)S(1)}, bf16[104,256]{1,0:T(8,128)(2,1)S(1)}, u32[]{:S(2)}, u32[]{:S(2)}) %collective-permute-start.3) | collective-permute-done | bytes 53280 | tf_op jit(solution)/shard_map/ppermute | solution.py:415
  17.5 2.8 %collective-permute-done.4.z3 = bf16[104,256]{1,0:T(8,128)(2,1)S(1)} collective-permute-done((bf16[104,256]{1,0:T(8,128)(2,1)S(1)}, bf16[104,256]{1,0:T(8,128)(2,1)S(1)}, u32[]{:S(2)}, u32[]{:S(2)}) %collective-permute-start.4) | collective-permute-done | bytes 53280 | tf_op jit(solution)/shard_map/ppermute | solution.py:415
  20.4 0.0 collective-permute-done.5.z1
  20.4 0.1 combine4.1
  20.5 5.5 %collective-permute-start.7 = (bf16[104,256]{1,0:T(8,128)(2,1)S(1)}, bf16[104,256]{1,0:T(8,128)(2,1)S(1)}, u32[]{:S(2)}, u32[]{:S(2)}) collective-permute-start(bf16[104,256]{1,0:T(8,128)(2,1)S(1)} %get-tuple-element.51.own_ref), channel_id=1, source_target_pairs={{0,192},{4,196},{8,200},{12,204},{16,208},{20,212},{24,216},{28,22... | collective-permute-start | bytes 159752 | tf_op jit(solution)/shard_map/ppermute | solution.py:415
  26.0 1.5 %collective-permute-start.6 = (bf16[104,256]{1,0:T(8,128)(2,1)S(1)}, bf16[104,256]{1,0:T(8,128)(2,1)S(1)}, u32[]{:S(2)}, u32[]{:S(2)}) collective-permute-start(bf16[104,256]{1,0:T(8,128)(2,1)S(1)} %get-tuple-element.51.own_ref), channel_id=1, source_target_pairs={{0,64},{4,68},{8,72},{12,76},{16,80},{20,84},{24,88},{28,92},{32,9... | collective-permute-start | bytes 159752 | tf_op jit(solution)/shard_map/ppermute | solution.py:415
  27.4 1.2 %collective-permute-done.7.near_ref = bf16[104,256]{1,0:T(8,128)(2,1)S(1)} collective-permute-done((bf16[104,256]{1,0:T(8,128)(2,1)S(1)}, bf16[104,256]{1,0:T(8,128)(2,1)S(1)}, u32[]{:S(2)}, u32[]{:S(2)}) %collective-permute-start.7) | collective-permute-done | bytes 53280 | tf_op jit(solution)/shard_map/ppermute | solution.py:415
  28.7 1.4 %collective-permute-start.8 = (bf16[104,256]{1,0:T(8,128)(2,1)S(1)}, bf16[104,256]{1,0:T(8,128)(2,1)S(1)}, u32[]{:S(2)}, u32[]{:S(2)}) collective-permute-start(bf16[104,256]{1,0:T(8,128)(2,1)S(1)} %collective-permute-done.7.near_ref), channel_id=1, source_target_pairs={{0,64},{4,68},{8,72},{12,76},{16,80},{20,84},{24,88},{28,92},{32,9... | collective-permute-start | bytes 159752 | tf_op jit(solution)/shard_map/ppermute | solution.py:415
  30.1 1.0 %collective-permute-done.6.pair_ref = bf16[104,256]{1,0:T(8,128)(2,1)S(1)} collective-permute-done((bf16[104,256]{1,0:T(8,128)(2,1)S(1)}, bf16[104,256]{1,0:T(8,128)(2,1)S(1)}, u32[]{:S(2)}, u32[]{:S(2)}) %collective-permute-start.6) | collective-permute-done | bytes 53280 | tf_op jit(solution)/shard_map/ppermute | solution.py:415
  31.1 0.8 %known.1 = (f32[2,256,128]{2,1,0:T(8,128)S(1)}, f32[2,256,128]{2,1,0:T(8,128)S(1)}, f32[16,256]{1,0:T(8,128)S(1)}, f32[16,256]{1,0:T(8,128)S(1)}, f32[16,256]{1,...) custom-call(bf16[104,256]{1,0:T(8,128)(2,1)S(1)} %collective-permute-done.6, ...), custom_call_target="tpu_custom_call" | custom-call | flops 4194304 | bytes 524288 | tf_op jit(solution)/shard_map/known/pallas_call | solution.py:402
  31.9 1.8 %collective-permute-done.8.far_ref = bf16[104,256]{1,0:T(8,128)(2,1)S(1)} collective-permute-done((bf16[104,256]{1,0:T(8,128)(2,1)S(1)}, bf16[104,256]{1,0:T(8,128)(2,1)S(1)}, u32[]{:S(2)}, u32[]{:S(2)}) %collective-permute-start.8) | collective-permute-done | bytes 53280 | tf_op jit(solution)/shard_map/ppermute | solution.py:415
  33.7 1.2 %finish.1 = (bf16[256,256]{1,0:T(8,128)(2,1)}, bf16[256,256]{1,0:T(8,128)(2,1)}, bf16[256,256]{1,0:T(8,128)(2,1)}, f32[16,256]{1,0:T(8,128)}, f32[16,256]{1,0:T(8,128)}, /*index=5*/f32[1,256]{1,0:T(1,128)}) custom-call(bf16[104,256]{1,0:T(8,128)(2,1)S(1)} %get-tuple-element.51.own_ref, bf16[104,256]{1,0:T(8,128)(2,1)S(1)} %collective-permute-done.6.pair_ref, ...), custom_call_target="tpu_custom_call" | custom-call | bytes 524288 | tf_op jit(solution)/shard_map/finish/pallas_call | solution.py:402
  (1 shorter events, 0.0 us)
Async XLA Ops:
  3.1 6.2 %collective-permute-start = (bf16[104,256]{1,0:T(8,128)(2,1)S(1)}, bf16[104,256]{1,0:T(8,128)(2,1)S(1)}, u32[]{:S(2)}, u32[]{:S(2)}) collective-permute-start(bf16[104,256]{1,0:T(8,128)(2,1)S(1)} %get-tuple-element.41.z0), channel_id=1, source_target_pairs={{0,8},{4,12},{8,0},{12,4},{16,24},{20,28},{24,16},{28,20},{32,40},... | collective-permute-start | bytes 159752 | tf_op jit(solution)/shard_map/ppermute | solution.py:415
  6.2 5.3 %collective-permute-start.1 = (bf16[104,256]{1,0:T(8,128)(2,1)S(1)}, bf16[104,256]{1,0:T(8,128)(2,1)S(1)}, u32[]{:S(2)}, u32[]{:S(2)}) collective-permute-start(bf16[104,256]{1,0:T(8,128)(2,1)S(1)} %get-tuple-element.41.z0), channel_id=1, source_target_pairs={{0,12},{4,8},{8,4},{12,0},{16,28},{20,24},{24,20},{28,16},{32,44},... | collective-permute-start | bytes 159752 | tf_op jit(solution)/shard_map/ppermute | solution.py:415
  7.4 4.2 %collective-permute-start.2 = (bf16[104,256]{1,0:T(8,128)(2,1)S(1)}, bf16[104,256]{1,0:T(8,128)(2,1)S(1)}, u32[]{:S(2)}, u32[]{:S(2)}) collective-permute-start(bf16[104,256]{1,0:T(8,128)(2,1)S(1)} %get-tuple-element.41.z0), channel_id=1, source_target_pairs={{0,4},{4,0},{8,12},{12,8},{16,20},{20,16},{24,28},{28,24},{32,36},... | collective-permute-start | bytes 159752 | tf_op jit(solution)/shard_map/ppermute | solution.py:415
  11.7 5.8 %collective-permute-start.3 = (bf16[104,256]{1,0:T(8,128)(2,1)S(1)}, bf16[104,256]{1,0:T(8,128)(2,1)S(1)}, u32[]{:S(2)}, u32[]{:S(2)}) collective-permute-start(bf16[104,256]{1,0:T(8,128)(2,1)S(1)} %get-tuple-element.48.z0), channel_id=1, source_target_pairs={{0,32},{4,36},{8,40},{12,44},{16,48},{20,52},{24,56},{28,60},{32,0... | collective-permute-start | bytes 159752 | tf_op jit(solution)/shard_map/ppermute | solution.py:415
  15.0 5.3 %collective-permute-start.4 = (bf16[104,256]{1,0:T(8,128)(2,1)S(1)}, bf16[104,256]{1,0:T(8,128)(2,1)S(1)}, u32[]{:S(2)}, u32[]{:S(2)}) collective-permute-start(bf16[104,256]{1,0:T(8,128)(2,1)S(1)} %get-tuple-element.48.z0), channel_id=1, source_target_pairs={{0,48},{4,52},{8,56},{12,60},{16,32},{20,36},{24,40},{28,44},{32,1... | collective-permute-start | bytes 159752 | tf_op jit(solution)/shard_map/ppermute | solution.py:415
  16.1 4.3 %collective-permute-start.5 = (bf16[104,256]{1,0:T(8,128)(2,1)S(1)}, bf16[104,256]{1,0:T(8,128)(2,1)S(1)}, u32[]{:S(2)}, u32[]{:S(2)}) collective-permute-start(bf16[104,256]{1,0:T(8,128)(2,1)S(1)} %get-tuple-element.48.z0), channel_id=1, source_target_pairs={{0,16},{4,20},{8,24},{12,28},{16,0},{20,4},{24,8},{28,12},{32,48},... | collective-permute-start | bytes 159752 | tf_op jit(solution)/shard_map/ppermute | solution.py:415
  20.5 8.2 %collective-permute-start.7 = (bf16[104,256]{1,0:T(8,128)(2,1)S(1)}, bf16[104,256]{1,0:T(8,128)(2,1)S(1)}, u32[]{:S(2)}, u32[]{:S(2)}) collective-permute-start(bf16[104,256]{1,0:T(8,128)(2,1)S(1)} %get-tuple-element.51.own_ref), channel_id=1, source_target_pairs={{0,192},{4,196},{8,200},{12,204},{16,208},{20,212},{24,216},{28,22... | collective-permute-start | bytes 159752 | tf_op jit(solution)/shard_map/ppermute | solution.py:415
  26.0 5.1 %collective-permute-start.6 = (bf16[104,256]{1,0:T(8,128)(2,1)S(1)}, bf16[104,256]{1,0:T(8,128)(2,1)S(1)}, u32[]{:S(2)}, u32[]{:S(2)}) collective-permute-start(bf16[104,256]{1,0:T(8,128)(2,1)S(1)} %get-tuple-element.51.own_ref), channel_id=1, source_target_pairs={{0,64},{4,68},{8,72},{12,76},{16,80},{20,84},{24,88},{28,92},{32,9... | collective-permute-start | bytes 159752 | tf_op jit(solution)/shard_map/ppermute | solution.py:415
  28.7 5.0 %collective-permute-start.8 = (bf16[104,256]{1,0:T(8,128)(2,1)S(1)}, bf16[104,256]{1,0:T(8,128)(2,1)S(1)}, u32[]{:S(2)}, u32[]{:S(2)}) collective-permute-start(bf16[104,256]{1,0:T(8,128)(2,1)S(1)} %collective-permute-done.7.near_ref), channel_id=1, source_target_pairs={{0,64},{4,68},{8,72},{12,76},{16,80},{20,84},{24,88},{28,92},{32,9... | collective-permute-start | bytes 159752 | tf_op jit(solution)/shard_map/ppermute | solution.py:415

commit v7 on v6

--- a/solution.py
+++ b/solution.py
@@ -282,19 +282,21 @@
     modes = dec_t.shape[0]
     digit, offset = place(stride, 4)
     offset = offset.astype(F32)
+    odd, high = lax.rem(digit, 2) == 1, digit >= 2
 
     def gather(i, n=modes):
-        have = [parts(k, i, n) for k in range(4)]
-        pick = []
-        for j in range(4):
-            k = digit ^ j
-            pick.append(jnp.where(k >= 2, jnp.where(k == 2, have[2], have[3]), jnp.where(k == 0, have[0], have[1])))
-        return pick
+        a, b, c, d = (parts(k, i, n) for k in range(4))
+        a, b = lax.select(odd, b, a), lax.select(odd, a, b)
+        c, d = lax.select(odd, d, c), lax.select(odd, c, d)
+        a, c = lax.select(high, c, a), lax.select(high, a, c)
+        b, d = lax.select(high, d, b), lax.select(high, b, d)
+        return [x.astype(F32) for x in (a, b, c, d)]
 
     e, f, g, h, p, d = (gather(i) for i in range(6))
     k = gather(6, 8)
     one = dec_t * float(count * stride)
-    w = [jnp.exp(one * (-float(j))) for j in range(4)]
+    w = [None, jnp.exp(-one)]
+    w += [w[1] * w[1], w[1] * w[1] * w[1]]
     e_t, f_t, g_t, h_t, p_t, d_t, k_t = e[0], f[0], g[0], h[0], p[0], d[0], k[0]
     enter = jnp.zeros_like(dec_t)
     for j in range(1, 4):
@@ -321,7 +323,7 @@
     modes = dec_t_ref.shape[0]
 
     def parts(k, i, n):
-        return (z0, z1, z2, z3)[k][pl.ds(i * modes, n), :].astype(F32)
+        return (z0, z1, z2, z3)[k][pl.ds(i * modes, n), :]
 
     block, s_out[...], r_out[...] = combine(stride, count, parts, dec_t_ref[...], s_ref[...], r_ref[...])
     for i, part in enumerate(block):
@@ -352,7 +354,7 @@
         fetch(sems, *[(old, hbm) for old, _, hbm in outs[:1]])
 
     def parts(k, i, n):
-        return (own_ref, pair_ref, far_ref, near_ref)[k][pl.ds(i * modes, n), :].astype(F32)
+        return (own_ref, pair_ref, far_ref, near_ref)[k][pl.ds(i * modes, n), :]
 
     block, s, r = combine(stride, count, parts, dec_t_ref[...], s_ref[...], r_ref[...])
     c_ref[...] = jnp.where(right, s - s_known[...], r - r_known[...])

time: 35.2 us -> 35.1 us (level)
  no operation moved by 1% of the time
where the time goes in v7:
time: 35.1 us; the launch traced here: 34.9 us
  starting transfers between devices  17 us (48%)
  waiting for transfers between devices  10.6 us (30%)
  Pallas kernels  6.58 us (19%)
  between operations  0.69 us (2%)
    ppermute x9, starting transfers between devices, exchange(): return lax.ppermute(array, 'seq', [(i, i ^ mask) for i in range(size)])  17 us
    ppermute x9, waiting for transfers between devices, exchange(): return lax.ppermute(array, 'seq', [(i, i ^ mask) for i in range(size)])  10.6 us
    pallas_call x6, Pallas kernels, call(): pl.pallas_call(kernel, out_shape=outs, in_specs=[pl.BlockSpec(memory_spac...  6.58 us
  transfers between devices with their start and end apart: 9, of which 6 were waited for; matrix products, arithmetic and copies ran while one was open for 0% of the time, Pallas kernels for 8%

profile of v7, /device:TPU:32, one launch (start us, length us, event | category | flops | bytes accessed | tf_op | source)
XLA Modules:
  0.0 34.9 jit_solution(18359878556716721801)
XLA Ops:
  0.6 2.5 %summary.1 = (bf16[104,256]{1,0:T(8,128)(2,1)S(1)}, f32[2,256,128]{2,1,0:T(8,128)S(1)}, f32[2,256,128]{2,1,0:T(8,128)S(1)}, f32[2,128,128]{2,1,0:T(8,128)S(1)}, ...) custom-call(f32[16,256]{1,0:T(8,128)} %bitcast.6, ...), custom_call_target="tpu_custom_call" | custom-call | flops 12582912 | bytes 524288 | tf_op jit(solution)/shard_map/summary/pallas_call | solution.py:404
  3.1 3.1 %collective-permute-start = (bf16[104,256]{1,0:T(8,128)(2,1)S(1)}, bf16[104,256]{1,0:T(8,128)(2,1)S(1)}, u32[]{:S(2)}, u32[]{:S(2)}) collective-permute-start(bf16[104,256]{1,0:T(8,128)(2,1)S(1)} %get-tuple-element.41.z0), channel_id=1, source_target_pairs={{0,8},{4,12},{8,0},{12,4},{16,24},{20,28},{24,16},{28,20},{32,40},... | collective-permute-start | bytes 159752 | tf_op jit(solution)/shard_map/ppermute | solution.py:417
  6.2 1.1 %collective-permute-start.1 = (bf16[104,256]{1,0:T(8,128)(2,1)S(1)}, bf16[104,256]{1,0:T(8,128)(2,1)S(1)}, u32[]{:S(2)}, u32[]{:S(2)}) collective-permute-start(bf16[104,256]{1,0:T(8,128)(2,1)S(1)} %get-tuple-element.41.z0), channel_id=1, source_target_pairs={{0,12},{4,8},{8,4},{12,0},{16,28},{20,24},{24,20},{28,16},{32,44},... | collective-permute-start | bytes 159752 | tf_op jit(solution)/shard_map/ppermute | solution.py:417
  7.4 0.0 collective-permute-start.2
  7.4 1.9 %conv.1 = (f32[2,256,128]{2,1,0:T(8,128)S(1)}, f32[2,256,128]{2,1,0:T(8,128)S(1)}, f32[2,128,128]{2,1,0:T(8,128)S(1)}, f32[2,128,128]{2,1,0:T(8,128)S(1)}, f32[16,256]{1,0:T(8,128)S(1)}, /*index=5*/f32[16,256]{1,0:T(8,128)S(1)}) custom-call(f32[16,256]{1,0:T(8,128)} %bitcast.7, f32[1,256]{1,0:T(1,128)} %bitcast.8, ...), custom_call_target="tpu_custom_call" | custom-call | flops 8388608 | bytes 524288 | tf_op jit(solution)/shard_map/conv/pallas_call | solution.py:404
  9.3 0.0 collective-permute-done.z2
  9.3 2.3 %collective-permute-done.1.z3 = bf16[104,256]{1,0:T(8,128)(2,1)S(1)} collective-permute-done((bf16[104,256]{1,0:T(8,128)(2,1)S(1)}, bf16[104,256]{1,0:T(8,128)(2,1)S(1)}, u32[]{:S(2)}, u32[]{:S(2)}) %collective-permute-start.1) | collective-permute-done | bytes 53280 | tf_op jit(solution)/shard_map/ppermute | solution.py:417
  11.6 0.0 collective-permute-done.2.z1
  11.6 0.1 combine1.1
  11.7 3.3 %collective-permute-start.3 = (bf16[104,256]{1,0:T(8,128)(2,1)S(1)}, bf16[104,256]{1,0:T(8,128)(2,1)S(1)}, u32[]{:S(2)}, u32[]{:S(2)}) collective-permute-start(bf16[104,256]{1,0:T(8,128)(2,1)S(1)} %get-tuple-element.48.z0), channel_id=1, source_target_pairs={{0,32},{4,36},{8,40},{12,44},{16,48},{20,52},{24,56},{28,60},{32,0... | collective-permute-start | bytes 159752 | tf_op jit(solution)/shard_map/ppermute | solution.py:417
  15.0 1.1 %collective-permute-start.4 = (bf16[104,256]{1,0:T(8,128)(2,1)S(1)}, bf16[104,256]{1,0:T(8,128)(2,1)S(1)}, u32[]{:S(2)}, u32[]{:S(2)}) collective-permute-start(bf16[104,256]{1,0:T(8,128)(2,1)S(1)} %get-tuple-element.48.z0), channel_id=1, source_target_pairs={{0,48},{4,52},{8,56},{12,60},{16,32},{20,36},{24,40},{28,44},{32,1... | collective-permute-start | bytes 159752 | tf_op jit(solution)/shard_map/ppermute | solution.py:417
  16.0 0.0 collective-permute-start.5
  16.0 1.4 %collective-permute-done.3.z2 = bf16[104,256]{1,0:T(8,128)(2,1)S(1)} collective-permute-done((bf16[104,256]{1,0:T(8,128)(2,1)S(1)}, bf16[104,256]{1,0:T(8,128)(2,1)S(1)}, u32[]{:S(2)}, u32[]{:S(2)}) %collective-permute-start.3) | collective-permute-done | bytes 53280 | tf_op jit(solution)/shard_map/ppermute | solution.py:417
  17.5 2.8 %collective-permute-done.4.z3 = bf16[104,256]{1,0:T(8,128)(2,1)S(1)} collective-permute-done((bf16[104,256]{1,0:T(8,128)(2,1)S(1)}, bf16[104,256]{1,0:T(8,128)(2,1)S(1)}, u32[]{:S(2)}, u32[]{:S(2)}) %collective-permute-start.4) | collective-permute-done | bytes 53280 | tf_op jit(solution)/shard_map/ppermute | solution.py:417
  20.3 0.0 collective-permute-done.5.z1
  20.3 0.1 combine4.1
  20.4 5.5 %collective-permute-start.7 = (bf16[104,256]{1,0:T(8,128)(2,1)S(1)}, bf16[104,256]{1,0:T(8,128)(2,1)S(1)}, u32[]{:S(2)}, u32[]{:S(2)}) collective-permute-start(bf16[104,256]{1,0:T(8,128)(2,1)S(1)} %get-tuple-element.51.own_ref), channel_id=1, source_target_pairs={{0,192},{4,196},{8,200},{12,204},{16,208},{20,212},{24,216},{28,22... | collective-permute-start | bytes 159752 | tf_op jit(solution)/shard_map/ppermute | solution.py:417
  25.9 1.5 %collective-permute-start.6 = (bf16[104,256]{1,0:T(8,128)(2,1)S(1)}, bf16[104,256]{1,0:T(8,128)(2,1)S(1)}, u32[]{:S(2)}, u32[]{:S(2)}) collective-permute-start(bf16[104,256]{1,0:T(8,128)(2,1)S(1)} %get-tuple-element.51.own_ref), channel_id=1, source_target_pairs={{0,64},{4,68},{8,72},{12,76},{16,80},{20,84},{24,88},{28,92},{32,9... | collective-permute-start | bytes 159752 | tf_op jit(solution)/shard_map/ppermute | solution.py:417
  27.4 1.2 %collective-permute-done.7.near_ref = bf16[104,256]{1,0:T(8,128)(2,1)S(1)} collective-permute-done((bf16[104,256]{1,0:T(8,128)(2,1)S(1)}, bf16[104,256]{1,0:T(8,128)(2,1)S(1)}, u32[]{:S(2)}, u32[]{:S(2)}) %collective-permute-start.7) | collective-permute-done | bytes 53280 | tf_op jit(solution)/shard_map/ppermute | solution.py:417
  28.6 1.4 %collective-permute-start.8 = (bf16[104,256]{1,0:T(8,128)(2,1)S(1)}, bf16[104,256]{1,0:T(8,128)(2,1)S(1)}, u32[]{:S(2)}, u32[]{:S(2)}) collective-permute-start(bf16[104,256]{1,0:T(8,128)(2,1)S(1)} %collective-permute-done.7.near_ref), channel_id=1, source_target_pairs={{0,64},{4,68},{8,72},{12,76},{16,80},{20,84},{24,88},{28,92},{32,9... | collective-permute-start | bytes 159752 | tf_op jit(solution)/shard_map/ppermute | solution.py:417
  30.0 1.0 %collective-permute-done.6.pair_ref = bf16[104,256]{1,0:T(8,128)(2,1)S(1)} collective-permute-done((bf16[104,256]{1,0:T(8,128)(2,1)S(1)}, bf16[104,256]{1,0:T(8,128)(2,1)S(1)}, u32[]{:S(2)}, u32[]{:S(2)}) %collective-permute-start.6) | collective-permute-done | bytes 53280 | tf_op jit(solution)/shard_map/ppermute | solution.py:417
  31.1 0.8 %known.1 = (f32[2,256,128]{2,1,0:T(8,128)S(1)}, f32[2,256,128]{2,1,0:T(8,128)S(1)}, f32[16,256]{1,0:T(8,128)S(1)}, f32[16,256]{1,0:T(8,128)S(1)}, f32[16,256]{1,...) custom-call(bf16[104,256]{1,0:T(8,128)(2,1)S(1)} %collective-permute-done.6, ...), custom_call_target="tpu_custom_call" | custom-call | flops 4194304 | bytes 524288 | tf_op jit(solution)/shard_map/known/pallas_call | solution.py:404
  31.8 1.8 %collective-permute-done.8.far_ref = bf16[104,256]{1,0:T(8,128)(2,1)S(1)} collective-permute-done((bf16[104,256]{1,0:T(8,128)(2,1)S(1)}, bf16[104,256]{1,0:T(8,128)(2,1)S(1)}, u32[]{:S(2)}, u32[]{:S(2)}) %collective-permute-start.8) | collective-permute-done | bytes 53280 | tf_op jit(solution)/shard_map/ppermute | solution.py:417
  33.6 1.2 %finish.1 = (bf16[256,256]{1,0:T(8,128)(2,1)}, bf16[256,256]{1,0:T(8,128)(2,1)}, bf16[256,256]{1,0:T(8,128)(2,1)}, f32[16,256]{1,0:T(8,128)}, f32[16,256]{1,0:T(8,128)}, /*index=5*/f32[1,256]{1,0:T(1,128)}) custom-call(bf16[104,256]{1,0:T(8,128)(2,1)S(1)} %get-tuple-element.51.own_ref, bf16[104,256]{1,0:T(8,128)(2,1)S(1)} %collective-permute-done.6.pair_ref, ...), custom_call_target="tpu_custom_call" | custom-call | bytes 524288 | tf_op jit(solution)/shard_map/finish/pallas_call | solution.py:404
  (1 shorter events, 0.0 us)
Async XLA Ops:
  3.1 6.2 %collective-permute-start = (bf16[104,256]{1,0:T(8,128)(2,1)S(1)}, bf16[104,256]{1,0:T(8,128)(2,1)S(1)}, u32[]{:S(2)}, u32[]{:S(2)}) collective-permute-start(bf16[104,256]{1,0:T(8,128)(2,1)S(1)} %get-tuple-element.41.z0), channel_id=1, source_target_pairs={{0,8},{4,12},{8,0},{12,4},{16,24},{20,28},{24,16},{28,20},{32,40},... | collective-permute-start | bytes 159752 | tf_op jit(solution)/shard_map/ppermute | solution.py:417
  6.2 5.3 %collective-permute-start.1 = (bf16[104,256]{1,0:T(8,128)(2,1)S(1)}, bf16[104,256]{1,0:T(8,128)(2,1)S(1)}, u32[]{:S(2)}, u32[]{:S(2)}) collective-permute-start(bf16[104,256]{1,0:T(8,128)(2,1)S(1)} %get-tuple-element.41.z0), channel_id=1, source_target_pairs={{0,12},{4,8},{8,4},{12,0},{16,28},{20,24},{24,20},{28,16},{32,44},... | collective-permute-start | bytes 159752 | tf_op jit(solution)/shard_map/ppermute | solution.py:417
  7.4 4.2 %collective-permute-start.2 = (bf16[104,256]{1,0:T(8,128)(2,1)S(1)}, bf16[104,256]{1,0:T(8,128)(2,1)S(1)}, u32[]{:S(2)}, u32[]{:S(2)}) collective-permute-start(bf16[104,256]{1,0:T(8,128)(2,1)S(1)} %get-tuple-element.41.z0), channel_id=1, source_target_pairs={{0,4},{4,0},{8,12},{12,8},{16,20},{20,16},{24,28},{28,24},{32,36},... | collective-permute-start | bytes 159752 | tf_op jit(solution)/shard_map/ppermute | solution.py:417
  11.7 5.8 %collective-permute-start.3 = (bf16[104,256]{1,0:T(8,128)(2,1)S(1)}, bf16[104,256]{1,0:T(8,128)(2,1)S(1)}, u32[]{:S(2)}, u32[]{:S(2)}) collective-permute-start(bf16[104,256]{1,0:T(8,128)(2,1)S(1)} %get-tuple-element.48.z0), channel_id=1, source_target_pairs={{0,32},{4,36},{8,40},{12,44},{16,48},{20,52},{24,56},{28,60},{32,0... | collective-permute-start | bytes 159752 | tf_op jit(solution)/shard_map/ppermute | solution.py:417
  15.0 5.3 %collective-permute-start.4 = (bf16[104,256]{1,0:T(8,128)(2,1)S(1)}, bf16[104,256]{1,0:T(8,128)(2,1)S(1)}, u32[]{:S(2)}, u32[]{:S(2)}) collective-permute-start(bf16[104,256]{1,0:T(8,128)(2,1)S(1)} %get-tuple-element.48.z0), channel_id=1, source_target_pairs={{0,48},{4,52},{8,56},{12,60},{16,32},{20,36},{24,40},{28,44},{32,1... | collective-permute-start | bytes 159752 | tf_op jit(solution)/shard_map/ppermute | solution.py:417
  16.0 4.3 %collective-permute-start.5 = (bf16[104,256]{1,0:T(8,128)(2,1)S(1)}, bf16[104,256]{1,0:T(8,128)(2,1)S(1)}, u32[]{:S(2)}, u32[]{:S(2)}) collective-permute-start(bf16[104,256]{1,0:T(8,128)(2,1)S(1)} %get-tuple-element.48.z0), channel_id=1, source_target_pairs={{0,16},{4,20},{8,24},{12,28},{16,0},{20,4},{24,8},{28,12},{32,48},... | collective-permute-start | bytes 159752 | tf_op jit(solution)/shard_map/ppermute | solution.py:417
  20.4 8.2 %collective-permute-start.7 = (bf16[104,256]{1,0:T(8,128)(2,1)S(1)}, bf16[104,256]{1,0:T(8,128)(2,1)S(1)}, u32[]{:S(2)}, u32[]{:S(2)}) collective-permute-start(bf16[104,256]{1,0:T(8,128)(2,1)S(1)} %get-tuple-element.51.own_ref), channel_id=1, source_target_pairs={{0,192},{4,196},{8,200},{12,204},{16,208},{20,212},{24,216},{28,22... | collective-permute-start | bytes 159752 | tf_op jit(solution)/shard_map/ppermute | solution.py:417
  25.9 5.1 %collective-permute-start.6 = (bf16[104,256]{1,0:T(8,128)(2,1)S(1)}, bf16[104,256]{1,0:T(8,128)(2,1)S(1)}, u32[]{:S(2)}, u32[]{:S(2)}) collective-permute-start(bf16[104,256]{1,0:T(8,128)(2,1)S(1)} %get-tuple-element.51.own_ref), channel_id=1, source_target_pairs={{0,64},{4,68},{8,72},{12,76},{16,80},{20,84},{24,88},{28,92},{32,9... | collective-permute-start | bytes 159752 | tf_op jit(solution)/shard_map/ppermute | solution.py:417
  28.6 5.0 %collective-permute-start.8 = (bf16[104,256]{1,0:T(8,128)(2,1)S(1)}, bf16[104,256]{1,0:T(8,128)(2,1)S(1)}, u32[]{:S(2)}, u32[]{:S(2)}) collective-permute-start(bf16[104,256]{1,0:T(8,128)(2,1)S(1)} %collective-permute-done.7.near_ref), channel_id=1, source_target_pairs={{0,64},{4,68},{8,72},{12,76},{16,80},{20,84},{24,88},{28,92},{32,9... | collective-permute-start | bytes 159752 | tf_op jit(solution)/shard_map/ppermute | solution.py:417

commit v8 on v7

--- a/solution.py
+++ b/solution.py
@@ -230,8 +230,8 @@
 
 
 def add_state(local_ref, total_ref, scale_ref, state_ref, w_ref, order, tiles, modes):
-    def one(i, _):
-        ln = lanes_of(i)
+    def one(i):
+        ln = pl.ds(i * LANES, LANES)
 
         def spread(ref, m):
             return jnp.broadcast_to(ref[pl.ds(m, 1), ln], (SEGS, LANES))
@@ -246,9 +246,9 @@
                 if n < len(order) - 1:
                     c[m] = c[m] * w[m]
             total_ref[i, here, :] = y
-        return 0
-
-    lax.fori_loop(0, tiles, one, 0)
+
+    for i in range(tiles):
+        one(i)
 
 
 def known_kernel(

time: 35.1 us -> 35.1 us (level)
  no operation moved by 1% of the time
where the time goes in v8:
time: 35.1 us; the launch traced here: 34.9 us
  starting transfers between devices  17 us (48%)
  waiting for transfers between devices  10.7 us (30%)
  Pallas kernels  6.56 us (19%)
  between operations  0.69 us (2%)
    ppermute x9, starting transfers between devices, exchange(): return lax.ppermute(array, 'seq', [(i, i ^ mask) for i in range(size)])  17 us
    ppermute x9, waiting for transfers between devices, exchange(): return lax.ppermute(array, 'seq', [(i, i ^ mask) for i in range(size)])  10.7 us
    pallas_call x6, Pallas kernels, call(): pl.pallas_call(kernel, out_shape=outs, in_specs=[pl.BlockSpec(memory_spac...  6.56 us
  transfers between devices with their start and end apart: 9, of which 6 were waited for; matrix products, arithmetic and copies ran while one was open for 0% of the time, Pallas kernels for 8%

profile of v8, /device:TPU:32, one launch (start us, length us, event | category | flops | bytes accessed | tf_op | source)
XLA Modules:
  0.0 34.9 jit_solution(7719858773804418652)
XLA Ops:
  0.6 2.5 %summary.1 = (bf16[104,256]{1,0:T(8,128)(2,1)S(1)}, f32[2,256,128]{2,1,0:T(8,128)S(1)}, f32[2,256,128]{2,1,0:T(8,128)S(1)}, f32[2,128,128]{2,1,0:T(8,128)S(1)}, ...) custom-call(f32[16,256]{1,0:T(8,128)} %bitcast.6, ...), custom_call_target="tpu_custom_call" | custom-call | flops 12582912 | bytes 524288 | tf_op jit(solution)/shard_map/summary/pallas_call | solution.py:404
  3.1 3.1 %collective-permute-start = (bf16[104,256]{1,0:T(8,128)(2,1)S(1)}, bf16[104,256]{1,0:T(8,128)(2,1)S(1)}, u32[]{:S(2)}, u32[]{:S(2)}) collective-permute-start(bf16[104,256]{1,0:T(8,128)(2,1)S(1)} %get-tuple-element.41.z0), channel_id=1, source_target_pairs={{0,8},{4,12},{8,0},{12,4},{16,24},{20,28},{24,16},{28,20},{32,40},... | collective-permute-start | bytes 159752 | tf_op jit(solution)/shard_map/ppermute | solution.py:417
  6.2 1.1 %collective-permute-start.1 = (bf16[104,256]{1,0:T(8,128)(2,1)S(1)}, bf16[104,256]{1,0:T(8,128)(2,1)S(1)}, u32[]{:S(2)}, u32[]{:S(2)}) collective-permute-start(bf16[104,256]{1,0:T(8,128)(2,1)S(1)} %get-tuple-element.41.z0), channel_id=1, source_target_pairs={{0,12},{4,8},{8,4},{12,0},{16,28},{20,24},{24,20},{28,16},{32,44},... | collective-permute-start | bytes 159752 | tf_op jit(solution)/shard_map/ppermute | solution.py:417
  7.4 0.0 collective-permute-start.2
  7.4 1.9 %conv.1 = (f32[2,256,128]{2,1,0:T(8,128)S(1)}, f32[2,256,128]{2,1,0:T(8,128)S(1)}, f32[2,128,128]{2,1,0:T(8,128)S(1)}, f32[2,128,128]{2,1,0:T(8,128)S(1)}, f32[16,256]{1,0:T(8,128)S(1)}, /*index=5*/f32[16,256]{1,0:T(8,128)S(1)}) custom-call(f32[16,256]{1,0:T(8,128)} %bitcast.7, f32[1,256]{1,0:T(1,128)} %bitcast.8, ...), custom_call_target="tpu_custom_call" | custom-call | flops 8388608 | bytes 524288 | tf_op jit(solution)/shard_map/conv/pallas_call | solution.py:404
  9.3 0.0 collective-permute-done.z2
  9.3 2.3 %collective-permute-done.1.z3 = bf16[104,256]{1,0:T(8,128)(2,1)S(1)} collective-permute-done((bf16[104,256]{1,0:T(8,128)(2,1)S(1)}, bf16[104,256]{1,0:T(8,128)(2,1)S(1)}, u32[]{:S(2)}, u32[]{:S(2)}) %collective-permute-start.1) | collective-permute-done | bytes 53280 | tf_op jit(solution)/shard_map/ppermute | solution.py:417
  11.6 0.0 collective-permute-done.2.z1
  11.6 0.1 combine1.1
  11.7 3.3 %collective-permute-start.3 = (bf16[104,256]{1,0:T(8,128)(2,1)S(1)}, bf16[104,256]{1,0:T(8,128)(2,1)S(1)}, u32[]{:S(2)}, u32[]{:S(2)}) collective-permute-start(bf16[104,256]{1,0:T(8,128)(2,1)S(1)} %get-tuple-element.48.z0), channel_id=1, source_target_pairs={{0,32},{4,36},{8,40},{12,44},{16,48},{20,52},{24,56},{28,60},{32,0... | collective-permute-start | bytes 159752 | tf_op jit(solution)/shard_map/ppermute | solution.py:417
  15.0 1.1 %collective-permute-start.4 = (bf16[104,256]{1,0:T(8,128)(2,1)S(1)}, bf16[104,256]{1,0:T(8,128)(2,1)S(1)}, u32[]{:S(2)}, u32[]{:S(2)}) collective-permute-start(bf16[104,256]{1,0:T(8,128)(2,1)S(1)} %get-tuple-element.48.z0), channel_id=1, source_target_pairs={{0,48},{4,52},{8,56},{12,60},{16,32},{20,36},{24,40},{28,44},{32,1... | collective-permute-start | bytes 159752 | tf_op jit(solution)/shard_map/ppermute | solution.py:417
  16.0 0.0 collective-permute-start.5
  16.0 1.4 %collective-permute-done.3.z2 = bf16[104,256]{1,0:T(8,128)(2,1)S(1)} collective-permute-done((bf16[104,256]{1,0:T(8,128)(2,1)S(1)}, bf16[104,256]{1,0:T(8,128)(2,1)S(1)}, u32[]{:S(2)}, u32[]{:S(2)}) %collective-permute-start.3) | collective-permute-done | bytes 53280 | tf_op jit(solution)/shard_map/ppermute | solution.py:417
  17.5 2.8 %collective-permute-done.4.z3 = bf16[104,256]{1,0:T(8,128)(2,1)S(1)} collective-permute-done((bf16[104,256]{1,0:T(8,128)(2,1)S(1)}, bf16[104,256]{1,0:T(8,128)(2,1)S(1)}, u32[]{:S(2)}, u32[]{:S(2)}) %collective-permute-start.4) | collective-permute-done | bytes 53280 | tf_op jit(solution)/shard_map/ppermute | solution.py:417
  20.3 0.0 collective-permute-done.5.z1
  20.3 0.1 combine4.1
  20.4 5.5 %collective-permute-start.7 = (bf16[104,256]{1,0:T(8,128)(2,1)S(1)}, bf16[104,256]{1,0:T(8,128)(2,1)S(1)}, u32[]{:S(2)}, u32[]{:S(2)}) collective-permute-start(bf16[104,256]{1,0:T(8,128)(2,1)S(1)} %get-tuple-element.51.own_ref), channel_id=1, source_target_pairs={{0,192},{4,196},{8,200},{12,204},{16,208},{20,212},{24,216},{28,22... | collective-permute-start | bytes 159752 | tf_op jit(solution)/shard_map/ppermute | solution.py:417
  25.9 1.5 %collective-permute-start.6 = (bf16[104,256]{1,0:T(8,128)(2,1)S(1)}, bf16[104,256]{1,0:T(8,128)(2,1)S(1)}, u32[]{:S(2)}, u32[]{:S(2)}) collective-permute-start(bf16[104,256]{1,0:T(8,128)(2,1)S(1)} %get-tuple-element.51.own_ref), channel_id=1, source_target_pairs={{0,64},{4,68},{8,72},{12,76},{16,80},{20,84},{24,88},{28,92},{32,9... | collective-permute-start | bytes 159752 | tf_op jit(solution)/shard_map/ppermute | solution.py:417
  27.4 1.2 %collective-permute-done.7.near_ref = bf16[104,256]{1,0:T(8,128)(2,1)S(1)} collective-permute-done((bf16[104,256]{1,0:T(8,128)(2,1)S(1)}, bf16[104,256]{1,0:T(8,128)(2,1)S(1)}, u32[]{:S(2)}, u32[]{:S(2)}) %collective-permute-start.7) | collective-permute-done | bytes 53280 | tf_op jit(solution)/shard_map/ppermute | solution.py:417
  28.6 1.4 %collective-permute-start.8 = (bf16[104,256]{1,0:T(8,128)(2,1)S(1)}, bf16[104,256]{1,0:T(8,128)(2,1)S(1)}, u32[]{:S(2)}, u32[]{:S(2)}) collective-permute-start(bf16[104,256]{1,0:T(8,128)(2,1)S(1)} %collective-permute-done.7.near_ref), channel_id=1, source_target_pairs={{0,64},{4,68},{8,72},{12,76},{16,80},{20,84},{24,88},{28,92},{32,9... | collective-permute-start | bytes 159752 | tf_op jit(solution)/shard_map/ppermute | solution.py:417
  30.0 1.0 %collective-permute-done.6.pair_ref = bf16[104,256]{1,0:T(8,128)(2,1)S(1)} collective-permute-done((bf16[104,256]{1,0:T(8,128)(2,1)S(1)}, bf16[104,256]{1,0:T(8,128)(2,1)S(1)}, u32[]{:S(2)}, u32[]{:S(2)}) %collective-permute-start.6) | collective-permute-done | bytes 53280 | tf_op jit(solution)/shard_map/ppermute | solution.py:417
  31.1 0.7 %known.1 = (f32[2,256,128]{2,1,0:T(8,128)S(1)}, f32[2,256,128]{2,1,0:T(8,128)S(1)}, f32[16,256]{1,0:T(8,128)S(1)}, f32[16,256]{1,0:T(8,128)S(1)}, f32[16,256]{1,...) custom-call(bf16[104,256]{1,0:T(8,128)(2,1)S(1)} %collective-permute-done.6, ...), custom_call_target="tpu_custom_call" | custom-call | flops 4194304 | bytes 524288 | tf_op jit(solution)/shard_map/known/pallas_call | solution.py:404
  31.8 1.8 %collective-permute-done.8.far_ref = bf16[104,256]{1,0:T(8,128)(2,1)S(1)} collective-permute-done((bf16[104,256]{1,0:T(8,128)(2,1)S(1)}, bf16[104,256]{1,0:T(8,128)(2,1)S(1)}, u32[]{:S(2)}, u32[]{:S(2)}) %collective-permute-start.8) | collective-permute-done | bytes 53280 | tf_op jit(solution)/shard_map/ppermute | solution.py:417
  33.6 1.2 %finish.1 = (bf16[256,256]{1,0:T(8,128)(2,1)}, bf16[256,256]{1,0:T(8,128)(2,1)}, bf16[256,256]{1,0:T(8,128)(2,1)}, f32[16,256]{1,0:T(8,128)}, f32[16,256]{1,0:T(8,128)}, /*index=5*/f32[1,256]{1,0:T(1,128)}) custom-call(bf16[104,256]{1,0:T(8,128)(2,1)S(1)} %get-tuple-element.51.own_ref, bf16[104,256]{1,0:T(8,128)(2,1)S(1)} %collective-permute-done.6.pair_ref, ...), custom_call_target="tpu_custom_call" | custom-call | bytes 524288 | tf_op jit(solution)/shard_map/finish/pallas_call | solution.py:404
  (1 shorter events, 0.0 us)
Async XLA Ops:
  3.1 6.2 %collective-permute-start = (bf16[104,256]{1,0:T(8,128)(2,1)S(1)}, bf16[104,256]{1,0:T(8,128)(2,1)S(1)}, u32[]{:S(2)}, u32[]{:S(2)}) collective-permute-start(bf16[104,256]{1,0:T(8,128)(2,1)S(1)} %get-tuple-element.41.z0), channel_id=1, source_target_pairs={{0,8},{4,12},{8,0},{12,4},{16,24},{20,28},{24,16},{28,20},{32,40},... | collective-permute-start | bytes 159752 | tf_op jit(solution)/shard_map/ppermute | solution.py:417
  6.2 5.3 %collective-permute-start.1 = (bf16[104,256]{1,0:T(8,128)(2,1)S(1)}, bf16[104,256]{1,0:T(8,128)(2,1)S(1)}, u32[]{:S(2)}, u32[]{:S(2)}) collective-permute-start(bf16[104,256]{1,0:T(8,128)(2,1)S(1)} %get-tuple-element.41.z0), channel_id=1, source_target_pairs={{0,12},{4,8},{8,4},{12,0},{16,28},{20,24},{24,20},{28,16},{32,44},... | collective-permute-start | bytes 159752 | tf_op jit(solution)/shard_map/ppermute | solution.py:417
  7.4 4.2 %collective-permute-start.2 = (bf16[104,256]{1,0:T(8,128)(2,1)S(1)}, bf16[104,256]{1,0:T(8,128)(2,1)S(1)}, u32[]{:S(2)}, u32[]{:S(2)}) collective-permute-start(bf16[104,256]{1,0:T(8,128)(2,1)S(1)} %get-tuple-element.41.z0), channel_id=1, source_target_pairs={{0,4},{4,0},{8,12},{12,8},{16,20},{20,16},{24,28},{28,24},{32,36},... | collective-permute-start | bytes 159752 | tf_op jit(solution)/shard_map/ppermute | solution.py:417
  11.7 5.8 %collective-permute-start.3 = (bf16[104,256]{1,0:T(8,128)(2,1)S(1)}, bf16[104,256]{1,0:T(8,128)(2,1)S(1)}, u32[]{:S(2)}, u32[]{:S(2)}) collective-permute-start(bf16[104,256]{1,0:T(8,128)(2,1)S(1)} %get-tuple-element.48.z0), channel_id=1, source_target_pairs={{0,32},{4,36},{8,40},{12,44},{16,48},{20,52},{24,56},{28,60},{32,0... | collective-permute-start | bytes 159752 | tf_op jit(solution)/shard_map/ppermute | solution.py:417
  15.0 5.3 %collective-permute-start.4 = (bf16[104,256]{1,0:T(8,128)(2,1)S(1)}, bf16[104,256]{1,0:T(8,128)(2,1)S(1)}, u32[]{:S(2)}, u32[]{:S(2)}) collective-permute-start(bf16[104,256]{1,0:T(8,128)(2,1)S(1)} %get-tuple-element.48.z0), channel_id=1, source_target_pairs={{0,48},{4,52},{8,56},{12,60},{16,32},{20,36},{24,40},{28,44},{32,1... | collective-permute-start | bytes 159752 | tf_op jit(solution)/shard_map/ppermute | solution.py:417
  16.0 4.3 %collective-permute-start.5 = (bf16[104,256]{1,0:T(8,128)(2,1)S(1)}, bf16[104,256]{1,0:T(8,128)(2,1)S(1)}, u32[]{:S(2)}, u32[]{:S(2)}) collective-permute-start(bf16[104,256]{1,0:T(8,128)(2,1)S(1)} %get-tuple-element.48.z0), channel_id=1, source_target_pairs={{0,16},{4,20},{8,24},{12,28},{16,0},{20,4},{24,8},{28,12},{32,48},... | collective-permute-start | bytes 159752 | tf_op jit(solution)/shard_map/ppermute | solution.py:417
  20.4 8.2 %collective-permute-start.7 = (bf16[104,256]{1,0:T(8,128)(2,1)S(1)}, bf16[104,256]{1,0:T(8,128)(2,1)S(1)}, u32[]{:S(2)}, u32[]{:S(2)}) collective-permute-start(bf16[104,256]{1,0:T(8,128)(2,1)S(1)} %get-tuple-element.51.own_ref), channel_id=1, source_target_pairs={{0,192},{4,196},{8,200},{12,204},{16,208},{20,212},{24,216},{28,22... | collective-permute-start | bytes 159752 | tf_op jit(solution)/shard_map/ppermute | solution.py:417
  25.9 5.1 %collective-permute-start.6 = (bf16[104,256]{1,0:T(8,128)(2,1)S(1)}, bf16[104,256]{1,0:T(8,128)(2,1)S(1)}, u32[]{:S(2)}, u32[]{:S(2)}) collective-permute-start(bf16[104,256]{1,0:T(8,128)(2,1)S(1)} %get-tuple-element.51.own_ref), channel_id=1, source_target_pairs={{0,64},{4,68},{8,72},{12,76},{16,80},{20,84},{24,88},{28,92},{32,9... | collective-permute-start | bytes 159752 | tf_op jit(solution)/shard_map/ppermute | solution.py:417
  28.6 5.0 %collective-permute-start.8 = (bf16[104,256]{1,0:T(8,128)(2,1)S(1)}, bf16[104,256]{1,0:T(8,128)(2,1)S(1)}, u32[]{:S(2)}, u32[]{:S(2)}) collective-permute-start(bf16[104,256]{1,0:T(8,128)(2,1)S(1)} %collective-permute-done.7.near_ref), channel_id=1, source_target_pairs={{0,64},{4,68},{8,72},{12,76},{16,80},{20,84},{24,88},{28,92},{32,9... | collective-permute-start | bytes 159752 | tf_op jit(solution)/shard_map/ppermute | solution.py:417
